TPU v7x, 128 devices: a whole 4x4x4 slice. The times are simulated.
128 devices in a mesh: seq: 64 (over x, y, z_hi, core), ch: 2 (over z_lo).
Axes of the slice: x: 4, y: 4, z: 4 (z_hi: 2, z_lo: 2; z = z_hi * 2 + z_lo), core: 2. Of those that a mesh axis runs over, the one named last changes fastest.
Arguments:
- inputs: bfloat16 [64, 2048, 652], P('seq', None, 'ch'), may hold values from -6 to 6
- offsets: int32 [64], P('seq'), may hold values from 0 to 683, as said below
- owners: int32 [64], replicated, may hold values from 0 to 63, each once
- cotangent: bfloat16 [64, 1024, 768], P('seq', None, 'ch'), may hold values from -6 to 6
- norm1_gain: float32 [652], P('ch'), may hold values from 0.5 to 1.5
- norm1_bias: float32 [652], P('ch'), may hold values from -4 to 4
- norm1_moments: float32 [2, 2, 652], P(None, None, 'ch'), as said below
- norm2_gain: float32 [768], P('ch'), may hold values from 0.5 to 1.5
- norm2_bias: float32 [768], P('ch'), may hold values from -4 to 4
- norm2_moments: float32 [2, 2, 768], P(None, None, 'ch'), as said below
- norm3_gain: float32 [384], P('ch'), may hold values from 0.5 to 1.5
- norm3_bias: float32 [384], P('ch'), may hold values from -4 to 4
- norm3_moments: float32 [2, 2, 384], P(None, None, 'ch'), as said below
- conv1_copy: bfloat16 [5, 652, 768], P(None, None, 'ch'), may hold values from -0.109375 to 0.109375
- conv1_master: float32 [5, 652, 768], P(None, None, ('seq', 'ch')), may hold values from -0.109375 to 0.109375
- conv1_first: float32 [5, 652, 768], P(None, None, ('seq', 'ch')), may hold values from -96 to 96
- conv1_second: float32 [5, 652, 768], P(None, None, ('seq', 'ch')), may hold values from 622.592 to 4980.736
- conv1_average: float32 [5, 652, 768], P(None, None, ('seq', 'ch')), may hold values from -0.109375 to 0.109375
- basis1: float32 [652, 652], replicated, as said below
- conv2_copy: bfloat16 [3, 768, 384], P(None, None, 'ch'), may hold values from -0.125 to 0.125
- conv2_master: float32 [3, 768, 384], P(None, None, ('seq', 'ch')), may hold values from -0.125 to 0.125
- conv2_first: float32 [3, 768, 384], P(None, None, ('seq', 'ch')), may hold values from -96 to 96
- conv2_second: float32 [3, 768, 384], P(None, None, ('seq', 'ch')), may hold values from 622.592 to 4980.736
- conv2_average: float32 [3, 768, 384], P(None, None, ('seq', 'ch')), may hold values from -0.125 to 0.125
- basis2: float32 [768, 768], replicated, as said below
- project_copy: bfloat16 [768, 384], P(None, 'ch'), may hold values from -0.3125 to 0.3125
- project_master: float32 [768, 384], P(None, ('seq', 'ch')), may hold values from -0.3125 to 0.3125
- project_first: float32 [768, 384], P(None, ('seq', 'ch')), may hold values from -96 to 96
- project_second: float32 [768, 384], P(None, ('seq', 'ch')), may hold values from 622.592 to 4980.736
- project_average: float32 [768, 384], P(None, ('seq', 'ch')), may hold values from -0.3125 to 0.3125
- basis3: float32 [768, 768], replicated, as said below
Outputs:
- output: bfloat16 [64, 1024, 768], P('seq', None, 'ch')
- input_grad: float32 [64, 2048, 652], P('seq', None, 'ch')
- norm1_new_values: float32 [2, 652], P(None, 'ch')
- norm1_new_first: float32 [2, 652], P(None, 'ch')
- norm1_new_second: float32 [2, 652], P(None, 'ch')
- norm2_new_values: float32 [2, 768], P(None, 'ch')
- norm2_new_first: float32 [2, 768], P(None, 'ch')
- norm2_new_second: float32 [2, 768], P(None, 'ch')
- norm3_new_values: float32 [2, 384], P(None, 'ch')
- norm3_new_first: float32 [2, 384], P(None, 'ch')
- norm3_new_second: float32 [2, 384], P(None, 'ch')
- conv1_new_master: float32 [5, 652, 768], P(None, None, ('seq', 'ch'))
- conv1_new_copy: bfloat16 [5, 652, 768], P(None, None, 'ch')
- conv1_new_first: float32 [5, 652, 768], P(None, None, ('seq', 'ch'))
- conv1_new_second: float32 [5, 652, 768], P(None, None, ('seq', 'ch'))
- conv1_new_average: float32 [5, 652, 768], P(None, None, ('seq', 'ch'))
- conv2_new_master: float32 [3, 768, 384], P(None, None, ('seq', 'ch'))
- conv2_new_copy: bfloat16 [3, 768, 384], P(None, None, 'ch')
- conv2_new_first: float32 [3, 768, 384], P(None, None, ('seq', 'ch'))
- conv2_new_second: float32 [3, 768, 384], P(None, None, ('seq', 'ch'))
- conv2_new_average: float32 [3, 768, 384], P(None, None, ('seq', 'ch'))
- project_new_master: float32 [768, 384], P(None, ('seq', 'ch'))
- project_new_copy: bfloat16 [768, 384], P(None, 'ch')
- project_new_first: float32 [768, 384], P(None, ('seq', 'ch'))
- project_new_second: float32 [768, 384], P(None, ('seq', 'ch'))
- project_new_average: float32 [768, 384], P(None, ('seq', 'ch'))
Inputs may be any that keep to these rules, and one draw needn't show every extreme that they name: offsets[s] counts the leading padded bins of sequence s; one sequence has none and at least one has 683. `owners`: a permutation of the indices along seq. `basis1`: orthogonal. `basis2`: orthogonal. `basis3`: orthogonal. `norm1_moments`: second moments positive. `norm2_moments`: second moments positive. `norm3_moments`: second moments positive.
All inputs are finite; a program needn't handle non-finite values.
Results may differ from a plain program's by a relative error of at most 0.017.
Values may be sent and summed in bfloat16 or wider, within the bound.
A program may use at most 192 MiB of HBM per device.

v0:
```python
import math

import jax
import jax.numpy as jnp
from jax import lax
from jax.sharding import Mesh
from jax.sharding import PartitionSpec as P

STEP = 8
SEQ = ("seq_0", "seq_1", "seq_2", "seq_3")
SEQ_CH = ("seq_0", "seq_1", "seq_2", "seq_3", "ch")


highest = lax.Precision.HIGHEST
eps_norm = 1e-05
beta_one = 0.9
beta_two = 0.95
adam_eps = 1e-08
decay_rate = 0.01
average_rate = 0.9
norm_rate = 0.05


def sent_to_all(array, axis):
    count = lax.axis_size(axis)
    return lax.all_to_all(
        jnp.broadcast_to(array[None], (count, *array.shape)), axis, 0, 0, tiled=True
    )


def over_copies(array, axis):
    everything = sent_to_all(array, axis)
    return jnp.sum(everything, axis=0)


def packed_total(arrays, axis):
    ends = [0]
    for a in arrays:
        ends.append(ends[-1] + a.size)
    running = over_copies(jnp.concatenate([a.ravel() for a in arrays]), axis)
    return tuple((running[b:e].reshape(a.shape) for a, b, e in zip(arrays, ends, ends[1:])))


def laid_out(pieces, dim):
    pieces = jnp.moveaxis(pieces, 0, dim)
    lengths = pieces.shape
    return pieces.reshape(*lengths[:dim], lengths[dim] * lengths[dim + 1], *lengths[dim + 2 :])


def collect(array, axis, dim):
    return laid_out(sent_to_all(array, axis), dim)


def split_up(array, dim, count):
    lengths = array.shape
    pieces = array.reshape(*lengths[:dim], count, lengths[dim] // count, *lengths[dim + 1 :])
    return jnp.moveaxis(pieces, dim, 0)


def sum_at_owner(array, axis, dim):
    pieces = split_up(array, dim, lax.axis_size(axis))
    arrived = lax.all_to_all(pieces, axis, split_axis=0, concat_axis=0, tiled=True)
    return arrived.astype(jnp.float32).sum(axis=0)


def sent_and_summed(array, axis, dim):
    count = lax.axis_size(axis)
    pieces = lax.all_to_all(split_up(array, dim, count), axis, 0, 0, tiled=True)
    return jnp.sum(pieces, axis=0)


def sum_in_two_steps(array, axes, dim):
    far, near = axes
    pieces = split_up(array, dim, lax.axis_size(far))
    nearer = sent_and_summed(pieces, near, dim + 1)
    arrived = lax.all_to_all(nearer, far, split_axis=0, concat_axis=0, tiled=True)
    return arrived.sum(axis=0)


def in_one_piece(arrays, axis, dim, along):
    ends, at = ([], 0)
    for a in arrays[:-1]:
        at += a.shape[along]
        ends.append(at)
    both = jnp.concatenate(arrays, axis=along)
    return tuple(jnp.split(sum_in_two_steps(both, axis, dim), ends, axis=along))


def in_one_piece_2(arrays, axis, dim, along):
    widths = [a.shape[along] for a in arrays]
    both = jnp.concatenate(arrays, axis=along)
    result = lax.all_gather(both, axis, axis=dim, tiled=True)
    return tuple(jnp.split(result, [sum(widths[:k]) for k in range(1, len(widths))], axis=along))


def valid_rows(offsets, length, repeat_factor):
    positions = jnp.arange(length, dtype=jnp.int32)
    return (positions[None, :] >= repeat_factor * offsets[:, None]).astype(jnp.float32)[:, :, None]


def norm_forward(values, validity, gain_values, bias_values):
    weighted = jnp.sum(values * validity, axis=(0, 1))
    sums, squares, population = packed_total(
        (weighted, jnp.sum(validity * values * values, axis=(0, 1)), jnp.sum(validity)), SEQ
    )
    center = sums / population
    spread = squares / population - center * center
    inverse = lax.rsqrt(spread + eps_norm)
    scaled = (values - center) * inverse
    before = scaled * gain_values + bias_values
    return (jax.nn.gelu(before) * validity, (scaled, before, inverse, population))


def norm_backward(upstream, validity, gain_values, saved):
    scaled, before, inverse, population = saved
    slopes = jax.vjp(jax.nn.gelu, before)[1](upstream * validity)[0]
    gain_grad, bias_grad = packed_total(
        (jnp.sum(slopes * scaled, axis=(0, 1)), jnp.sum(slopes, axis=(0, 1))), SEQ
    )
    result = (
        validity
        * (gain_values * inverse)
        * (slopes - bias_grad / population - scaled * gain_grad / population)
    )
    return (result, jnp.stack([gain_grad, bias_grad]))


def convolve(values, weight):
    taps_count = weight.shape[0]
    margin = (taps_count - 1) // 2
    length = values.shape[1]
    padded = jnp.pad(values, ((0, 0), (margin, margin), (0, 0)))
    summed = jnp.zeros(values.shape[:2] + (weight.shape[2],), jnp.float32)
    for tap_index in range(taps_count):
        summed = summed + lax.dot_general(
            padded[:, tap_index : tap_index + length],
            weight[tap_index],
            (((2,), (0,)), ((), ())),
            preferred_element_type=jnp.float32,
        )
    return summed


def convolve_back(gradient, weight):
    taps_count = weight.shape[0]
    margin = (taps_count - 1) // 2
    length = gradient.shape[1]
    padded = jnp.pad(gradient, ((0, 0), (margin, margin), (0, 0)))
    summed = jnp.zeros(gradient.shape[:2] + (weight.shape[1],), jnp.float32)
    for tap_index in range(taps_count):
        start = 2 * margin - tap_index
        summed = summed + lax.dot_general(
            padded[:, start : start + length],
            weight[tap_index],
            (((2,), (1,)), ((), ())),
            preferred_element_type=jnp.float32,
        )
    return summed


def weight_gradient(values, gradient, taps_count):
    margin = (taps_count - 1) // 2
    length = values.shape[1]
    padded = jnp.pad(values, ((0, 0), (margin, margin), (0, 0)))
    return jnp.stack(
        [
            lax.dot_general(
                padded[:, tap_index : tap_index + length],
                gradient,
                (((0, 1), (0, 1)), ((), ())),
                preferred_element_type=jnp.float32,
            )
            for tap_index in range(taps_count)
        ]
    )


def to_owner(matrix, order_list, seq_devices):
    leading = matrix.shape[:-1]
    blocks = matrix.reshape(leading + (seq_devices, matrix.shape[-1] // seq_devices))
    return jnp.take(blocks, order_list, axis=len(leading)).reshape(matrix.shape)


def rotated_adam(gradient, master, first_moment, second, average, rotation, step_rate):
    turned = jnp.einsum("ij,...iw->...jw", rotation, gradient, precision=highest)
    first_new = beta_one * first_moment + (1.0 - beta_one) * turned
    second_new = beta_two * second + (1.0 - beta_two) * turned * turned
    direction = (
        first_new
        / (1.0 - beta_one**STEP)
        / (jnp.sqrt(second_new / (1.0 - beta_two**STEP)) + adam_eps)
    )
    update = jnp.einsum("ij,...jw->...iw", rotation, direction, precision=highest)
    master_new = master - step_rate * (update + decay_rate * master)
    average_new = average_rate * average + (1.0 - average_rate) * master_new
    return (master_new, first_new, second_new, average_new)


def norm_adam(gradient, parameters, moments):
    first_new = beta_one * moments[0] + (1.0 - beta_one) * gradient
    second_new = beta_two * moments[1] + (1.0 - beta_two) * gradient * gradient
    direction = (
        first_new
        / (1.0 - beta_one**STEP)
        / (jnp.sqrt(second_new / (1.0 - beta_two**STEP)) + adam_eps)
    )
    return (parameters - norm_rate * direction, first_new, second_new)


def local(
    inputs,
    offsets,
    owners,
    cotangent,
    norm1_gain,
    norm1_bias,
    norm1_moments,
    norm2_gain,
    norm2_bias,
    norm2_moments,
    norm3_gain,
    norm3_bias,
    norm3_moments,
    conv1_copy,
    conv1_master,
    conv1_first,
    conv1_second,
    conv1_average,
    basis1,
    conv2_copy,
    conv2_master,
    conv2_first,
    conv2_second,
    conv2_average,
    basis2,
    project_copy,
    project_master,
    project_first,
    project_second,
    project_average,
    basis3,
):
    length = cotangent.shape[1]
    bin_valid = valid_rows(offsets, length, 1)
    in_valid = valid_rows(offsets, 2 * length, 2)
    normed_local, saved_in = norm_forward(
        inputs.astype(jnp.float32), in_valid, norm1_gain, norm1_bias
    )
    normed_in = collect(normed_local.astype(jnp.bfloat16), "ch", 2)
    hidden1 = convolve(normed_in, conv1_copy)
    paired = hidden1.reshape(hidden1.shape[0], length, 2, hidden1.shape[2])
    pooled = jnp.logaddexp(paired[:, :, 0], paired[:, :, 1]) - math.log(2.0)
    mid_local, saved_mid = norm_forward(pooled, bin_valid, norm2_gain, norm2_bias)
    normed_mid = collect(mid_local.astype(jnp.bfloat16), "ch", 2)
    hidden2 = convolve(normed_mid, conv2_copy)
    out_local, saved_out = norm_forward(hidden2, bin_valid, norm3_gain, norm3_bias)
    normed_out = out_local.astype(jnp.bfloat16)
    inner_whole = collect(normed_out, "ch", 2)
    project_slice = lax.all_to_all(project_copy, "ch", split_axis=0, concat_axis=1, tiled=True)
    branch = lax.dot_general(
        inner_whole, project_slice, (((2,), (1,)), ((), ())), preferred_element_type=jnp.float32
    )
    output = (pooled + branch).astype(jnp.bfloat16)
    upstream = collect(cotangent, "ch", 2)
    project_grad = lax.dot_general(
        upstream, normed_out, (((0, 1), (0, 1)), ((), ())), preferred_element_type=jnp.float32
    )
    out_grad = lax.dot_general(
        upstream, project_copy, (((2,), (0,)), ((), ())), preferred_element_type=jnp.float32
    )
    hidden2_back, norm3_grads = norm_backward(out_grad, bin_valid, norm3_gain, saved_out)
    hidden2_grad = hidden2_back.astype(jnp.bfloat16)
    conv2_grad = weight_gradient(normed_mid, hidden2_grad, 3)
    grad_whole = collect(hidden2_grad, "ch", 2)
    conv2_slice = lax.all_to_all(conv2_copy, "ch", split_axis=1, concat_axis=2, tiled=True)
    mid_grad = convolve_back(grad_whole, conv2_slice)
    pooled_back, norm2_grads = norm_backward(mid_grad, bin_valid, norm2_gain, saved_mid)
    pooled_grad = pooled_back + cotangent.astype(jnp.float32)
    weight_even = jax.nn.sigmoid(paired[:, :, 0] - paired[:, :, 1])
    hidden1_grad = (
        jnp.stack([pooled_grad * weight_even, pooled_grad * (1.0 - weight_even)], axis=2)
        .reshape(hidden1.shape)
        .astype(jnp.bfloat16)
    )
    conv1_grad = weight_gradient(normed_in, hidden1_grad, 5)
    in_partial = convolve_back(hidden1_grad, conv1_copy)
    in_act_grad = sum_at_owner(in_partial.astype(jnp.bfloat16), "ch", 2)
    input_grad, norm1_grads = norm_backward(in_act_grad, in_valid, norm1_gain, saved_in)
    norm1_state = norm_adam(norm1_grads, jnp.stack([norm1_gain, norm1_bias]), norm1_moments)
    norm2_state = norm_adam(norm2_grads, jnp.stack([norm2_gain, norm2_bias]), norm2_moments)
    norm3_state = norm_adam(norm3_grads, jnp.stack([norm3_gain, norm3_bias]), norm3_moments)
    seq_devices = lax.axis_size(SEQ)
    inverse = jnp.argsort(owners)
    reduced = (
        sum_in_two_steps(
            to_owner(conv1_grad, owners, seq_devices), (("seq_0", "seq_1", "seq_2"), "seq_3"), 2
        ),
        *in_one_piece(
            (
                to_owner(conv2_grad, owners, seq_devices),
                to_owner(project_grad, owners, seq_devices)[None],
            ),
            (("seq_0", "seq_1", "seq_2"), "seq_3"),
            2,
            0,
        ),
    )
    first_result = rotated_adam(
        reduced[0], conv1_master, conv1_first, conv1_second, conv1_average, basis1, 0.02
    )
    second_result = rotated_adam(
        reduced[1], conv2_master, conv2_first, conv2_second, conv2_average, basis2, 0.02
    )
    third_result = rotated_adam(
        reduced[2][0], project_master, project_first, project_second, project_average, basis3, 0.05
    )
    copies = (
        lax.all_gather(first_result[0].astype(jnp.bfloat16), SEQ, axis=2, tiled=True),
        *in_one_piece_2(
            (second_result[0].astype(jnp.bfloat16), third_result[0][None].astype(jnp.bfloat16)),
            SEQ,
            2,
            0,
        ),
    )
    conv1_new_copy = to_owner(copies[0], inverse, seq_devices)
    conv2_new_copy = to_owner(copies[1], inverse, seq_devices)
    project_new_copy = to_owner(copies[2][0], inverse, seq_devices)
    return (
        output,
        input_grad,
        norm1_state[0],
        norm1_state[1],
        norm1_state[2],
        norm2_state[0],
        norm2_state[1],
        norm2_state[2],
        norm3_state[0],
        norm3_state[1],
        norm3_state[2],
        first_result[0],
        conv1_new_copy,
        first_result[1],
        first_result[2],
        first_result[3],
        second_result[0],
        conv2_new_copy,
        second_result[1],
        second_result[2],
        second_result[3],
        third_result[0],
        project_new_copy,
        third_result[1],
        third_result[2],
        third_result[3],
    )


def solution(mesh):
    finer = Mesh(
        mesh.devices.reshape(4, 4, 2, 2, mesh.shape["ch"]),
        ("seq_0", "seq_1", "seq_2", "seq_3", "ch"),
    )
    in_specs = (
        P(SEQ, None, "ch"),
        P(SEQ),
        P(),
        P(SEQ, None, "ch"),
        P("ch"),
        P("ch"),
        P(None, None, "ch"),
        P("ch"),
        P("ch"),
        P(None, None, "ch"),
        P("ch"),
        P("ch"),
        P(None, None, "ch"),
        P(None, None, "ch"),
        P(None, None, SEQ_CH),
        P(None, None, SEQ_CH),
        P(None, None, SEQ_CH),
        P(None, None, SEQ_CH),
        P(),
        P(None, None, "ch"),
        P(None, None, SEQ_CH),
        P(None, None, SEQ_CH),
        P(None, None, SEQ_CH),
        P(None, None, SEQ_CH),
        P(),
        P(None, "ch"),
        P(None, SEQ_CH),
        P(None, SEQ_CH),
        P(None, SEQ_CH),
        P(None, SEQ_CH),
        P(),
    )
    out_specs = (
        P(SEQ, None, "ch"),
        P(SEQ, None, "ch"),
        P(None, "ch"),
        P(None, "ch"),
        P(None, "ch"),
        P(None, "ch"),
        P(None, "ch"),
        P(None, "ch"),
        P(None, "ch"),
        P(None, "ch"),
        P(None, "ch"),
        P(None, None, SEQ_CH),
        P(None, None, "ch"),
        P(None, None, SEQ_CH),
        P(None, None, SEQ_CH),
        P(None, None, SEQ_CH),
        P(None, None, SEQ_CH),
        P(None, None, "ch"),
        P(None, None, SEQ_CH),
        P(None, None, SEQ_CH),
        P(None, None, SEQ_CH),
        P(None, SEQ_CH),
        P(None, "ch"),
        P(None, SEQ_CH),
        P(None, SEQ_CH),
        P(None, SEQ_CH),
    )
    return jax.shard_map(local, mesh=finer, in_specs=in_specs, out_specs=out_specs, check_vma=False)
```

profile of v0, /device:TPU:1, one launch (start us, length us, event | category | flops | bytes accessed | tf_op | source)
XLA Modules:
  0.0 773.4 jit_solution(17228999259192487731)
XLA Ops:
  8.7 8.3 %multiply_reduce_fusion = (f32[326]{0:T(512)S(1)}, f32[326]{0:T(512)S(1)}) fusion(bf16[1,2048,326]{1,2,0:T(8,128)(2,1)} %param.31, f32[2048]{0:T(1024)S(1)} %fusion.245), kind=kLoop, calls=%fused_computation.15 | loop fusion | flops 3337588 | bytes 1346096 | tf_op jit(solution)/shard_map/reduce_sum | solution.py:102
  17.7 22.8 %all_to_all.120 = f32[64,1,653]{2,1,0:T(1,128)S(1)} all-to-all(f32[64,1,653]{2,1,0:T(1,128)S(1)} %broadcast_in_dim.180), channel_id=1, replica_groups=mesh['seq_0'=4,'seq_1'=4,'seq_2'=2,'seq_3'=2,'ch'=2] {'seq_0','seq_1','s..., dimensions={0} | all-to-all | bytes 334336 | tf_op jit(solution)/shard_map/all_to_all | solution.py:26
  43.2 19.0 %multiply_convert_fusion = (bf16[1,2048,326]{1,0,2:T(2,128)(2,1)S(1)}, f32[1,2048,326]{1,0,2:T(1,128)}, f32[1,2048,326]{1,0,2:T(1,128)}) fusion(f32[2048]{0:T(1024)S(1)} %fusion.245, f32[326]{0:T(512)} %param.36, f32[326]{0:T(512)} %param.35, f32[326]{0:T(512)S(1)} %get-tuple-element.206, f32[326]{0:T(512)S(1)} %get-tuple-element.247, ...), kind=kLoop, calls=%fused_computation.41 | loop fusion | flops 10014720 | bytes 8025184 | tf_op jit(solution)/shard_map/convert_element_type | solution.py:249
  64.8 5.3 all-to-all-start.1
  70.7 30.3 %all-to-all-done.1 = bf16[2,1,2048,326]{2,3,1,0:T(8,128)(2,1)} async-done(((bf16[2,1,2048,326]{2,3,1,0:T(8,128)(2,1)}), bf16[2,1,2048,326]{2,3,1,0:T(8,128)(2,1)}, u32[]{:S(2)}, u32[]{:S(2)}) %all-to-all-start.1) | async-done | bytes 2670624 | tf_op jit(solution)/shard_map/all_to_all | solution.py:26
  101.0 3.9 reshape.1082
  104.9 7.2 fusion.11
  112.1 6.2 fusion.13
  118.3 6.2 fusion.9
  128.3 3.9 fusion.190
  132.9 7.9 %add_add_fusion = f32[2048,384]{1,0:T(8,128)} fusion(f32[2048,384]{1,0:T(8,128)} %fusion.9, f32[2048,384]{1,0:T(8,128)S(1)} %fusion.190, f32[2048,384]{1,0:T(8,128)S(1)} %copy-done.17, f32[2048,384]{1,0:T(8,128)S(1)} %copy-done.16, bf16[1,2048,652]{1,2,0:T(8,128)(2,1)S(1)} %copy-done.10, bf16[5,652,384]{2,1,0:T(8,128)(2,1)} %param.44), kind=kOutput, calls=%fused_computation.10 | convolution fusion | flops 1028653056 | bytes 18903040 | tf_op jit(solution)/shard_map/dot_general | solution.py:135
  140.8 5.1 reshape.1088
  145.9 5.5 fusion.294
  154.6 16.0 %all_to_all.121 = f32[64,1,769]{2,1,0:T(1,128)S(1)} all-to-all(f32[64,1,769]{2,1,0:T(1,128)S(1)} %broadcast_in_dim.183), channel_id=1, replica_groups=mesh['seq_0'=4,'seq_1'=4,'seq_2'=2,'seq_3'=2,'ch'=2] {'seq_0','seq_1','s..., dimensions={0} | all-to-all | bytes 393728 | tf_op jit(solution)/shard_map/all_to_all | solution.py:26
  176.0 4.6 all-to-all-start.3
  182.8 16.8 %all-to-all-done.3 = bf16[2,1,1024,384]{3,2,1,0:T(8,128)(2,1)} async-done(((bf16[2,1,1024,384]{3,2,1,0:T(8,128)(2,1)}), bf16[2,1,1024,384]{3,2,1,0:T(8,128)(2,1)}, u32[]{:S(2)}, u32[]{:S(2)}) %all-to-all-start.3) | async-done | bytes 1572896 | tf_op jit(solution)/shard_map/all_to_all | solution.py:26
  199.7 4.6 all-to-all-start.10
  210.8 11.6 %all-to-all-done.10 = bf16[3,768,192]{2,0,1:T(4,128)(2,1)} async-done(((bf16[3,768,192]{2,0,1:T(4,128)(2,1)}), bf16[3,768,192]{2,0,1:T(4,128)(2,1)}, u32[]{:S(2)}, u32[]{:S(2)}) %all-to-all-start.10) | async-done | bytes 884768 | tf_op jit(solution)/shard_map/all_to_all | solution.py:275
  223.7 4.9 all-to-all-start.7
  235.6 10.2 %all-to-all-done.7 = bf16[2,1,1024,384]{3,2,1,0:T(8,128)(2,1)} async-done(((bf16[2,1,1024,384]{3,2,1,0:T(8,128)(2,1)}), bf16[2,1,1024,384]{3,2,1,0:T(8,128)(2,1)}, u32[]{:S(2)}, u32[]{:S(2)}) %all-to-all-start.7) | async-done | bytes 1572896 | tf_op jit(solution)/shard_map/all_to_all | solution.py:26
  246.5 7.1 all-to-all-start.4
  270.1 10.0 %all-to-all-start.8 = ((f32[64,1,384]{2,1,0:T(1,128)}), f32[64,1,384]{2,1,0:T(1,128)S(1)}, u32[]{:S(2)}, u32[]{:S(2)}) async-start(f32[64,1,384]{2,1,0:T(1,128)} %broadcast_in_dim.189), calls=%async_computation.8 | async-start | bytes 196608 | tf_op jit(solution)/shard_map/all_to_all | solution.py:26
  282.0 4.9 reshape.1188
  286.9 4.9 reshape.1186
  305.4 5.0 gather_fusion.2
  336.0 4.0 all-to-all-done.9
  340.1 6.4 all-to-all-start.16
  348.5 4.2 multiply_reduce_fusion.3
  353.5 10.3 %all-to-all-start.11 = ((f32[64,1,768]{2,1,0:T(1,128)}), f32[64,1,768]{2,1,0:T(1,128)}, u32[]{:S(2)}, u32[]{:S(2)}) async-start(f32[64,1,768]{2,1,0:T(1,128)} %broadcast_in_dim.191), calls=%async_computation.11 | async-start | bytes 393216 | tf_op jit(solution)/shard_map/all_to_all | solution.py:26
  380.1 4.7 fusion.57
  387.8 4.7 convert_element_type.158
  392.5 4.7 convert_element_type.157
  399.8 3.8 dot_general.148
  403.6 5.6 fusion.75
  422.8 6.5 copy.316
  429.3 7.5 gather_fusion
  436.9 7.1 copy.317
  443.9 9.3 %gather.37 = f32[5,652,32,12]{1,3,2,0:T(8,128)} reshape(f32[5,652,64,6]{1,3,2,0:T(8,128)} %copy.317) | data formatting | bytes 10014720 | tf_op jit(solution)/shard_map/jit(_take)/gather | solution.py:181
  453.2 5.6 fusion.51
  460.2 5.0 fusion.53
  476.0 5.4 fusion.188
  481.5 5.0 all-to-all-done.5
  487.4 15.6 %all_to_all.122 = f32[2,32,5,652,6]{3,1,4,2,0:T(8,128)} all-to-all(f32[2,32,5,652,6]{3,1,4,2,0:T(8,128)} %copy.319), channel_id=1, replica_groups=mesh['seq_0'=4,'seq_1'=4,'seq_2'=2,'seq_3'=2,'ch'=2] {'seq_3'}, dimensions={0} | all-to-all | bytes 10014720 | tf_op jit(solution)/shard_map/all_to_all | solution.py:68
  503.0 8.4 %all-to-all-start.17 = ((f32[32,4,768,3]{2,1,3,0:T(4,128)}), f32[32,4,768,3]{2,1,3,0:T(4,128)}, u32[]{:S(2)}, u32[]{:S(2)}) async-start(f32[32,4,768,3]{2,1,3,0:T(4,128)} %copy.339), calls=%async_computation.17 | async-start | bytes 2359296 | tf_op jit(solution)/shard_map/all_to_all | solution.py:76
  514.7 8.0 %add_convert_fusion = bf16[2048,652]{0,1:T(8,128)(2,1)} fusion(f32[2048,652]{0,1:T(8,128)S(1)} %bitcast.454, f32[2048,652]{0,1:T(8,128)} %fusion.188, f32[2048,652]{0,1:T(8,128)S(1)} %fusion.55, f32[2048,652]{0,1:T(8,128)} %fusion.53, bf16[1,2048,384]{2,1,0:T(8,128)(2,1)S(1)} %copy-done.2, bf16[5,652,384]{2,1,0:T(8,128)(2,1)} %param.44), kind=kOutput, calls=%fused_computation.8 | convolution fusion | flops 1032183808 | bytes 26177536 | tf_op jit(solution)/shard_map/dot_general | solution.py:152
  522.7 3.8 reshape.1107
  526.5 4.3 all-to-all-done.17
  530.8 5.0 all-to-all-start.12
  535.8 5.1 reduce_sum.253
  541.0 5.5 copy.321
  553.8 11.4 %all-to-all-done.12 = bf16[2,1,2048,326]{2,3,1,0:T(8,128)(2,1)} async-done(((bf16[2,1,2048,326]{2,3,1,0:T(8,128)(2,1)}), bf16[2,1,2048,326]{2,3,1,0:T(8,128)(2,1)}, u32[]{:S(2)}, u32[]{:S(2)}) %all-to-all-start.12) | async-done | bytes 2670624 | tf_op jit(solution)/shard_map/all_to_all | solution.py:62
  565.2 6.1 all-to-all-start.15
  585.1 4.1 convert_reduce_fusion
  589.2 29.5 %all-to-all-done.15 = f32[32,5,652,6]{2,3,1,0:T(8,128)} async-done(((f32[32,5,652,6]{2,3,1,0:T(8,128)}), f32[32,5,652,6]{2,3,1,0:T(8,128)}, u32[]{:S(2)}, u32[]{:S(2)}) %all-to-all-start.15) | async-done | bytes 2503712 | tf_op jit(solution)/shard_map/all_to_all | solution.py:76
  627.6 24.5 %multiply_reduce_fusion.1 = (f32[326]{0:T(512)S(1)}, f32[326]{0:T(512)S(1)}, f32[1,2048,326]{1,0,2:T(1,128)}) fusion(f32[1,2048,326]{1,0,2:T(1,128)} %get-tuple-element.217, f32[1,2048,326]{1,0,2:T(1,128)} %get-tuple-element.216, f32[2048]{0:T(1024)S(1)} %copy-done.38, f32[2048,326]{0,1:T(8,128)} %convert_reduce_fusion), kind=kLoop, calls=%fused_computation.40 | loop fusion | flops 15355252 | bytes 10693168 | tf_op jit(solution)/shard_map/reduce_sum | solution.py:118
  652.9 11.1 %all-to-all-start.13 = ((f32[64,1,652]{2,1,0:T(1,128)}), f32[64,1,652]{2,1,0:T(1,128)S(1)}, u32[]{:S(2)}, u32[]{:S(2)}) async-start(f32[64,1,652]{2,1,0:T(1,128)} %broadcast_in_dim.192), calls=%async_computation.13 | async-start | bytes 393216 | tf_op jit(solution)/shard_map/all_to_all | solution.py:26
  664.6 9.9 %all-to-all-done.13 = f32[64,1,652]{2,1,0:T(1,128)S(1)} async-done(((f32[64,1,652]{2,1,0:T(1,128)}), f32[64,1,652]{2,1,0:T(1,128)S(1)}, u32[]{:S(2)}, u32[]{:S(2)}) %all-to-all-start.13) | async-done | bytes 166944 | tf_op jit(solution)/shard_map/all_to_all | solution.py:26
  676.0 8.9 %fusion.15 = f32[1,2048,326]{1,0,2:T(1,128)} fusion(f32[1,2048,326]{1,0,2:T(1,128)} %get-tuple-element.217, f32[1,2048,326]{1,0,2:T(1,128)} %get-tuple-element.207, f32[326]{0:T(512)S(1)} %get-tuple-element.245, f32[326]{0:T(512)S(1)} %get-tuple-element.244, f32[]{:T(128)} %bitcast.2, f32[2048]{0:T(1024)S(1)} %copy-done.38, f32[326]{0:T(512)S(1)} %copy-done.80), kind=kLoop, calls=%fused_computation.32 | loop fusion | flops 4005888 | bytes 8023884 | tf_op jit(solution)/shard_map/mul | solution.py:121
  703.4 33.4 %all-gather.3.cloned.1.call-done = bf16[5,652,384]{1,0,2:T(8,128)(2,1)} async-done(((bf16[5,652,6]{1,0,2:T(8,128)(2,1)}), bf16[5,652,384]{1,0,2:T(8,128)(2,1)}) %all-gather.3.cloned.1.call-update) | async-done | bytes 2503696 | tf_op jit(solution)/shard_map/all_gather | solution.py:318
  736.8 5.1 copy.347
  741.9 4.8 gather_fusion.1
  746.8 4.3 copy.324
  751.1 6.4 gather.39
  761.2 5.2 copy.344
  (352 shorter events, 204.2 us)
Async XLA Ops:
  7.2 564.6 %copy-start = (f32[768,768]{1,0:T(8,128)S(1)}, f32[768,768]{1,0:T(8,128)}, u32[]{:S(2)}) copy-start(f32[768,768]{1,0:T(8,128)} %param.55) | copy-start | bytes 7077892
  8.0 54.2 %copy-start.37 = (f32[2048]{0:T(1024)}, f32[2048]{0:T(1024)S(1)}, u32[]{:S(2)}) copy-start(f32[2048]{0:T(1024)S(1)} %fusion.245) | copy-start | bytes 24580
  64.8 36.2 %all-to-all-start.1 = ((bf16[2,1,2048,326]{2,3,1,0:T(8,128)(2,1)}), bf16[2,1,2048,326]{2,3,1,0:T(8,128)(2,1)}, u32[]{:S(2)}, u32[]{:S(2)}) async-start(bf16[2,1,2048,326]{2,3,1,0:T(8,128)(2,1)} %broadcast_in_dim.182), calls=%async_computation.1 | async-start | bytes 5373952 | tf_op jit(solution)/shard_map/all_to_all | solution.py:26
  104.9 7.2 copy-start.9
  151.5 19.8 %copy-start.52 = (f32[384]{0:T(512)S(1)}, f32[384]{0:T(512)}, u32[]{:S(2)}) copy-start(f32[384]{0:T(512)} %param.38) | copy-start | bytes 4612
  151.5 21.1 %copy-start.81 = (f32[384]{0:T(512)S(1)}, f32[384]{0:T(512)}, u32[]{:S(2)}) copy-start(f32[384]{0:T(512)} %param.39) | copy-start | bytes 4612
  174.7 5.9 copy-start.24
  176.0 23.6 %all-to-all-start.3 = ((bf16[2,1,1024,384]{3,2,1,0:T(8,128)(2,1)}), bf16[2,1,1024,384]{3,2,1,0:T(8,128)(2,1)}, u32[]{:S(2)}, u32[]{:S(2)}) async-start(bf16[2,1,1024,384]{3,2,1,0:T(8,128)(2,1)} %broadcast_in_dim.184), calls=%async_computation.3 | async-start | bytes 3145728 | tf_op jit(solution)/shard_map/all_to_all | solution.py:26
  180.6 23.6 %copy-start.93 = (s32[64]{0:T(128)S(1)}, s32[64]{0:T(128)}, u32[]{:S(2)}) copy-start(s32[64]{0:T(128)} %param.33) | copy-start | bytes 772
  199.7 22.7 %all-to-all-start.10 = ((bf16[3,768,192]{2,0,1:T(4,128)(2,1)}), bf16[3,768,192]{2,0,1:T(4,128)(2,1)}, u32[]{:S(2)}, u32[]{:S(2)}) async-start(bf16[3,768,192]{2,0,1:T(4,128)(2,1)} %copy.300), calls=%async_computation.10 | async-start | bytes 3145728 | tf_op jit(solution)/shard_map/all_to_all | solution.py:275
  208.2 14.2 %copy-start.21 = (bf16[1,1024,384]{2,1,0:T(8,128)(2,1)S(1)}, bf16[1,1024,384]{2,1,0:T(8,128)(2,1)}, u32[]{:S(2)}) copy-start(bf16[1,1024,384]{2,1,0:T(8,128)(2,1)} %param.34) | copy-start | bytes 2359300
  223.7 22.1 %all-to-all-start.7 = ((bf16[2,1,1024,384]{3,2,1,0:T(8,128)(2,1)}), bf16[2,1,1024,384]{3,2,1,0:T(8,128)(2,1)}, u32[]{:S(2)}, u32[]{:S(2)}) async-start(bf16[2,1,1024,384]{3,2,1,0:T(8,128)(2,1)} %broadcast_in_dim.188), calls=%async_computation.7 | async-start | bytes 3145728 | tf_op jit(solution)/shard_map/all_to_all | solution.py:26
  234.8 58.4 %copy-start.20 = (f32[1024,192]{0,1:T(8,128)}, f32[1024,192]{0,1:T(8,128)S(1)}, u32[]{:S(2)}) copy-start(f32[1024,192]{0,1:T(8,128)S(1)} %get-tuple-element.251) | copy-start | bytes 2359300
  246.5 17.2 %all-to-all-start.4 = ((f32[64,1,385]{2,1,0:T(1,128)}), f32[64,1,385]{2,1,0:T(1,128)S(1)}, u32[]{:S(2)}, u32[]{:S(2)}) async-start(f32[64,1,385]{2,1,0:T(1,128)} %broadcast_in_dim.185), calls=%async_computation.4 | async-start | bytes 262144 | tf_op jit(solution)/shard_map/all_to_all | solution.py:26
  270.1 21.7 %all-to-all-start.8 = ((f32[64,1,384]{2,1,0:T(1,128)}), f32[64,1,384]{2,1,0:T(1,128)S(1)}, u32[]{:S(2)}, u32[]{:S(2)}) async-start(f32[64,1,384]{2,1,0:T(1,128)} %broadcast_in_dim.189), calls=%async_computation.8 | async-start | bytes 196608 | tf_op jit(solution)/shard_map/all_to_all | solution.py:26
  326.1 14.0 %all-to-all-start.9 = ((bf16[2,1,1024,192]{2,3,1,0:T(8,128)(2,1)}), bf16[2,1,1024,192]{2,3,1,0:T(8,128)(2,1)S(1)}, u32[]{:S(2)}, u32[]{:S(2)}) async-start(bf16[2,1,1024,192]{2,3,1,0:T(8,128)(2,1)} %broadcast_in_dim.190), calls=%async_computation.9 | async-start | bytes 1572864 | tf_op jit(solution)/shard_map/all_to_all | solution.py:26
  336.0 10.4 %copy-start.33 = (bf16[1,384,2,192]{1,3,2,0:T(8,128)(2,1)S(1)}, bf16[1,384,2,192]{1,3,2,0:T(8,128)(2,1)}, u32[]{:S(2)}) copy-start(bf16[1,384,2,192]{1,3,2,0:T(8,128)(2,1)} %get-tuple-element.222) | copy-start | bytes 884740
  340.1 12.7 %all-to-all-start.16 = ((f32[2,32,4,768,3]{3,1,4,2,0:T(8,128)}), f32[2,32,4,768,3]{3,1,4,2,0:T(8,128)}, u32[]{:S(2)}, u32[]{:S(2)}) async-start(f32[2,32,4,768,3]{3,1,4,2,0:T(8,128)} %copy.337), calls=%async_computation.16 | async-start | bytes 4718592 | tf_op jit(solution)/shard_map/all_to_all | solution.py:68
  348.5 15.3 %copy-start.92 = (pred[32,2]{0,1:T(4,128)(4,1)S(1)}, pred[32,2]{0,1:T(4,128)(4,1)}, u32[]{:S(2)}) copy-start(pred[32,2]{0,1:T(4,128)(4,1)} %copy-done.91) | copy-start | bytes 196
  348.5 16.0 %copy-start.36 = (bf16[768,192]{0,1:T(8,128)(2,1)S(1)}, bf16[768,192]{0,1:T(8,128)(2,1)}, u32[]{:S(2)}) copy-start(bf16[768,192]{0,1:T(8,128)(2,1)} %param.56) | copy-start | bytes 884740
  353.5 20.9 %all-to-all-start.11 = ((f32[64,1,768]{2,1,0:T(1,128)}), f32[64,1,768]{2,1,0:T(1,128)}, u32[]{:S(2)}, u32[]{:S(2)}) async-start(f32[64,1,768]{2,1,0:T(1,128)} %broadcast_in_dim.191), calls=%async_computation.11 | async-start | bytes 393216 | tf_op jit(solution)/shard_map/all_to_all | solution.py:26
  374.4 97.1 %all-to-all-start.6 = ((bf16[2,384,192]{1,2,0:T(8,128)(2,1)}), bf16[2,384,192]{1,2,0:T(8,128)(2,1)S(1)}, u32[]{:S(2)}, u32[]{:S(2)}) async-start(bf16[2,384,192]{1,2,0:T(8,128)(2,1)} %bitcast.477), calls=%async_computation.6 | async-start | bytes 589824 | tf_op jit(solution)/shard_map/all_to_all | solution.py:259
  403.6 5.6 copy-start.11
  403.6 5.6 copy-start.27
  453.2 5.6 copy-start.3
  453.2 5.6 copy-start.65
  472.5 14.0 %all-to-all-start.5 = ((bf16[2,1,1024,192]{2,3,1,0:T(8,128)(2,1)}), bf16[2,1,1024,192]{2,3,1,0:T(8,128)(2,1)S(1)}, u32[]{:S(2)}, u32[]{:S(2)}) async-start(bf16[2,1,1024,192]{2,3,1,0:T(8,128)(2,1)} %broadcast_in_dim.186), calls=%async_computation.5 | async-start | bytes 1572864 | tf_op jit(solution)/shard_map/all_to_all | solution.py:26
  503.0 11.7 %slice-start = ((s8[5373952]{0:T(1024)(128)(4,1)}), s8[1179648]{0:T(1024)(128)(4,1)S(1)}, s32[]{:S(2)}) async-start(s8[5373952]{0:T(1024)(128)(4,1)} %bitcast.453), calls=%async_computation.20 | async-start | bytes 2359296
  503.0 27.8 %all-to-all-start.17 = ((f32[32,4,768,3]{2,1,3,0:T(4,128)}), f32[32,4,768,3]{2,1,3,0:T(4,128)}, u32[]{:S(2)}, u32[]{:S(2)}) async-start(f32[32,4,768,3]{2,1,3,0:T(4,128)} %copy.339), calls=%async_computation.17 | async-start | bytes 2359296 | tf_op jit(solution)/shard_map/all_to_all | solution.py:76
  530.8 34.4 %all-to-all-start.12 = ((bf16[2,1,2048,326]{2,3,1,0:T(8,128)(2,1)}), bf16[2,1,2048,326]{2,3,1,0:T(8,128)(2,1)}, u32[]{:S(2)}, u32[]{:S(2)}) async-start(bf16[2,1,2048,326]{2,3,1,0:T(8,128)(2,1)} %bitcast.459), calls=%async_computation.12 | async-start | bytes 5373952 | tf_op jit(solution)/shard_map/all_to_all | solution.py:62
  541.0 7.0 copy-start.66
  541.0 7.1 copy-start.67
  548.0 5.1 copy-start.69
  551.1 14.1 %copy-start.45 = (f32[768,3]{0,1:T(4,128)}, f32[768,3]{0,1:T(4,128)S(1)}, u32[]{:S(2)}) copy-start(f32[768,3]{0,1:T(4,128)S(1)} %get-tuple-element.238) | copy-start | bytes 27652
  551.1 14.1 %copy-start.46 = (f32[768,3]{0,1:T(4,128)}, f32[768,3]{0,1:T(4,128)S(1)}, u32[]{:S(2)}) copy-start(f32[768,3]{0,1:T(4,128)S(1)} %get-tuple-element.239) | copy-start | bytes 27652
  553.2 12.1 %copy-start.47 = (f32[768,3]{0,1:T(4,128)}, f32[768,3]{0,1:T(4,128)S(1)}, u32[]{:S(2)}) copy-start(f32[768,3]{0,1:T(4,128)S(1)} %fusion.142) | copy-start | bytes 27652
  553.8 18.0 %copy-start.48 = (f32[3,768,3]{1,2,0:T(4,128)S(1)}, f32[3,768,3]{1,2,0:T(4,128)}, u32[]{:S(2)}) copy-start(f32[3,768,3]{1,2,0:T(4,128)} %param.52) | copy-start | bytes 82948
  565.2 53.6 %all-to-all-start.15 = ((f32[32,5,652,6]{2,3,1,0:T(8,128)}), f32[32,5,652,6]{2,3,1,0:T(8,128)}, u32[]{:S(2)}, u32[]{:S(2)}) async-start(f32[32,5,652,6]{2,3,1,0:T(8,128)} %copy.321), calls=%async_computation.15 | async-start | bytes 7864320 | tf_op jit(solution)/shard_map/all_to_all | solution.py:76
  571.3 113.6 %all-gather.5.cloned.1.call-start = ((), (), s32[]{:S(2)}) async-start(), calls=%async_computation.19 | async-start | bytes 1198080 | tf_op jit(solution)/shard_map/all_gather | solution.py:92
  571.8 5.7 copy-start.51
  571.8 6.4 copy-start.53
  571.9 6.4 copy-start.83
  571.9 6.4 copy-start.54
  571.9 6.4 copy-start.84
  571.9 9.5 %copy-start.61 = (f32[192]{0:T(256)S(1)}, f32[192]{0:T(256)}, u32[]{:S(2)}) copy-start(f32[192]{0:T(256)} %param.41) | copy-start | bytes 2308
  571.9 9.5 %copy-start.64 = (f32[192]{0:T(256)S(1)}, f32[192]{0:T(256)}, u32[]{:S(2)}) copy-start(f32[192]{0:T(256)} %copy-done.62) | copy-start | bytes 2308
  571.9 9.5 %copy-start.72 = (f32[192]{0:T(256)S(1)}, f32[192]{0:T(256)}, u32[]{:S(2)}) copy-start(f32[192]{0:T(256)} %param.42) | copy-start | bytes 2308
  571.9 9.5 %copy-start.88 = (f32[192]{0:T(256)S(1)}, f32[192]{0:T(256)}, u32[]{:S(2)}) copy-start(f32[192]{0:T(256)} %get-tuple-element.248) | copy-start | bytes 2308
  571.9 10.2 %copy-start.19 = (bf16[2,1,1024,192]{2,3,1,0:T(8,128)(2,1)S(1)}, bf16[2,1,1024,192]{2,3,1,0:T(8,128)(2,1)}, u32[]{:S(2)}) copy-start(bf16[2,1,1024,192]{2,3,1,0:T(8,128)(2,1)} %copy-done.18) | copy-start | bytes 2359300
  572.0 10.1 %copy-start.31 = (bf16[2,384,192]{1,2,0:T(8,128)(2,1)S(1)}, bf16[2,384,192]{1,2,0:T(8,128)(2,1)}, u32[]{:S(2)}) copy-start(bf16[2,384,192]{1,2,0:T(8,128)(2,1)} %copy-done.30) | copy-start | bytes 884740
  574.2 7.3 copy-start.89
  577.5 7.6 copy-start.58
  577.5 7.6 copy-start.85
  578.2 158.6 %all-gather.3.cloned.1.call-start = ((), (), s32[]{:S(2)}) async-start(), calls=%async_computation.18 | async-start | bytes 4792320 | tf_op jit(solution)/shard_map/all_gather | solution.py:318
  589.2 32.0 %copy-start.41 = (f32[5,652,6]{1,2,0:T(8,128)S(1)}, f32[5,652,6]{1,2,0:T(8,128)}, u32[]{:S(2)}) copy-start(f32[5,652,6]{1,2,0:T(8,128)} %param.46) | copy-start | bytes 234724
  589.2 32.0 %copy-start.42 = (f32[5,652,6]{1,2,0:T(8,128)S(1)}, f32[5,652,6]{1,2,0:T(8,128)}, u32[]{:S(2)}) copy-start(f32[5,652,6]{1,2,0:T(8,128)} %param.47) | copy-start | bytes 234724
  589.2 35.0 %copy-start.43 = (f32[5,652,6]{1,2,0:T(8,128)S(1)}, f32[5,652,6]{1,2,0:T(8,128)}, u32[]{:S(2)}) copy-start(f32[5,652,6]{1,2,0:T(8,128)} %param.48) | copy-start | bytes 234724
  589.2 35.0 %copy-start.44 = (f32[5,652,6]{1,2,0:T(8,128)S(1)}, f32[5,652,6]{1,2,0:T(8,128)}, u32[]{:S(2)}) copy-start(f32[5,652,6]{1,2,0:T(8,128)} %param.45) | copy-start | bytes 234724
  621.2 6.3 copy-start.38
  627.5 36.5 %copy-start.86 = (f32[2,2,384]{2,1,0:T(2,128)S(1)}, f32[2,2,384]{2,1,0:T(2,128)}, u32[]{:S(2)}) copy-start(f32[2,2,384]{2,1,0:T(2,128)} %param.40) | copy-start | bytes 18436
  627.5 47.9 %copy-start.87 = (f32[2,2,326]{2,1,0:T(2,128)S(1)}, f32[2,2,326]{2,1,0:T(2,128)}, u32[]{:S(2)}) copy-start(f32[2,2,326]{2,1,0:T(2,128)} %param.37) | copy-start | bytes 15652
  627.5 48.5 %copy-start.80 = (f32[326]{0:T(512)S(1)}, f32[326]{0:T(512)}, u32[]{:S(2)}) copy-start(f32[326]{0:T(512)} %get-tuple-element.205) | copy-start | bytes 3916
  652.9 21.6 %all-to-all-start.13 = ((f32[64,1,652]{2,1,0:T(1,128)}), f32[64,1,652]{2,1,0:T(1,128)S(1)}, u32[]{:S(2)}, u32[]{:S(2)}) async-start(f32[64,1,652]{2,1,0:T(1,128)} %broadcast_in_dim.192), calls=%async_computation.13 | async-start | bytes 393216 | tf_op jit(solution)/shard_map/all_to_all | solution.py:26
  751.1 6.4 copy-start.90
  (50 other events, 156.3 us)
Sparse Core Ops, SparseCore 0:
  578.3 84.3 all-gather.4
  665.7 71.0 all-gather.2
where the time goes:
time: 787 us; the launch traced here: 773 us
  local copies, waits for them, and re-layouts  201 us (26%)
  waiting for transfers between devices  169 us (21%)
  other arithmetic  122 us (16%)
  matrix products  116 us (15%)
  starting transfers between devices  94.8 us (12%)
  blocking collectives  54.3 us (7%)
  between operations  16.6 us (2%)
    all_to_all x9, waiting for transfers between devices, sent_to_all(): lax.all_to_all(jnp.broadcast_to(array[None], (count, *array.shape)), axis...  78.4 us
    gather x15, local copies, waits for them, and re-layouts, to_owner(): return jnp.take(blocks, order_list, axis=len(leading)).reshape(matrix.shape)  61.9 us
    all_to_all x9, starting transfers between devices, sent_to_all(): lax.all_to_all(jnp.broadcast_to(array[None], (count, *array.shape)), axis...  60.3 us
    all_to_all x2, blocking collectives, sent_to_all(): lax.all_to_all(jnp.broadcast_to(array[None], (count, *array.shape)), axis...  38.7 us
    dot_general x8, matrix products, convolve(): lax.dot_general(padded[:, tap_index:tap_index + length], weight[tap_index...  35.9 us
    all_to_all x2, waiting for transfers between devices, sum_in_two_steps(): lax.all_to_all(nearer, far, split_axis=0, concat_axis=0, tiled=True)  33.9 us
    dot_general x8, matrix products, convolve_back(): lax.dot_general(padded[:, start:start + length], weight[tap_index], (((2,...  33.4 us
    all_gather x1, waiting for transfers between devices, local(): lax.all_gather(first_result[0].astype(jnp.bfloat16), SEQ, axis=2, tiled=T...  33.4 us
  transfers between devices with their start and end apart: 17, of which 13 were waited for; matrix products, arithmetic and copies ran while one was open for 35% of the time, Pallas kernels for 0%

commit v1 on v0

v1 whole, which is shorter than its diff:
```python
import math

import jax
import jax.numpy as jnp
import numpy as np
from jax import lax
from jax.experimental import pallas as pl
from jax.experimental.pallas import tpu as pltpu
from jax.sharding import Mesh
from jax.sharding import PartitionSpec as P

STEP = 8
SEQ = ("seq_0", "seq_1", "seq_2", "seq_3")
SEQ_CH = ("seq_0", "seq_1", "seq_2", "seq_3", "ch")
MESH = pl.DeviceIdType.MESH
bf16 = jnp.bfloat16
f32 = jnp.float32

eps_norm = 1e-05
beta_one = 0.9
beta_two = 0.95
adam_eps = 1e-08
decay_rate = 0.01
average_rate = 0.9
norm_rate = 0.05

C0, C1, H = 652, 768, 384
HALF0, HALF1, HALFH = 326, 384, 192
BINS = 1024
OWN = 512
WIN = 528
LANES = 1152
PAD = 768

GELU_K = math.sqrt(2.0 / math.pi)
GELU_C = 0.044715


def gelu(v):
    return 0.5 * v * (1.0 + jnp.tanh(GELU_K * (v + GELU_C * (v * v * v))))


def gelu_slope(v):
    square = v * v
    t = jnp.tanh(GELU_K * v * (1.0 + GELU_C * square))
    return 0.5 * (1.0 + t) + 0.5 * GELU_K * v * (1.0 - t * t) * (1.0 + 3.0 * GELU_C * square)


def dot(a, b, dims=((1,), (0,))):
    return lax.dot_general(a, b, (dims, ((), ())), preferred_element_type=f32)


def iota(shape, dim):
    return lax.broadcasted_iota(jnp.int32, shape, dim)


class Place:
    def __init__(self):
        self.x, self.y, self.zh, self.c, self.zl = [lax.axis_index(n) for n in SEQ_CH]
        self.z = 2 * self.zh + self.zl
        self.e = 2 * self.z + self.c
        self.g = 4 * self.x + self.y

    def at(self, **other):
        v = {"x": self.x, "y": self.y, "z": self.z, "c": self.c}
        v.update(other)
        z = v["z"]
        return (v["x"], v["y"], lax.div(z, 2), v["c"], lax.rem(z, 2))


def remote(src, dst, send, recv, device):
    return pltpu.make_async_remote_copy(
        src_ref=src, dst_ref=dst, send_sem=send, recv_sem=recv, device_id=device, device_id_type=MESH
    )


def column_peers(p):
    out = []
    for k in range(1, 8):
        z = lax.rem(p.z + k // 2, 4)
        c = lax.rem(p.c + k % 2, 2)
        out.append((p.at(z=z, c=c), z, c))
    return out


def plane_peers(p):
    out = []
    for k in range(1, 16):
        x = lax.rem(p.x + k // 4, 4)
        y = lax.rem(p.y + k % 4, 4)
        out.append((p.at(x=x, y=y), x, y))
    return out


class Total:
    def __init__(self, p, bufs, sems):
        self.p = p
        self.b1, self.b2 = bufs
        self.s1, self.r1, self.s2, self.r2 = sems

    def start(self, value):
        p = self.p
        self.b1[p.e] = value
        self.c1 = []
        for k, (device, _, _) in enumerate(column_peers(p)):
            cp = remote(self.b1.at[p.e], self.b1.at[p.e], self.s1.at[k], self.r1.at[p.e], device)
            cp.start()
            self.c1.append(cp)

    def middle(self):
        p = self.p
        for device, z, c in column_peers(p):
            e = 2 * z + c
            remote(self.b1.at[e], self.b1.at[e], self.s1.at[0], self.r1.at[e], device).wait_recv()
        total = self.b1[0]
        for k in range(1, 8):
            total = total + self.b1[k]
        for cp in self.c1:
            cp.wait_send()
        self.b2[p.g] = total
        self.c2 = []
        for k, (device, _, _) in enumerate(plane_peers(p)):
            cp = remote(self.b2.at[p.g], self.b2.at[p.g], self.s2.at[k], self.r2.at[p.g], device)
            cp.start()
            self.c2.append(cp)

    def end(self):
        p = self.p
        for device, x, y in plane_peers(p):
            g = 4 * x + y
            remote(self.b2.at[g], self.b2.at[g], self.s2.at[0], self.r2.at[g], device).wait_recv()
        total = self.b2[0]
        for k in range(1, 16):
            total = total + self.b2[k]
        for cp in self.c2:
            cp.wait_send()
        return total


TAP_CORE = (0, 0, 1, 1, 0)
UNIT_CORE = (0, 1, 0, 1)


def step_kernel(
    xt, offs, cot, w1, w2, wp, pvec, owners_row, e1, bw1, e2, bw2,
    out, gin, s1, s2, stats,
    xw, raw, aa, ww1, ww2, wwp, pooled, diff, cc, mm, hid, og, no, hh, mid, gg, gp, perm,
    slope, sl_send, sl_home, ob, small, offw, acc, tr,
    a1a, a1b, ab1, ab2,
    ss, rs, ls, as1, ar1, as2, ar2,
):
    p = Place()
    c, zl = p.c, p.zl
    flip = p.at(z=3 - p.z)
    direct = p.at(z=p.z + 1 - 2 * zl)
    other_core = p.at(c=1 - c)

    bar = pltpu.get_barrier_semaphore()
    for device, _, _ in column_peers(p):
        pl.semaphore_signal(bar, inc=1, device_id=device, device_id_type=MESH)
    for device, _, _ in plane_peers(p):
        pl.semaphore_signal(bar, inc=1, device_id=device, device_id_type=MESH)

    own_w = [
        pltpu.make_async_copy(w1, ww1.at[:, :, pl.ds(pl.multiple_of(384 * zl, 128), 384)], ls.at[0]),
        pltpu.make_async_copy(w2, ww2.at[:, pl.ds(pl.multiple_of(192 * zl, 16), 192), :], ls.at[1]),
        pltpu.make_async_copy(wp, wwp.at[pl.ds(pl.multiple_of(192 * zl, 16), 192), :], ls.at[2]),
    ]
    for cp in own_w:
        cp.start()

    pl.semaphore_wait(bar, 22)

    is_self = c == zl
    not_self = c != zl
    home_chip = 2 * p.zh + c

    def window(j):
        return xt.at[:, pl.ds(pl.multiple_of(896 * j, 128), LANES)]

    def cot_window(j):
        return cot.at[pl.ds(pl.multiple_of(496 * j, 16), WIN), :]

    cc_mine = cc.at[:, pl.ds(pl.multiple_of(384 * zl, 128), 384)]
    x_a = remote(window(c), xw.at[zl], ss.at[0], rs.at[0 + zl], p.at(z=home_chip, c=c))
    x_b = remote(window(1 - c), xw.at[zl], ss.at[1], rs.at[0 + zl], p.at(z=home_chip, c=1 - c))
    c_a = remote(cot_window(c), cc_mine, ss.at[2], rs.at[2 + zl], p.at(z=home_chip, c=c))
    c_b = remote(cot_window(1 - c), cc_mine, ss.at[3], rs.at[2 + zl], p.at(z=home_chip, c=1 - c))
    o_a = remote(offs, offw, ss.at[4], rs.at[4], other_core)

    @pl.when(not_self)
    def _():
        x_a.start()

    @pl.when(is_self)
    def _():
        pltpu.make_async_copy(window(c), xw.at[zl], rs.at[0 + zl]).start()

    x_b.start()
    o_a.start()

    my_lanes = pl.ds(pl.multiple_of(384 * zl, 128), 384)
    its_lanes = pl.ds(pl.multiple_of(384 - 384 * zl, 128), 384)
    my_rows = pl.ds(pl.multiple_of(192 * zl, 16), 192)
    its_rows = pl.ds(pl.multiple_of(192 - 192 * zl, 16), 192)

    def tap_over(t):
        to = direct if t == 4 else flip
        return remote(w1.at[t], ww1.at[t, :, my_lanes], ss.at[5 + t], rs.at[5 + t], to)

    def tap_here(t):
        return remote(
            ww1.at[t, :, its_lanes], ww1.at[t, :, its_lanes], ss.at[10 + t], rs.at[10 + t], other_core
        )

    def unit_ref(u, rows):
        return ww2.at[u, rows, :] if u < 3 else wwp.at[rows, :]

    def unit_over(u):
        return remote(
            w2.at[u] if u < 3 else wp, unit_ref(u, my_rows), ss.at[15 + u], rs.at[15 + u], flip
        )

    def unit_here(u):
        return remote(
            unit_ref(u, its_rows), unit_ref(u, its_rows), ss.at[19 + u], rs.at[19 + u], other_core
        )

    for t in range(5):
        pl.when(c == TAP_CORE[t])(lambda t=t: tap_over(t).start())

    @pl.when(not_self)
    def _():
        c_a.start()

    @pl.when(is_self)
    def _():
        pltpu.make_async_copy(cot_window(c), cc_mine, rs.at[2 + zl]).start()

    c_b.start()
    for u in range(4):
        pl.when(c == UNIT_CORE[u])(lambda u=u: unit_over(u).start())

    off_home = offs[0:1, 0:1]
    total_s = jnp.zeros((8, HALF0), f32)
    total_q = jnp.zeros((8, HALF0), f32)
    for k in range(8):
        lanes = pl.ds(256 * k, 256)
        mask = ((iota((8, 256), 1) + 256 * k).astype(f32) >= 2.0 * off_home).astype(bf16)
        xb = xt[:, lanes]
        xf = xb.astype(f32)
        sq = xf * xf
        hi = sq.astype(bf16)
        lo = (sq - hi.astype(f32)).astype(bf16)
        nt = ((1,), (1,))
        total_s = total_s + dot(mask, xb, nt)
        total_q = total_q + (dot(mask, hi, nt) + dot(mask, lo, nt))
    small[...] = jnp.zeros_like(small)
    small[0:1, 0:HALF0] = total_s[0:1]
    small[1:2, 0:HALF0] = total_q[0:1]
    here = small[...]
    here = jnp.where(zl == 0, here, pltpu.roll(here, HALF0, 1))
    count = jnp.maximum(BINS - off_home, 0.0)
    lane8 = iota((8, PAD), 1)
    row8 = iota((8, PAD), 0)
    here = here + jnp.where((lane8 == PAD - 1) & (row8 == 0), count, 0.0)
    t1 = Total(p, (a1a, a1b), (as1.at[0], ar1.at[0], as2.at[0], ar2.at[0]))
    t1.start(here + pvec[...])
    t1.middle()

    nat1 = dot(owners_row[...], e1[...])[0:1] * 6.0 + bw1[0:1]
    nat2 = dot(owners_row[...], e2[...])[0:1] * 3.0 + bw2[0:1]
    for k in range(6):
        perm[pl.ds(128 * k, 128), :] = (
            (iota((128, PAD), 0) + 128 * k).astype(f32) == nat1
        ).astype(bf16)
    perm2 = (iota((H, H), 0).astype(f32) == nat2).astype(bf16)

    row = iota((128, 128), 0)
    pick = (iota((128, 128), 1) == jnp.where(row < 64, 2 * row, 2 * row - 127)).astype(bf16)
    for k in range(2):
        remote(xw.at[k], xw.at[k], ss.at[0], rs.at[0 + k], other_core).wait_recv()
    tr[...] = jnp.zeros_like(tr)
    for k in range(9):
        lanes = pl.ds(128 * k, 128)
        tr[0, :, 0:HALF0] = dot(pick, xw[0, :, lanes], ((1,), (1,)))
        tr[1, :, 0:HALF0] = dot(pick, xw[1, :, lanes], ((1,), (1,)))
        both = (tr[0] + pltpu.roll(tr[1], HALF0, 1)).astype(bf16)
        raw[0, pl.ds(64 * k, 64), :] = both[0:64]
        raw[1, pl.ds(64 * k, 64), :] = both[64:128]

    first = t1.end()
    n1 = first[0:1, PAD - 1 : PAD]
    n2 = 0.5 * n1
    inv_n1 = 1.0 / n1
    inv_n2 = 1.0 / n2
    real = iota((1, PAD), 1) < C0
    mean1 = jnp.where(real, first[0:1], 0.0) * inv_n1
    var1 = first[1:2] * inv_n1 - mean1 * mean1
    rs1 = lax.rsqrt(var1 + eps_norm)
    gain1, bias1 = first[2:3], first[3:4]
    gain2, bias2 = first[4:5], first[5:6]
    gain3, bias3 = first[6:7, 0:H], first[6:7, H : 2 * H]

    remote(offs, offw, ss.at[4], rs.at[4], other_core).wait()
    off = jnp.where(is_self, offs[0:1, 0:1], offw[0:1, 0:1])

    bin0 = 496 * c
    own0 = pl.multiple_of(16 * c, 16)
    raw0 = pl.multiple_of(48 * c, 16)
    rawown = pl.multiple_of(64 * c, 16)

    def valid_mask(rows, at=0):
        return ((iota((rows, 1), 0) + (bin0 + at)).astype(f32) >= off).astype(f32)

    def own_mask(rows, at=0):
        r = iota((rows, 1), 0) + at
        return ((r >= 16 * c) & (r < 16 * c + OWN)).astype(f32)

    not_first = (iota((WIN, 1), 0) > 0).astype(f32)
    not_last = (iota((WIN, 1), 0) < WIN - 1).astype(f32)

    def before(v):
        return (pltpu.roll(v, 1, 0) * not_first).astype(bf16)

    def after(v):
        return (pltpu.roll(v, WIN - 1, 0) * not_last).astype(bf16)

    small[0:1] = rs1 * gain1
    small[1:2] = bias1 - mean1 * (rs1 * gain1)
    small[2:3] = mean1
    small[3:4] = rs1

    @pl.loop(0, 6)
    def _(k):
        lanes = pl.ds(pl.multiple_of(128 * k, 128), 128)
        scale, shift = small[0:1, lanes], small[1:2, lanes]
        valid = valid_mask(WIN)
        for par in range(2):
            v = raw[par, pl.ds(raw0, WIN), lanes].astype(f32)
            v = gelu(v * scale + shift) * valid
            aa[par, :, lanes] = before(v)
            aa[2 + par, :, lanes] = v.astype(bf16)
            aa[4 + par, :, lanes] = after(v)

    own_w[0].wait()
    for t in range(5):

        def there(t=t):
            cp = tap_over(t)
            remote(
                ww1.at[t, :, its_lanes], ww1.at[t, :, its_lanes], ss.at[5 + t], rs.at[5 + t], flip
            ).wait_recv()
            tap_here(t).start()
            cp.wait_send()

        pl.when(c == TAP_CORE[t])(there)
    for t in range(5):
        pl.when(c == TAP_CORE[t])(lambda t=t: tap_here(t).wait_send())
        pl.when(c != TAP_CORE[t])(lambda t=t: tap_here(t).wait_recv())

    acc[...] = jnp.zeros_like(acc)

    @pl.loop(0, 3)
    def _(k):
        rows = pl.ds(pl.multiple_of(176 * k, 16), 176)
        h0 = jnp.zeros((176, C1), f32)
        for t in range(5):
            h0 = h0 + dot(aa[t, rows, 0:C0], ww1[t])
        h1 = jnp.zeros((176, C1), f32)
        for t in range(5):
            h1 = h1 + dot(aa[t + 1, rows, 0:C0], ww1[t])
        d = h0 - h1
        v = jnp.maximum(h0, h1) + (jnp.log(1.0 + jnp.exp(-jnp.abs(d))) - math.log(2.0))
        diff[rows, :] = d
        pooled[rows, :] = v
        m = valid_mask(176, 176 * k) * own_mask(176, 176 * k)
        vm = v * m
        acc[0:1] += jnp.sum(vm, axis=0, keepdims=True)
        acc[1:2] += jnp.sum(vm * v, axis=0, keepdims=True)

    t2 = Total(p, (ab1.at[0], ab2.at[0]), (as1.at[1], ar1.at[1], as2.at[1], ar2.at[1]))
    t2.start(acc[0:2])
    t2.middle()
    own_w[1].wait()
    own_w[2].wait()
    for u in range(4):

        def there_u(u=u):
            remote(
                unit_ref(u, its_rows), unit_ref(u, its_rows), ss.at[15 + u], rs.at[15 + u], flip
            ).wait_recv()
            unit_here(u).start()
            unit_over(u).wait_send()

        pl.when(c == UNIT_CORE[u])(there_u)
    for k in range(2):
        part = cc.at[:, pl.ds(384 * k, 384)]
        remote(part, part, ss.at[0], rs.at[2 + k], other_core).wait_recv()
    for u in range(4):
        pl.when(c == UNIT_CORE[u])(lambda u=u: unit_here(u).wait_send())
        pl.when(c != UNIT_CORE[u])(lambda u=u: unit_here(u).wait_recv())
    og[...] = dot(cc[...], wwp[...], ((1,), (1,)))

    @pl.when(not_self)
    def _():
        x_a.wait_send()
        c_a.wait_send()

    x_b.wait_send()
    c_b.wait_send()

    second = t2.end()
    mean2 = second[0:1] * inv_n2
    var2 = second[1:2] * inv_n2 - mean2 * mean2
    rs2 = lax.rsqrt(var2 + eps_norm)
    acc[2:3] = rs2 * gain2
    acc[3:4] = bias2 - mean2 * (rs2 * gain2)
    acc[4:5] = mean2
    acc[5:6] = rs2

    @pl.loop(0, 6)
    def _(k):
        lanes = pl.ds(pl.multiple_of(128 * k, 128), 128)
        v = gelu(pooled[:, lanes] * acc[2:3, lanes] + acc[3:4, lanes]) * valid_mask(WIN)
        mm[0, :, lanes] = before(v)
        mm[1, :, lanes] = v.astype(bf16)
        mm[2, :, lanes] = after(v)

    h2 = jnp.zeros((WIN, H), f32)
    for t in range(3):
        h2 = h2 + dot(mm[t], ww2[t], ((1,), (1,)))
    hid[...] = h2
    m = valid_mask(WIN) * own_mask(WIN)
    h2m = h2 * m
    acc[6:7, 0:H] = jnp.sum(h2m, axis=0, keepdims=True)
    acc[6:7, H : 2 * H] = jnp.sum(h2m * h2, axis=0, keepdims=True)
    t3 = Total(p, (ab1.at[1], ab2.at[1]), (as1.at[2], ar1.at[2], as2.at[2], ar2.at[2]))
    t3.start(acc[6:8])
    t3.middle()
    third = t3.end()
    mean3 = third[0:1, 0:H] * inv_n2
    var3 = third[0:1, H : 2 * H] * inv_n2 - mean3 * mean3
    rs3 = lax.rsqrt(var3 + eps_norm)
    valid = valid_mask(WIN)
    own = own_mask(WIN)
    h2 = hid[...]
    scaled = (h2 - mean3) * rs3
    pre = scaled * gain3 + bias3
    no[...] = (gelu(pre) * valid).astype(bf16)
    slopes = gelu_slope(pre) * og[...] * valid
    og[...] = slopes
    hid[...] = scaled
    acc[6:7, 0:H] = jnp.sum(slopes * scaled * own, axis=0, keepdims=True)
    acc[6:7, H : 2 * H] = jnp.sum(slopes * own, axis=0, keepdims=True)
    t4 = Total(p, (ab1.at[2], ab2.at[2]), (as1.at[3], ar1.at[3], as2.at[3], ar2.at[3]))
    t4.start(acc[6:8])
    ob[...] = (pooled[...] + dot(no[...], wwp[...])).astype(bf16)
    t4.middle()
    out_rows = pl.ds(pl.multiple_of(512 * c, 16), OWN)
    own_rows = pl.ds(own0, OWN)

    def out_copy(k):
        return remote(
            ob.at[own_rows, pl.ds(384 * k, 384)],
            out.at[out_rows, :],
            ss.at[23 + k],
            rs.at[23 + c],
            p.at(z=2 * p.zh + k, c=zl),
        )

    def to_self(k):
        return (zl == k) & is_self

    for k in range(2):
        pl.when(jnp.logical_not(to_self(k)))(lambda k=k: out_copy(k).start())

        def local(k=k):
            pltpu.make_async_copy(
                ob.at[own_rows, pl.ds(384 * k, 384)], out.at[out_rows, :], rs.at[23 + c]
            ).start()

        pl.when(to_self(k))(local)

    def put2(m, value):
        s2[:, pl.ds(24 * m, 24), :] = value.astype(bf16).reshape(16, 24, C1)

    tn = ((0,), (0,))
    nop = dot(no[own_rows, :], perm2).astype(bf16)
    put2(3, dot(nop, cc[own_rows, :], tn))
    fourth = t4.end()
    stats[4:5] = fourth[0:1]
    gain_mean = fourth[0:1, 0:H] * inv_n2
    bias_mean = fourth[0:1, H : 2 * H] * inv_n2
    hg = valid_mask(WIN) * (gain3 * rs3) * (og[...] - bias_mean - hid[...] * gain_mean)
    hh[0] = after(hg)
    hh[1] = hg.astype(bf16)
    hh[2] = before(hg)
    mid_grad = jnp.zeros((WIN, C1), f32)
    for t in range(3):
        mid_grad = mid_grad + dot(hh[t], ww2[t])
    mid[...] = mid_grad

    @pl.loop(0, 6)
    def _(k):
        lanes = pl.ds(pl.multiple_of(128 * k, 128), 128)
        v = pooled[:, lanes]
        slopes = gelu_slope(v * acc[2:3, lanes] + acc[3:4, lanes]) * mid[:, lanes] * valid_mask(WIN)
        scaled = (v - acc[4:5, lanes]) * acc[5:6, lanes]
        mid[:, lanes] = slopes
        pooled[:, lanes] = scaled
        mine = slopes * own_mask(WIN)
        acc[0:1, lanes] = jnp.sum(mine * scaled, axis=0, keepdims=True)
        acc[1:2, lanes] = jnp.sum(mine, axis=0, keepdims=True)

    t5 = Total(p, (ab1.at[3], ab2.at[3]), (as1.at[4], ar1.at[4], as2.at[4], ar2.at[4]))
    t5.start(acc[0:2])
    hp = dot(hh[1, own_rows, :], perm2).astype(bf16)
    put2(0, dot(hp, mm[0, own_rows, :], tn))
    t5.middle()
    for t in range(1, 3):
        put2(t, dot(hp, mm[t, own_rows, :], tn))
    fifth = t5.end()
    stats[2:4] = fifth
    acc[0:2] = fifth * inv_n2

    @pl.loop(0, 6)
    def _(k):
        lanes = pl.ds(pl.multiple_of(128 * k, 128), 128)
        back = acc[2:3, lanes] * (
            mid[:, lanes] - acc[1:2, lanes] - pooled[:, lanes] * acc[0:1, lanes]
        )
        pg = cc[:, lanes].astype(f32) + back * valid_mask(WIN)
        even = 1.0 / (1.0 + jnp.exp(-diff[:, lanes]))
        ge = pg * even
        go = pg * (1.0 - even)
        gg[0, :, lanes] = after(go)
        gg[1, :, lanes] = after(ge)
        gg[2, :, lanes] = go.astype(bf16)
        gg[3, :, lanes] = ge.astype(bf16)
        gg[4, :, lanes] = before(go)
        gg[5, :, lanes] = before(ge)

    gp[0] = dot(gg[3, own_rows, :], perm[...]).astype(bf16)
    gp[1] = dot(gg[2, own_rows, :], perm[...]).astype(bf16)
    for t in range(5):
        part = dot(gp[0], aa[t, own_rows, 0:C0], tn) + dot(gp[1], aa[t + 1, own_rows, 0:C0], tn)
        s1[t, :, 0:C0] = part.astype(bf16)
        s1[t, :, C0:PAD] = jnp.zeros((C1, PAD - C0), bf16)

    small[4:6] = jnp.zeros((2, PAD), f32)
    for par in range(2):
        for k in range(2):
            rows = pl.ds(pl.multiple_of(own0 + 256 * k, 16), 256)
            v = jnp.zeros((256, C0), f32)
            for t in range(5):
                v = v + dot(gg[t + 1 - par, rows, :], ww1[t], ((1,), (1,)))
            slope[:, 0:C0] = v
            slope[:, C0:PAD] = jnp.zeros((256, PAD - C0), f32)

            @pl.loop(0, 6)
            def _(q, par=par, k=k):
                lanes = pl.ds(pl.multiple_of(128 * q, 128), 128)
                xv = raw[par, pl.ds(pl.multiple_of(rawown + 256 * k, 16), 256), lanes].astype(f32)
                valid = valid_mask(256, 16 * c + 256 * k)
                slopes = gelu_slope(xv * small[0:1, lanes] + small[1:2, lanes]) * slope[:, lanes] * valid
                scaled = (xv - small[2:3, lanes]) * small[3:4, lanes]
                slope[:, lanes] = slopes
                small[4:5, lanes] += jnp.sum(slopes * scaled, axis=0, keepdims=True)
                small[5:6, lanes] += jnp.sum(slopes, axis=0, keepdims=True)

            dst = pl.ds(256 * k, 256)
            sl_send[0, par, dst, :] = slope[:, 0:384].astype(bf16)
            sl_send[1, par, dst, :] = pltpu.roll(slope[...], PAD - HALF0, 1)[:, 0:384].astype(bf16)

    t6 = Total(p, (ab1.at[4], ab2.at[4]), (as1.at[5], ar1.at[5], as2.at[5], ar2.at[5]))
    t6.start(small[4:6])

    def slope_copy(k):
        return remote(
            sl_send.at[k], sl_home.at[c], ss.at[25 + k], rs.at[25 + c], p.at(z=2 * p.zh + k, c=zl)
        )

    for k in range(2):
        pl.when(jnp.logical_not(to_self(k)))(lambda k=k: slope_copy(k).start())

        def local_s(k=k):
            pltpu.make_async_copy(sl_send.at[k], sl_home.at[c], rs.at[25 + c]).start()

        pl.when(to_self(k))(local_s)
    t6.middle()
    sixth = t6.end()
    stats[0:2] = sixth
    stats[5:8] = jnp.zeros((3, PAD), f32)

    small[4:6] = sixth * inv_n1
    small[6:7] = rs1 * gain1
    vec = small[...]
    vec = jnp.where(zl == 0, vec, pltpu.roll(vec, PAD - HALF0, 1))
    tr[0, 0:8, :] = vec
    cols = jnp.transpose(tr[0, :, 0:384])
    mean_c = cols[0:HALF0, 2:3]
    rs_c = cols[0:HALF0, 3:4]
    gm_c = cols[0:HALF0, 4:5]
    bm_c = cols[0:HALF0, 5:6]
    scale_c = cols[0:HALF0, 6:7]
    for j in range(2):
        remote(sl_home.at[j], sl_home.at[j], ss.at[0], rs.at[25 + j], other_core).wait_recv()
    rowq = iota((128, 256), 0)
    laneq = iota((128, 256), 1)
    put_even = (laneq == 2 * rowq).astype(bf16)
    put_odd = (laneq == 2 * rowq + 1).astype(bf16)
    for j in range(2):
        for k in range(4):
            bins = pl.ds(128 * k, 128)
            st = dot(sl_home[j, 0, bins, :], put_even, tn) + dot(sl_home[j, 1, bins, :], put_odd, tn)
            lanes = pl.ds(1024 * j + 256 * k, 256)
            xf = xt[:, lanes].astype(f32)
            scaled = (xf - mean_c) * rs_c
            ok = ((iota((1, 256), 1) + (1024 * j + 256 * k)).astype(f32) >= 2.0 * off_home).astype(f32)
            gin[:, lanes] = ok * (scale_c * (st[0:HALF0] - bm_c - scaled * gm_c))

    for k in range(2):

        def sent(k=k):
            out_copy(k).wait_send()
            slope_copy(k).wait_send()

        pl.when(jnp.logical_not(to_self(k)))(sent)
    for j in range(2):
        rows = out.at[pl.ds(512 * j, 512), :]
        remote(rows, rows, ss.at[0], rs.at[23 + j], other_core).wait_recv()


VMEM = pl.BlockSpec(memory_space=pltpu.VMEM)
ANY = pl.BlockSpec(memory_space=pl.ANY)


def run_step(xt, offs, cot, w1, w2, wp, pvec, owners_row, consts):
    shape = jax.ShapeDtypeStruct
    dma = pltpu.SemaphoreType.DMA
    scratch = [
        pltpu.VMEM((2, HALF0, LANES), bf16),
        pltpu.VMEM((2, 576, PAD), bf16),
        pltpu.VMEM((6, WIN, PAD), bf16),
        pltpu.VMEM((5, C0, C1), bf16),
        pltpu.VMEM((3, H, C1), bf16),
        pltpu.VMEM((H, C1), bf16),
        pltpu.VMEM((WIN, C1), f32),
        pltpu.VMEM((WIN, C1), f32),
        pltpu.VMEM((WIN, C1), bf16),
        pltpu.VMEM((3, WIN, C1), bf16),
        pltpu.VMEM((WIN, H), f32),
        pltpu.VMEM((WIN, H), f32),
        pltpu.VMEM((WIN, H), bf16),
        pltpu.VMEM((3, WIN, H), bf16),
        pltpu.VMEM((WIN, C1), f32),
        pltpu.VMEM((6, WIN, C1), bf16),
        pltpu.VMEM((2, OWN, C1), bf16),
        pltpu.VMEM((C1, C1), bf16),
        pltpu.VMEM((256, PAD), f32),
        pltpu.VMEM((2, 2, OWN, 384), bf16),
        pltpu.VMEM((2, 2, OWN, 384), bf16),
        pltpu.VMEM((WIN, C1), bf16),
        pltpu.VMEM((8, PAD), f32),
        pltpu.VMEM((8, 128), f32),
        pltpu.VMEM((8, PAD), f32),
        pltpu.VMEM((2, 128, PAD), f32),
        pltpu.VMEM((8, 8, PAD), f32),
        pltpu.VMEM((16, 8, PAD), f32),
        pltpu.VMEM((5, 8, 2, PAD), f32),
        pltpu.VMEM((5, 16, 2, PAD), f32),
        dma((32,)),
        dma((32,)),
        dma((4,)),
        dma((6, 8)),
        dma((6, 8)),
        dma((6, 16)),
        dma((6, 16)),
    ]
    return pl.pallas_call(
        step_kernel,
        out_shape=(
            shape((BINS, 384), bf16),
            shape((HALF0, 2 * BINS), f32),
            shape((5, C1, PAD), bf16),
            shape((16, 96, C1), bf16),
            shape((8, PAD), f32),
        ),
        in_specs=[VMEM, VMEM, ANY, ANY, ANY, ANY] + [VMEM] * 6,
        out_specs=(ANY, VMEM, VMEM, VMEM, VMEM),
        scratch_shapes=scratch,
        compiler_params=pltpu.CompilerParams(
            collective_id=0, has_side_effects=True, vmem_limit_bytes=63 * 2**20
        ),
    )(xt, offs, cot, w1, w2, wp, pvec, owners_row, consts["e1"], consts["bw1"], consts["e2"], consts["bw2"])


def adam_block(first, second, turned):
    first_new = beta_one * first + (1.0 - beta_one) * turned
    second_new = beta_two * second + (1.0 - beta_two) * turned * turned
    direction = (
        first_new
        / (1.0 - beta_one**STEP)
        / (jnp.sqrt(second_new / (1.0 - beta_two**STEP)) + adam_eps)
    )
    return first_new, second_new, direction


def master_block(master, update, rate, average):
    master_new = master - rate * (update + decay_rate * master)
    return master_new, average_rate * average + (1.0 - average_rate) * master_new


def tail_kernel(
    s1, s2, b1, b2, b3,
    m1, f1, q1, a1, m2, f2, q2, a2, m3, f3, q3, a3,
    owners_row, owners_col, rep1, rep2, ec1, bwc1, e3, bw3,
    cp1, cp2, cp3,
    nm1, nf1, nq1, na1, nm2, nf2, nq2, na2, nm3, nf3, nq3, na3,
    t1, t2, ra1, ua, ra2, rb1, rb2, ub1, ub2, rb3, rb4, pz, rz, dd, upd, nb, ga,
    ss, rs, ls,
):
    p = Place()
    x, y, zh, zl, z, c = p.x, p.y, p.zh, p.zl, p.z, p.c
    other_core = p.at(c=1 - c)
    xs = [(p.at(x=lax.rem(x + k, 4)), lax.rem(x + k, 4)) for k in (1, 2, 3)]
    ys = [(p.at(y=lax.rem(y + k, 4)), lax.rem(y + k, 4)) for k in (1, 2, 3)]
    column = column_peers(p)
    bar = pltpu.get_barrier_semaphore()
    for device, *_ in xs + ys + column:
        pl.semaphore_signal(bar, inc=1, device_id=device, device_id_type=MESH)
    pl.semaphore_wait(bar, 13)

    mine = pl.ds(pl.multiple_of(384 * c, 128), 384)
    others = pl.ds(pl.multiple_of(384 - 384 * c, 128), 384)
    ca = remote(s1.at[:, :, :, :, others], t1, ss.at[0], rs.at[0], other_core)
    cb = remote(s2.at[:, :, :, others], t2, ss.at[1], rs.at[1], other_core)
    ca.start()
    cb.start()
    ca.wait()
    cb.wait()
    for t in range(5):
        t1[t] = (t1[t].astype(f32) + s1[t, :, :, :, mine].astype(f32)).astype(bf16)
    t2[...] = (t2[...].astype(f32) + s2[:, :, :, mine].astype(f32)).astype(bf16)

    sent = []
    for k in range(3):
        xd, xi = xs[k]
        yd, yi = ys[k]
        sent.append(remote(t1.at[0:4, xi], ra1.at[k], ss.at[2 + k], rs.at[2 + k], xd))
        sent.append(remote(t1.at[4, :, yi], rb1.at[k], ss.at[5 + k], rs.at[5 + k], yd))
        sent.append(remote(t2.at[:, yi], rb2.at[k], ss.at[8 + k], rs.at[8 + k], yd))
    for cp in sent:
        cp.start()
    for cp in sent:
        cp.wait_recv()

    def total(own, parts):
        v = own.astype(f32)
        for k in range(3):
            v = v + parts[k].astype(f32)
        return v

    for t in range(4):
        ua[t] = total(t1[t, x], [ra1[k, t] for k in range(3)]).astype(bf16)
    ub1[...] = total(t1[4, :, y], [rb1[k] for k in range(3)]).astype(bf16)
    ub2[...] = total(t2[:, y], [rb2[k] for k in range(3)]).astype(bf16)
    late = []
    for k in range(3):
        xd, xi = xs[k]
        yd, yi = ys[k]
        late.append(remote(ua.at[:, yi], ra2.at[k], ss.at[11 + k], rs.at[11 + k], yd))
        late.append(remote(ub1.at[xi], rb3.at[k], ss.at[14 + k], rs.at[14 + k], xd))
        late.append(remote(ub2.at[xi], rb4.at[k], ss.at[17 + k], rs.at[17 + k], xd))
    for cp in late:
        cp.start()
    for cp in late:
        cp.wait_recv()
    va = total(ua[:, y], [ra2[k] for k in range(3)]).astype(bf16).reshape(192, 384)
    vb = total(ub1[x], [rb3[k] for k in range(3)]).astype(bf16)
    vc = total(ub2[x], [rb4[k] for k in range(3)]).astype(bf16)
    r1 = rep1[...]
    g1 = dot(r1[:, 0:192], va) + dot(r1[:, 192:240], vb)
    g2 = dot(rep2[...], vc)
    for e in range(8):
        pz[e, 0:48] = g1[48 * e : 48 * e + 48].astype(bf16)
        pz[e, 48:80] = g2[32 * e : 32 * e + 32].astype(bf16)
    near = []
    for k, (device, zi, ci) in enumerate(column):
        near.append(remote(pz.at[2 * zi + ci], rz.at[p.e], ss.at[20 + k], rs.at[20 + p.e], device))
    for cp in near:
        cp.start()
    rz[p.e] = pz[p.e]
    for device, zi, ci in column:
        e = 2 * zi + ci
        remote(rz.at[e], rz.at[e], ss.at[0], rs.at[20 + e], device).wait_recv()
    halves = []
    for half in range(2):
        v = rz[half].astype(f32)
        for k in range(1, 4):
            v = v + rz[2 * k + half].astype(f32)
        halves.append(v)
    grad = jnp.concatenate(halves, axis=1)

    nt = ((1,), (1,))
    basis1 = b1[...].astype(bf16)
    turned = dot(grad[0:40, 0:C0].astype(bf16), basis1)
    dd[...] = jnp.zeros_like(dd)
    for t in range(5):
        first_new, second_new, direction = adam_block(f1[t], q1[t], turned[8 * t : 8 * t + 6])
        nf1[t] = first_new
        nq1[t] = second_new
        dd[8 * t : 8 * t + 6, 0:C0] = direction
    update = dot(dd[0:40, 0:C0].astype(bf16), basis1, nt)
    nb[...] = jnp.zeros_like(nb)
    for t in range(5):
        master_new, average_new = master_block(m1[t], update[8 * t : 8 * t + 6], 0.02, a1[t])
        nm1[t] = master_new
        na1[t] = average_new
        nb[8 * t : 8 * t + 6, 0:C0] = master_new
    basis2 = b2[...].astype(bf16)
    turned = dot(grad[48:72].astype(bf16), basis2)
    for t in range(3):
        first_new, second_new, direction = adam_block(f2[t], q2[t], turned[8 * t : 8 * t + 3])
        nf2[t] = first_new
        nq2[t] = second_new
        dd[8 * t : 8 * t + 3, :] = direction
    update = dot(dd[0:24].astype(bf16), basis2, nt)
    for t in range(3):
        master_new, average_new = master_block(m2[t], update[8 * t : 8 * t + 3], 0.02, a2[t])
        nm2[t] = master_new
        na2[t] = average_new
        nb[40 + 4 * t : 43 + 4 * t, :] = master_new
    basis3 = b3[...].astype(bf16)
    turned = dot(grad[72:80].astype(bf16), basis3)
    first_new, second_new, direction = adam_block(f3[...], q3[...], turned[0:3])
    nf3[...] = first_new
    nq3[...] = second_new
    dd[0:8] = jnp.zeros((8, PAD), f32)
    dd[0:3] = direction
    update = dot(dd[0:8].astype(bf16), basis3, nt)
    master_new, average_new = master_block(m3[...], update[0:3], 0.05, a3[...])
    nm3[...] = master_new
    na3[...] = average_new
    nb[52:55, :] = master_new

    ga[c, x, y, zh] = nb[...].astype(bf16)
    mine_ga = ga.at[c, x, y, zh]
    zcp = remote(mine_ga, mine_ga, ss.at[28], rs.at[28], p.at(z=lax.rem(z + 2, 4)))
    zcp.start()
    zcp.wait()
    up, low = pl.ds(0, 32), pl.ds(32, 32)
    cps = []
    for k in range(3):
        xd, xi = xs[k]
        yd, yi = ys[k]
        va_ = ga.at[c, x, y, :, up]
        vb_ = ga.at[c, x, y, :, low]
        cps.append(remote(va_, va_, ss.at[29 + k], rs.at[29 + k], yd))
        cps.append(remote(vb_, vb_, ss.at[32 + k], rs.at[32 + k], xd))
    for cp in cps:
        cp.start()
    for k in range(3):
        yi = lax.rem(y + 3 - k, 4)
        xi = lax.rem(x + 3 - k, 4)
        va_ = ga.at[c, x, yi, :, up]
        vb_ = ga.at[c, xi, y, :, low]
        remote(va_, va_, ss.at[0], rs.at[29 + k], other_core).wait_recv()
        remote(vb_, vb_, ss.at[0], rs.at[32 + k], other_core).wait_recv()
    cps2 = []
    for k in range(3):
        xd, xi = xs[k]
        yd, yi = ys[k]
        va_ = ga.at[c, x, :, :, up]
        vb_ = ga.at[c, :, y, :, low]
        cps2.append(remote(va_, va_, ss.at[35 + k], rs.at[35 + k], xd))
        cps2.append(remote(vb_, vb_, ss.at[38 + k], rs.at[38 + k], yd))
    for cp in cps2:
        cp.start()

    natc = dot(ec1[...], owners_col[...]) * 6.0 + bwc1[...]
    lane = iota((512, 128), 1)
    place1 = jnp.concatenate(
        [((lane + 128 * k).astype(f32) == natc).astype(bf16) for k in range(3)], axis=1
    )
    natr = dot(owners_row[...], e3[...])[0:1] * 3.0 + bw3[0:1]
    place2 = (iota((768, 1024), 0).astype(f32) == natr).astype(bf16)
    for k in range(3):
        yi = lax.rem(y + 3 - k, 4)
        xi = lax.rem(x + 3 - k, 4)
        va_ = ga.at[c, xi, :, :, up]
        vb_ = ga.at[c, :, yi, :, low]
        remote(va_, va_, ss.at[0], rs.at[35 + k], other_core).wait_recv()
        remote(vb_, vb_, ss.at[0], rs.at[38 + k], other_core).wait_recv()
    both = remote(ga.at[c], ga.at[c], ss.at[41], rs.at[41], other_core)
    both.start()
    remote(ga.at[1 - c], ga.at[1 - c], ss.at[0], rs.at[41], other_core).wait_recv()
    tn = ((0,), (0,))
    for t in range(5):
        block = ga[:, :, :, :, 8 * t : 8 * t + 8, :].reshape(512, PAD)
        cp1[t] = dot(block[:, 0:C0], place1, tn).astype(bf16)
    block = ga[:, :, :, :, 40:56, :].reshape(1024, PAD)
    copy2 = dot(place2, block).astype(bf16)
    for t in range(3):
        cp2[t] = copy2[192 * t : 192 * t + 192]
    cp3[...] = copy2[576:768]
    for cp in sent + late + near + cps + cps2 + [both]:
        cp.wait_send()


def run_tail(s1, s2, bases, states, owners_row, owners_col, consts):
    shape = jax.ShapeDtypeStruct
    dma = pltpu.SemaphoreType.DMA
    scratch = [
        pltpu.VMEM((5, 4, 4, 48, 384), bf16),
        pltpu.VMEM((4, 4, 96, 384), bf16),
        pltpu.VMEM((3, 4, 4, 48, 384), bf16),
        pltpu.VMEM((4, 4, 48, 384), bf16),
        pltpu.VMEM((3, 4, 48, 384), bf16),
        pltpu.VMEM((3, 4, 48, 384), bf16),
        pltpu.VMEM((3, 4, 96, 384), bf16),
        pltpu.VMEM((4, 48, 384), bf16),
        pltpu.VMEM((4, 96, 384), bf16),
        pltpu.VMEM((3, 48, 384), bf16),
        pltpu.VMEM((3, 96, 384), bf16),
        pltpu.VMEM((8, 80, 384), bf16),
        pltpu.VMEM((8, 80, 384), bf16),
        pltpu.VMEM((40, PAD), f32),
        pltpu.VMEM((8, 128), f32),
        pltpu.VMEM((64, PAD), f32),
        pltpu.VMEM((2, 4, 4, 2, 64, PAD), bf16),
        dma((44,)),
        dma((44,)),
        dma((4,)),
    ]
    wide = [shape(a.shape, f32) for a in states]
    return pl.pallas_call(
        tail_kernel,
        out_shape=(
            shape((5, C0, 384), bf16),
            shape((3, HALFH, C1), bf16),
            shape((HALFH, C1), bf16),
            *wide,
        ),
        in_specs=[VMEM] * (5 + 12 + 8),
        out_specs=tuple([VMEM] * 15),
        scratch_shapes=scratch,
        compiler_params=pltpu.CompilerParams(
            collective_id=1, has_side_effects=True, vmem_limit_bytes=63 * 2**20
        ),
    )(
        s1, s2, *bases, *states, owners_row, owners_col,
        consts["rep1"], consts["rep2"], consts["ec1"], consts["bwc1"], consts["e3"], consts["bw3"],
    )


def make_consts():
    e1 = np.zeros((64, 768), np.float32)
    bw1 = np.zeros((8, 768), np.float32)
    e2 = np.zeros((64, 384), np.float32)
    bw2 = np.zeros((8, 384), np.float32)
    for s in range(64):
        g, zh, c = s // 4, (s // 2) % 2, s % 2
        for b in range(2):
            e = (2 * zh + b) * 2 + c
            for w in range(6):
                e1[s, (g * 8 + e) * 6 + w] = 1
                bw1[:, (g * 8 + e) * 6 + w] = b * 384 + w
            for w in range(3):
                e2[s, (g * 8 + e) * 3 + w] = 1
                bw2[:, (g * 8 + e) * 3 + w] = b * 192 + w
    rep1 = np.zeros((8 * 48, 240), np.float32)
    rep2 = np.zeros((8 * 32, 96), np.float32)
    for e in range(8):
        for t in range(5):
            for w in range(6):
                rep1[e * 48 + t * 8 + w, t * 48 + e * 6 + w] = 1
        for m in range(4):
            for w in range(3):
                rep2[e * 32 + m * 8 + w, m * 24 + e * 3 + w] = 1
    ec1 = np.zeros((512, 64), np.float32)
    bwc1 = np.full((512, 128), -4096.0, np.float32)
    e3 = np.zeros((64, 1024), np.float32)
    bw3 = np.full((8, 1024), -4096.0, np.float32)
    for k in range(64):
        c, g, zh = k // 32, (k // 2) % 16, k % 2
        s = g * 4 + zh * 2 + c
        ec1[8 * k : 8 * k + 8, s] = 1
        for w in range(6):
            bwc1[8 * k + w] = w
        e3[s, 16 * k : 16 * k + 16] = 1
        for m in range(4):
            for w in range(3):
                bw3[:, 16 * k + 4 * m + w] = 192 * m + w
    low = lambda a: jnp.asarray(a, bf16)
    return {
        "e1": low(e1), "bw1": jnp.asarray(bw1), "e2": low(e2), "bw2": jnp.asarray(bw2),
        "rep1": low(rep1), "rep2": low(rep2), "ec1": low(ec1), "bwc1": jnp.asarray(bwc1),
        "e3": low(e3), "bw3": jnp.asarray(bw3),
    }


def norm_adam(gradient, parameters, moments):
    first_new = beta_one * moments[0] + (1.0 - beta_one) * gradient
    second_new = beta_two * moments[1] + (1.0 - beta_two) * gradient * gradient
    direction = (
        first_new
        / (1.0 - beta_one**STEP)
        / (jnp.sqrt(second_new / (1.0 - beta_two**STEP)) + adam_eps)
    )
    return (parameters - norm_rate * direction, first_new, second_new)


def local(
    inputs, offsets, owners, cotangent,
    norm1_gain, norm1_bias, norm1_moments,
    norm2_gain, norm2_bias, norm2_moments,
    norm3_gain, norm3_bias, norm3_moments,
    conv1_copy, conv1_master, conv1_first, conv1_second, conv1_average, basis1,
    conv2_copy, conv2_master, conv2_first, conv2_second, conv2_average, basis2,
    project_copy, project_master, project_first, project_second, project_average, basis3,
):
    consts = make_consts()
    zl = lax.axis_index("ch")
    leader = lax.axis_index(SEQ) == 0

    def in_half(v, half, at=0):
        wide = jnp.zeros((PAD,), f32)
        return lax.dynamic_update_slice(wide, v, (at + zl * half,))

    rows = jnp.stack(
        [
            in_half(norm1_gain, HALF0),
            in_half(norm1_bias, HALF0),
            in_half(norm2_gain, HALF1),
            in_half(norm2_bias, HALF1),
            in_half(norm3_gain, HALFH) + in_half(norm3_bias, HALFH, H),
        ]
    )
    pvec = jnp.pad(jnp.where(leader, rows, 0.0), ((2, 1), (0, 0)))
    offs = jnp.broadcast_to(offsets.astype(f32)[:, None], (8, 128))
    owners_low = owners.astype(bf16)
    owners_row = jnp.broadcast_to(owners_low[None], (8, 64))
    owners_col = jnp.broadcast_to(owners_low[:, None], (64, 128))
    out, gin, s1, s2, stats = run_step(
        jnp.swapaxes(inputs[0], 0, 1), offs, cotangent[0], conv1_copy,
        jnp.swapaxes(conv2_copy, 1, 2), jnp.swapaxes(project_copy, 0, 1),
        pvec, owners_row, consts,
    )
    flip2 = lambda a: jnp.swapaxes(a, -1, -2)
    states = [
        conv1_master, conv1_first, conv1_second, conv1_average,
        conv2_master, conv2_first, conv2_second, conv2_average,
        project_master, project_first, project_second, project_average,
    ]
    cp1, cp2, cp3, *new = run_tail(
        s1.reshape(5, 4, 4, 48, PAD), s2.reshape(4, 4, 96, C1), (basis1, basis2, basis3),
        [flip2(a) for a in states], owners_row, owners_col, consts,
    )
    nm1, nf1, nq1, na1, nm2, nf2, nq2, na2, nm3, nf3, nq3, na3 = [flip2(a) for a in new]

    def my_half(v, half):
        return lax.dynamic_slice(v, (0, zl * half), (2, half))

    g3 = stats[4].reshape(2, H)
    s_1 = norm_adam(my_half(stats[0:2], HALF0), jnp.stack([norm1_gain, norm1_bias]), norm1_moments)
    s_2 = norm_adam(my_half(stats[2:4], HALF1), jnp.stack([norm2_gain, norm2_bias]), norm2_moments)
    s_3 = norm_adam(my_half(g3, HALFH), jnp.stack([norm3_gain, norm3_bias]), norm3_moments)
    return (
        out[None], jnp.swapaxes(gin, 0, 1)[None], *s_1, *s_2, *s_3,
        nm1, cp1, nf1, nq1, na1,
        nm2, flip2(cp2), nf2, nq2, na2,
        nm3, flip2(cp3), nf3, nq3, na3,
    )


def solution(mesh):
    finer = Mesh(mesh.devices.reshape(4, 4, 2, 2, mesh.shape["ch"]), SEQ_CH)
    owner3 = P(None, None, SEQ_CH)
    owner2 = P(None, SEQ_CH)
    half3 = P(None, None, "ch")
    in_specs = (
        P(SEQ, None, "ch"), P(SEQ), P(), P(SEQ, None, "ch"),
        P("ch"), P("ch"), half3, P("ch"), P("ch"), half3, P("ch"), P("ch"), half3,
        half3, owner3, owner3, owner3, owner3, P(),
        half3, owner3, owner3, owner3, owner3, P(),
        P(None, "ch"), owner2, owner2, owner2, owner2, P(),
    )
    vec = P(None, "ch")
    out_specs = (
        P(SEQ, None, "ch"), P(SEQ, None, "ch"), *[vec] * 9,
        owner3, half3, owner3, owner3, owner3,
        owner3, half3, owner3, owner3, owner3,
        owner2, vec, owner2, owner2, owner2,
    )
    return jax.shard_map(local, mesh=finer, in_specs=in_specs, out_specs=out_specs, check_vma=False)
```

time: 787 us -> 307 us (0.39); the launches traced: 773 us -> 303 us
  Pallas kernels: 0 us -> 269 us
  local copies, waits for them, and re-layouts: 201 us -> 28.4 us
  waiting for transfers between devices: 169 us -> 0 us
  other arithmetic: 122 us -> 3.39 us
  matrix products: 116 us -> 0 us
  starting transfers between devices: 94.8 us -> 0 us
  blocking collectives: 54.3 us -> 0 us
  between operations: 16.6 us -> 2 us
    pallas_call x0 -> x2, Pallas kernels: none -> 269 us  [the longest x1 164 us: run_step(): pl.pallas_call(step_kernel, out_shape=(shape((BINS, 384), bf16), shape((H...]
    all_to_all x15 -> x0, waiting for transfers between devices: 135 us -> none  [the longest x9 78.4 us: sent_to_all(): lax.all_to_all(jnp.broadcast_to(array[None], (count, *array.shape)), axis...]
    dot_general x33 -> x0, matrix products: 116 us -> none  [the longest x8 35.9 us: convolve(): lax.dot_general(padded[:, tap_index:tap_index + length], weight[tap_index...]
    all_to_all x15 -> x0, starting transfers between devices: 94.3 us -> none  [the longest x9 60.3 us: sent_to_all(): lax.all_to_all(jnp.broadcast_to(array[None], (count, *array.shape)), axis...]
    gather x15 -> x0, local copies, waits for them, and re-layouts: 61.9 us -> none  [to_owner(): return jnp.take(blocks, order_list, axis=len(leading)).reshape(matrix.shape)]
    all_to_all x3 -> x0, blocking collectives: 54.3 us -> none  [the longest x2 38.7 us: sent_to_all(): lax.all_to_all(jnp.broadcast_to(array[None], (count, *array.shape)), axis...]
    reduce_sum x16 -> x0, other arithmetic: 53.2 us -> none  [the longest x1 24.5 us: norm_backward(): jnp.sum(slopes * scaled, axis=(0, 1))]
    all_gather x2 -> x0, waiting for transfers between devices: 33.4 us -> none  [the longest x1 33.4 us: local(): lax.all_gather(first_result[0].astype(jnp.bfloat16), SEQ, axis=2, tiled=T...]
  transfers between devices with their start and end apart: 17 -> 0, of which waited for: 13 -> 0; matrix products, arithmetic and copies ran while one was open for 35% -> 0% of each run, Pallas kernels for 0% -> 0%
where the time goes in v1:
time: 307 us; the launch traced here: 303 us
  Pallas kernels  269 us (88%)
  local copies, waits for them, and re-layouts  28.4 us (9%)
  other arithmetic  3.39 us (1%)
    pallas_call x1, Pallas kernels, run_step(): pl.pallas_call(step_kernel, out_shape=(shape((BINS, 384), bf16), shape((H...  164 us
    pallas_call x1, Pallas kernels, run_tail(): pl.pallas_call(tail_kernel, out_shape=(shape((5, C0, 384), bf16), shape((...  105 us
    unnamed x57, local copies, waits for them, and re-layouts  20.5 us

profile of v1, /device:TPU:1, one launch (start us, length us, event | category | flops | bytes accessed | tf_op | source)
XLA Modules:
  0.0 302.7 jit_solution(17408759058821335428)
XLA Ops:
  1.3 0.7 convert_element_type.9
  2.0 0.7 stack.42
  2.7 0.7 stack.43
  3.4 0.7 stack.44
  4.0 0.7 stack.45
  4.7 0.6 broadcast_in_dim.33.owners_row
  5.3 0.7 constant_dynamic-update-slice_fusion.1
  6.0 0.1 dynamic_update_slice.25
  6.1 0.2 dynamic_update_slice.24
  6.3 0.7 constant_dynamic-update-slice_fusion
  7.0 0.6 broadcast_in_dim.31.offs
  7.6 0.8 dynamic_update_slice.28
  8.4 0.8 dynamic-slice_add_fusion
  9.2 0.1 add.81
  9.4 0.6 pad.4.pvec
  10.0 0.7 broadcast_in_dim.36.owners_col
  10.7 163.6 %shard_map.584 = (bf16[1024,384]{1,0:T(8,128)(2,1)}, f32[326,2048]{1,0:T(8,128)}, bf16[5,768,768]{2,1,0:T(8,128)(2,1)}, bf16[16,96,768]{2,1,0:T(8,128)(2,1)}, f32[8,768]{1,0:T(8,128)}) custom-call(bf16[326,2048]{1,0:T(8,128)(2,1)} %bitcast.63, f32[8,128]{1,0:T(8,128)} %broadcast_in_dim.31.offs, bf16[1024,384]{1,0:T(8,128)(2,1)} %bitcast.66, ...), custom_call_target="tpu_custom_call" | custom-call | tf_op jit(solution)/shard_map/pallas_call | solution.py:681
  174.3 0.0 copy-start.14
  174.3 0.0 copy-start.15
  174.3 0.0 copy-start.17
  174.3 0.0 copy-start.18
  174.4 0.0 copy-start.19
  174.4 0.0 copy-start.16
  174.4 6.0 %copy.67 = f32[1,2048,326]{1,0,2:T(1,128)} copy(f32[1,2048,326]{1,2,0:T(8,128)} %bitcast.61) | data formatting | bytes 5341184
  180.4 0.0 copy-done.14
  180.5 0.0 copy-done.15
  180.5 0.6 maximum_subtract_fusion.1
  181.1 0.0 copy-done.17
  181.1 0.0 copy-done.18
  181.1 0.0 copy-done.19
  181.1 0.7 maximum_subtract_fusion.2
  181.8 0.0 copy-done.16
  181.8 0.7 maximum_subtract_fusion
  182.5 105.2 %shard_map.585 = (bf16[5,652,384]{2,1,0:T(8,128)(2,1)}, bf16[3,192,768]{2,1,0:T(8,128)(2,1)}, bf16[192,768]{1,0:T(8,128)(2,1)}, f32[5,6,652]{2,1,0:T(8,128)}, f3...) custom-call(bf16[5,4,4,48,768]{4,3,2,1,0:T(8,128)(2,1)} %bitcast.60,, ...), custom_call_target="tpu_custom_call" | custom-call | tf_op jit(solution)/shard_map/pallas_call | solution.py:938
  287.7 0.0 copy-done.1
  287.7 0.9 copy.92
  288.6 1.6 copy.93
  290.2 0.0 copy-start
  290.2 3.5 %copy.94 = bf16[5,652,384]{2,1,0:T(8,128)(2,1)} copy(bf16[5,652,384]{2,1,0:T(8,128)(2,1)} %get-tuple-element.141) | data formatting | bytes 5007360
  293.7 0.0 copy-done.5
  293.7 0.0 copy-start.13
  293.7 0.0 copy-start.2
  293.7 0.0 copy-start.12
  293.7 0.0 copy-start.11
  293.7 0.0 copy-start.10
  293.8 0.7 copy.95
  294.4 0.0 copy-done.4
  294.4 0.6 copy.96
  295.1 0.0 copy-done.3
  295.1 0.6 copy.97
  295.7 0.0 copy-done.9
  295.7 0.6 copy.98
  296.3 0.0 copy-done
  296.3 0.9 copy.99
  297.2 0.0 copy-done.8
  297.2 0.6 copy.100
  297.9 0.6 copy.101
  298.5 0.6 copy.102
  299.1 0.0 copy-done.13
  299.1 0.6 copy.103
  299.7 0.7 copy.104
  300.4 0.6 copy.105
  301.0 0.6 copy.106
  301.6 0.6 copy.107
  (25 shorter events, 0.1 us)
Async XLA Ops:
  174.3 6.1 %copy-start.14 = (f32[8,768]{1,0:T(8,128)S(1)}, f32[8,768]{1,0:T(8,128)}, u32[]{:S(2)}) copy-start(f32[8,768]{1,0:T(8,128)} %get-tuple-element.48) | copy-start | bytes 73732
  174.3 6.1 %copy-start.15 = (f32[2,2,384]{2,1,0:T(2,128)S(1)}, f32[2,2,384]{2,1,0:T(2,128)}, u32[]{:S(2)}) copy-start(f32[2,2,384]{2,1,0:T(2,128)} %param.50) | copy-start | bytes 18436
  174.3 6.8 %copy-start.17 = (f32[2,2,192]{2,1,0:T(2,128)S(1)}, f32[2,2,192]{2,1,0:T(2,128)}, u32[]{:S(2)}) copy-start(f32[2,2,192]{2,1,0:T(2,128)} %param.53) | copy-start | bytes 9220
  174.3 6.7 %copy-start.18 = (f32[192]{0:T(256)S(1)}, f32[192]{0:T(256)}, u32[]{:S(2)}) copy-start(f32[192]{0:T(256)} %param.52) | copy-start | bytes 2308
  174.4 6.7 %copy-start.19 = (f32[192]{0:T(256)S(1)}, f32[192]{0:T(256)}, u32[]{:S(2)}) copy-start(f32[192]{0:T(256)} %param.51) | copy-start | bytes 2308
  174.4 7.4 %copy-start.16 = (f32[2,2,326]{2,1,0:T(2,128)S(1)}, f32[2,2,326]{2,1,0:T(2,128)}, u32[]{:S(2)}) copy-start(f32[2,2,326]{2,1,0:T(2,128)} %param.47) | copy-start | bytes 15652
  182.5 105.2 %copy-start.1 = (bf16[1024,384]{1,0:T(8,128)(2,1)S(1)}, bf16[1024,384]{1,0:T(8,128)(2,1)}, u32[]{:S(2)}) copy-start(bf16[1024,384]{1,0:T(8,128)(2,1)} %get-tuple-element.46) | copy-start | bytes 2359300
  290.1 3.5 %copy-start.5 = (f32[5,6,652]{2,1,0:T(8,128)S(1)}, f32[5,6,652]{2,1,0:T(8,128)}, u32[]{:S(2)}) copy-start(f32[5,6,652]{2,1,0:T(8,128)} %get-tuple-element.53) | copy-start | bytes 234724
  290.2 4.3 %copy-start.4 = (f32[5,6,652]{2,1,0:T(8,128)S(1)}, f32[5,6,652]{2,1,0:T(8,128)}, u32[]{:S(2)}) copy-start(f32[5,6,652]{2,1,0:T(8,128)} %get-tuple-element.54) | copy-start | bytes 234724
  290.2 4.9 %copy-start.3 = (f32[5,6,652]{2,1,0:T(8,128)S(1)}, f32[5,6,652]{2,1,0:T(8,128)}, u32[]{:S(2)}) copy-start(f32[5,6,652]{2,1,0:T(8,128)} %get-tuple-element.55) | copy-start | bytes 234724
  290.2 5.6 %copy-start.9 = (f32[3,3,768]{2,1,0:T(4,128)S(1)}, f32[3,3,768]{2,1,0:T(4,128)}, u32[]{:S(2)}) copy-start(f32[3,3,768]{2,1,0:T(4,128)} %get-tuple-element.56) | copy-start | bytes 82948
  290.2 6.2 %copy-start = (bf16[3,192,768]{2,1,0:T(8,128)(2,1)S(1)}, bf16[3,192,768]{2,1,0:T(8,128)(2,1)}, u32[]{:S(2)}) copy-start(bf16[3,192,768]{2,1,0:T(8,128)(2,1)} %get-tuple-element.57) | copy-start | bytes 2654212
  293.7 3.6 %copy-start.8 = (f32[3,3,768]{2,1,0:T(4,128)S(1)}, f32[3,3,768]{2,1,0:T(4,128)}, u32[]{:S(2)}) copy-start(f32[3,3,768]{2,1,0:T(4,128)} %get-tuple-element.58) | copy-start | bytes 82948
  293.7 4.2 %copy-start.7 = (f32[3,3,768]{2,1,0:T(4,128)S(1)}, f32[3,3,768]{2,1,0:T(4,128)}, u32[]{:S(2)}) copy-start(f32[3,3,768]{2,1,0:T(4,128)} %get-tuple-element.59) | copy-start | bytes 82948
  293.7 4.8 %copy-start.6 = (f32[3,3,768]{2,1,0:T(4,128)S(1)}, f32[3,3,768]{2,1,0:T(4,128)}, u32[]{:S(2)}) copy-start(f32[3,3,768]{2,1,0:T(4,128)} %get-tuple-element.60) | copy-start | bytes 82948
  293.7 5.4 %copy-start.13 = (f32[3,768]{1,0:T(4,128)S(1)}, f32[3,768]{1,0:T(4,128)}, u32[]{:S(2)}) copy-start(f32[3,768]{1,0:T(4,128)} %get-tuple-element.61) | copy-start | bytes 27652
  293.7 6.0 %copy-start.2 = (bf16[192,768]{1,0:T(8,128)(2,1)S(1)}, bf16[192,768]{1,0:T(8,128)(2,1)}, u32[]{:S(2)}) copy-start(bf16[192,768]{1,0:T(8,128)(2,1)} %get-tuple-element.62) | copy-start | bytes 884740
  293.7 6.7 %copy-start.12 = (f32[3,768]{1,0:T(4,128)S(1)}, f32[3,768]{1,0:T(4,128)}, u32[]{:S(2)}) copy-start(f32[3,768]{1,0:T(4,128)} %get-tuple-element.63) | copy-start | bytes 27652
  293.7 7.3 %copy-start.11 = (f32[3,768]{1,0:T(4,128)S(1)}, f32[3,768]{1,0:T(4,128)}, u32[]{:S(2)}) copy-start(f32[3,768]{1,0:T(4,128)} %get-tuple-element.64) | copy-start | bytes 27652
  293.7 7.9 %copy-start.10 = (f32[3,768]{1,0:T(4,128)S(1)}, f32[3,768]{1,0:T(4,128)}, u32[]{:S(2)}) copy-start(f32[3,768]{1,0:T(4,128)} %get-tuple-element.65) | copy-start | bytes 27652

commit v2 on v1

--- a/solution.py
+++ b/solution.py
@@ -142,14 +142,18 @@
 
 
 def step_kernel(
-    xt, offs, cot, w1, w2, wp, pvec, owners_row, e1, bw1, e2, bw2,
-    out, gin, s1, s2, stats,
-    xw, raw, aa, ww1, ww2, wwp, pooled, diff, cc, mm, hid, og, no, hh, mid, gg, gp, perm,
-    slope, sl_send, sl_home, ob, small, offw, acc, tr,
+    xt, offsets, owners, cot, w1, w2, wp, pg1, pb1, pg2, pb2, pg3, pb3,
+    e1, bw1, e2, bw2, rep1, rep2,
+    out, sl_home, grad, stats,
+    s1, s2, xw, raw, aa, ww1, ww2, wwp, pooled, diff, cc, hid, og, no, hh, mid, gg, gp, perm,
+    slope, small, offs, offw, acc, tr,
+    t1, t2, ra, rb, rd, re, ua, uc, va, pz, rz,
     a1a, a1b, ab1, ab2,
-    ss, rs, ls, as1, ar1, as2, ar2,
+    ss, rs, ls, as1, ar1, as2, ar2, gs, gr,
 ):
+    mm = gg.at[0:3]
     p = Place()
+    offs[...] = jnp.broadcast_to(offsets[...].astype(f32), (8, 128))
     c, zl = p.c, p.zl
     flip = p.at(z=3 - p.z)
     direct = p.at(z=p.z + 1 - 2 * zl)
@@ -199,6 +203,8 @@
     x_b.start()
     o_a.start()
 
+    mine = pl.ds(pl.multiple_of(384 * c, 128), 384)
+    others = pl.ds(pl.multiple_of(384 - 384 * c, 128), 384)
     my_lanes = pl.ds(pl.multiple_of(384 * zl, 128), 384)
     its_lanes = pl.ds(pl.multiple_of(384 - 384 * zl, 128), 384)
     my_rows = pl.ds(pl.multiple_of(192 * zl, 16), 192)
@@ -258,18 +264,33 @@
     small[...] = jnp.zeros_like(small)
     small[0:1, 0:HALF0] = total_s[0:1]
     small[1:2, 0:HALF0] = total_q[0:1]
+    small[2:3, 0:HALF0] = pg1[...].reshape(1, HALF0)
+    small[3:4, 0:HALF0] = pb1[...].reshape(1, HALF0)
+    small[4:5, 0:HALF1] = pg2[...].reshape(1, HALF1)
+    small[5:6, 0:HALF1] = pb2[...].reshape(1, HALF1)
+    small[6:7, 0:HALFH] = pg3[...].reshape(1, HALFH)
+    small[6:7, H : H + HALFH] = pb3[...].reshape(1, HALFH)
     here = small[...]
-    here = jnp.where(zl == 0, here, pltpu.roll(here, HALF0, 1))
+    half_row = iota((8, PAD), 0)
+    moved = jnp.where(
+        half_row < 4,
+        pltpu.roll(here, HALF0, 1),
+        jnp.where(half_row < 6, pltpu.roll(here, HALF1, 1), pltpu.roll(here, HALFH, 1)),
+    )
+    here = jnp.where(zl == 0, here, moved)
+    leader = (p.g == 0) & (p.zh == 0) & (c == 0)
+    here = jnp.where((half_row < 2) | leader, here, 0.0)
     count = jnp.maximum(BINS - off_home, 0.0)
     lane8 = iota((8, PAD), 1)
     row8 = iota((8, PAD), 0)
     here = here + jnp.where((lane8 == PAD - 1) & (row8 == 0), count, 0.0)
-    t1 = Total(p, (a1a, a1b), (as1.at[0], ar1.at[0], as2.at[0], ar2.at[0]))
-    t1.start(here + pvec[...])
-    t1.middle()
-
-    nat1 = dot(owners_row[...], e1[...])[0:1] * 6.0 + bw1[0:1]
-    nat2 = dot(owners_row[...], e2[...])[0:1] * 3.0 + bw2[0:1]
+    all1 = Total(p, (a1a, a1b), (as1.at[0], ar1.at[0], as2.at[0], ar2.at[0]))
+    all1.start(here)
+    all1.middle()
+
+    owners_row = jnp.broadcast_to(owners[...].astype(f32), (8, 64)).astype(bf16)
+    nat1 = dot(owners_row, e1[...])[0:1] * 6.0 + bw1[0:1]
+    nat2 = dot(owners_row, e2[...])[0:1] * 3.0 + bw2[0:1]
     for k in range(6):
         perm[pl.ds(128 * k, 128), :] = (
             (iota((128, PAD), 0) + 128 * k).astype(f32) == nat1
@@ -289,7 +310,7 @@
         raw[0, pl.ds(64 * k, 64), :] = both[0:64]
         raw[1, pl.ds(64 * k, 64), :] = both[64:128]
 
-    first = t1.end()
+    first = all1.end()
     n1 = first[0:1, PAD - 1 : PAD]
     n2 = 0.5 * n1
     inv_n1 = 1.0 / n1
@@ -379,9 +400,9 @@
         acc[0:1] += jnp.sum(vm, axis=0, keepdims=True)
         acc[1:2] += jnp.sum(vm * v, axis=0, keepdims=True)
 
-    t2 = Total(p, (ab1.at[0], ab2.at[0]), (as1.at[1], ar1.at[1], as2.at[1], ar2.at[1]))
-    t2.start(acc[0:2])
-    t2.middle()
+    all2 = Total(p, (ab1.at[0], ab2.at[0]), (as1.at[1], ar1.at[1], as2.at[1], ar2.at[1]))
+    all2.start(acc[0:2])
+    all2.middle()
     own_w[1].wait()
     own_w[2].wait()
     for u in range(4):
@@ -410,7 +431,7 @@
     x_b.wait_send()
     c_b.wait_send()
 
-    second = t2.end()
+    second = all2.end()
     mean2 = second[0:1] * inv_n2
     var2 = second[1:2] * inv_n2 - mean2 * mean2
     rs2 = lax.rsqrt(var2 + eps_norm)
@@ -435,10 +456,10 @@
     h2m = h2 * m
     acc[6:7, 0:H] = jnp.sum(h2m, axis=0, keepdims=True)
     acc[6:7, H : 2 * H] = jnp.sum(h2m * h2, axis=0, keepdims=True)
-    t3 = Total(p, (ab1.at[1], ab2.at[1]), (as1.at[2], ar1.at[2], as2.at[2], ar2.at[2]))
-    t3.start(acc[6:8])
-    t3.middle()
-    third = t3.end()
+    all3 = Total(p, (ab1.at[1], ab2.at[1]), (as1.at[2], ar1.at[2], as2.at[2], ar2.at[2]))
+    all3.start(acc[6:8])
+    all3.middle()
+    third = all3.end()
     mean3 = third[0:1, 0:H] * inv_n2
     var3 = third[0:1, H : 2 * H] * inv_n2 - mean3 * mean3
     rs3 = lax.rsqrt(var3 + eps_norm)
@@ -453,42 +474,42 @@
     hid[...] = scaled
     acc[6:7, 0:H] = jnp.sum(slopes * scaled * own, axis=0, keepdims=True)
     acc[6:7, H : 2 * H] = jnp.sum(slopes * own, axis=0, keepdims=True)
-    t4 = Total(p, (ab1.at[2], ab2.at[2]), (as1.at[3], ar1.at[3], as2.at[3], ar2.at[3]))
-    t4.start(acc[6:8])
-    ob[...] = (pooled[...] + dot(no[...], wwp[...])).astype(bf16)
-    t4.middle()
+    all4 = Total(p, (ab1.at[2], ab2.at[2]), (as1.at[3], ar1.at[3], as2.at[3], ar2.at[3]))
+    all4.start(acc[6:8])
     out_rows = pl.ds(pl.multiple_of(512 * c, 16), OWN)
     own_rows = pl.ds(own0, OWN)
+    gp[0] = (pooled[own_rows, :] + dot(no[own_rows, :], wwp[...])).astype(bf16)
+    all4.middle()
 
     def out_copy(k):
         return remote(
-            ob.at[own_rows, pl.ds(384 * k, 384)],
+            gp.at[0, :, pl.ds(384 * k, 384)],
             out.at[out_rows, :],
             ss.at[23 + k],
             rs.at[23 + c],
             p.at(z=2 * p.zh + k, c=zl),
         )
 
+    def out_local(k):
+        return pltpu.make_async_copy(
+            gp.at[0, :, pl.ds(384 * k, 384)], out.at[out_rows, :], ls.at[3]
+        )
+
     def to_self(k):
         return (zl == k) & is_self
 
     for k in range(2):
         pl.when(jnp.logical_not(to_self(k)))(lambda k=k: out_copy(k).start())
 
-        def local(k=k):
-            pltpu.make_async_copy(
-                ob.at[own_rows, pl.ds(384 * k, 384)], out.at[out_rows, :], rs.at[23 + c]
-            ).start()
-
-        pl.when(to_self(k))(local)
+        pl.when(to_self(k))(lambda k=k: out_local(k).start())
 
     def put2(m, value):
-        s2[:, pl.ds(24 * m, 24), :] = value.astype(bf16).reshape(16, 24, C1)
+        s2[:, :, pl.ds(24 * m, 24), :] = value.astype(bf16).reshape(4, 4, 24, C1)
 
     tn = ((0,), (0,))
     nop = dot(no[own_rows, :], perm2).astype(bf16)
     put2(3, dot(nop, cc[own_rows, :], tn))
-    fourth = t4.end()
+    fourth = all4.end()
     stats[4:5] = fourth[0:1]
     gain_mean = fourth[0:1, 0:H] * inv_n2
     bias_mean = fourth[0:1, H : 2 * H] * inv_n2
@@ -513,14 +534,16 @@
         acc[0:1, lanes] = jnp.sum(mine * scaled, axis=0, keepdims=True)
         acc[1:2, lanes] = jnp.sum(mine, axis=0, keepdims=True)
 
-    t5 = Total(p, (ab1.at[3], ab2.at[3]), (as1.at[4], ar1.at[4], as2.at[4], ar2.at[4]))
-    t5.start(acc[0:2])
+    all5 = Total(p, (ab1.at[3], ab2.at[3]), (as1.at[4], ar1.at[4], as2.at[4], ar2.at[4]))
+    all5.start(acc[0:2])
     hp = dot(hh[1, own_rows, :], perm2).astype(bf16)
     put2(0, dot(hp, mm[0, own_rows, :], tn))
-    t5.middle()
+    all5.middle()
     for t in range(1, 3):
         put2(t, dot(hp, mm[t, own_rows, :], tn))
-    fifth = t5.end()
+    s2_over = remote(s2.at[:, :, :, others], t2, gs.at[0], gr.at[0], other_core)
+    s2_over.start()
+    fifth = all5.end()
     stats[2:4] = fifth
     acc[0:2] = fifth * inv_n2
 
@@ -541,12 +564,103 @@
         gg[4, :, lanes] = before(go)
         gg[5, :, lanes] = before(ge)
 
+    def total(own, parts):
+        v = own.astype(f32)
+        for part in parts:
+            v = v + part.astype(f32)
+        return v.astype(bf16)
+
+    def along(k, axis):
+        if axis == "x":
+            i = lax.rem(p.x + k + 1, 4)
+            return p.at(x=i), i
+        i = lax.rem(p.y + k + 1, 4)
+        return p.at(y=i), i
+
+    s2_over.wait()
+    t2[...] = total(t2[...], [s2[:, :, :, mine]])
+    flying = []
+
+    def send(src, dst, sem, device):
+        cp = remote(src, dst, gs.at[sem], gr.at[sem], device)
+        cp.start()
+        flying.append(cp)
+
+    def arrived(dst, sem):
+        remote(dst, dst, gs.at[0], gr.at[sem], other_core).wait_recv()
+
+    for k in range(3):
+        device, i = along(k, "y")
+        send(t2.at[:, i], rd.at[k], 1 + k, device)
+
+    for k in range(2):
+
+        def out_sent(k=k):
+            out_copy(k).wait_send()
+
+        pl.when(jnp.logical_not(to_self(k)))(out_sent)
+        pl.when(to_self(k))(lambda k=k: out_local(k).wait())
     gp[0] = dot(gg[3, own_rows, :], perm[...]).astype(bf16)
     gp[1] = dot(gg[2, own_rows, :], perm[...]).astype(bf16)
+
+    TAP_AXIS = ("x", "y", "x", "y", "x")
+
+    def to_core(t):
+        return remote(s1.at[t, :, :, :, others], t1.at[t], gs.at[7 + t], gr.at[7 + t], other_core)
+
+    def to_axis(t):
+        to_core(t).wait_recv()
+        t1[t] = total(t1[t], [s1[t, :, :, :, mine]])
+        for k in range(3):
+            device, i = along(k, TAP_AXIS[t])
+            src = t1.at[t, i] if TAP_AXIS[t] == "x" else t1.at[t, :, i]
+            send(src, ra.at[t, k], 12 + 3 * t + k, device)
+
+    def to_other_axis(t):
+        for k in range(3):
+            arrived(ra.at[t, k], 12 + 3 * t + k)
+        own_part = t1[t, p.x] if TAP_AXIS[t] == "x" else t1[t, :, p.y]
+        ua[t] = total(own_part, [ra[t, k] for k in range(3)])
+        for k in range(3):
+            device, i = along(k, "y" if TAP_AXIS[t] == "x" else "x")
+            send(ua.at[t, i], rb.at[t, k], 27 + 3 * t + k, device)
+
+    def last_of(t):
+        for k in range(3):
+            arrived(rb.at[t, k], 27 + 3 * t + k)
+        own_part = ua[t, p.y] if TAP_AXIS[t] == "x" else ua[t, p.x]
+        va[t] = total(own_part, [rb[t, k] for k in range(3)])
+
     for t in range(5):
         part = dot(gp[0], aa[t, own_rows, 0:C0], tn) + dot(gp[1], aa[t + 1, own_rows, 0:C0], tn)
-        s1[t, :, 0:C0] = part.astype(bf16)
-        s1[t, :, C0:PAD] = jnp.zeros((C1, PAD - C0), bf16)
+        part = part.astype(bf16).reshape(4, 4, 48, C0)
+        s1[t, :, :, :, 0:C0] = part
+        s1[t, :, :, :, C0:PAD] = jnp.zeros((4, 4, 48, PAD - C0), bf16)
+        to_core(t).start()
+        if t > 0:
+            to_axis(t - 1)
+    to_axis(4)
+    for k in range(3):
+        arrived(rd.at[k], 1 + k)
+    uc[...] = total(t2[:, p.y], [rd[k] for k in range(3)])
+    for k in range(3):
+        device, i = along(k, "x")
+        send(uc.at[i], re.at[k], 4 + k, device)
+
+    def slope_part(half, par, k):
+        return (
+            gp.at[par, pl.ds(256 * k, 256), pl.ds(384 * half, 384)],
+            sl_home.at[c, par, pl.ds(256 * k, 256), :],
+        )
+
+    def slope_copy(half, par, k):
+        src, dst = slope_part(half, par, k)
+        n = 2 * par + k
+        return remote(src, dst, ss.at[25 + 4 * half + n], rs.at[25 + 4 * c + n], p.at(z=2 * p.zh + half, c=zl))
+
+    def slope_local(half, par, k):
+        src, dst = slope_part(half, par, k)
+        return pltpu.make_async_copy(src, dst, rs.at[25 + 4 * c + 2 * par + k])
 
     small[4:6] = jnp.zeros((2, PAD), f32)
     for par in range(2):
@@ -570,76 +684,98 @@
                 small[5:6, lanes] += jnp.sum(slopes, axis=0, keepdims=True)
 
             dst = pl.ds(256 * k, 256)
-            sl_send[0, par, dst, :] = slope[:, 0:384].astype(bf16)
-            sl_send[1, par, dst, :] = pltpu.roll(slope[...], PAD - HALF0, 1)[:, 0:384].astype(bf16)
-
-    t6 = Total(p, (ab1.at[4], ab2.at[4]), (as1.at[5], ar1.at[5], as2.at[5], ar2.at[5]))
-    t6.start(small[4:6])
-
-    def slope_copy(k):
-        return remote(
-            sl_send.at[k], sl_home.at[c], ss.at[25 + k], rs.at[25 + c], p.at(z=2 * p.zh + k, c=zl)
-        )
-
-    for k in range(2):
-        pl.when(jnp.logical_not(to_self(k)))(lambda k=k: slope_copy(k).start())
-
-        def local_s(k=k):
-            pltpu.make_async_copy(sl_send.at[k], sl_home.at[c], rs.at[25 + c]).start()
-
-        pl.when(to_self(k))(local_s)
-    t6.middle()
-    sixth = t6.end()
+            gp[par, dst, 0:384] = slope[:, 0:384].astype(bf16)
+            gp[par, dst, 384:768] = pltpu.roll(slope[...], PAD - HALF0, 1)[:, 0:384].astype(bf16)
+            for half in range(2):
+
+                def send_slope(half=half, par=par, k=k):
+                    slope_copy(half, par, k).start()
+
+                def keep_slope(half=half, par=par, k=k):
+                    slope_local(half, par, k).start()
+
+                pl.when(jnp.logical_not(to_self(half)))(send_slope)
+                pl.when(to_self(half))(keep_slope)
+            if (par, k) == (1, 0):
+                to_other_axis(0)
+                to_other_axis(1)
+
+    all6 = Total(p, (ab1.at[4], ab2.at[4]), (as1.at[5], ar1.at[5], as2.at[5], ar2.at[5]))
+    all6.start(small[4:6])
+
+    to_other_axis(2)
+    all6.middle()
+    to_other_axis(3)
+    for t in range(2):
+        last_of(t)
+    sixth = all6.end()
     stats[0:2] = sixth
-    stats[5:8] = jnp.zeros((3, PAD), f32)
-
-    small[4:6] = sixth * inv_n1
-    small[6:7] = rs1 * gain1
-    vec = small[...]
-    vec = jnp.where(zl == 0, vec, pltpu.roll(vec, PAD - HALF0, 1))
-    tr[0, 0:8, :] = vec
-    cols = jnp.transpose(tr[0, :, 0:384])
-    mean_c = cols[0:HALF0, 2:3]
-    rs_c = cols[0:HALF0, 3:4]
-    gm_c = cols[0:HALF0, 4:5]
-    bm_c = cols[0:HALF0, 5:6]
-    scale_c = cols[0:HALF0, 6:7]
+    stats[5:6] = mean1
+    stats[6:7] = rs1
+    stats[7:8] = rs1 * gain1
+    stats[8:10] = sixth * inv_n1
+    stats[10:16] = jnp.zeros((6, PAD), f32)
+    to_other_axis(4)
+    for k in range(3):
+        arrived(re.at[k], 4 + k)
+    vc = total(uc[p.x], [re[k] for k in range(3)])
+    for t in range(2, 5):
+        last_of(t)
+    g1 = dot(rep1[...], va[...].reshape(240, 384))
+    g2 = dot(rep2[...], vc)
+    for e in range(8):
+        pz[e, 0:48] = g1[48 * e : 48 * e + 48].astype(bf16)
+        pz[e, 48:80] = g2[32 * e : 32 * e + 32].astype(bf16)
+    for k, (device, zi, ci) in enumerate(column_peers(p)):
+        cp = remote(pz.at[2 * zi + ci], rz.at[p.e], gs.at[42 + k], gr.at[42 + p.e], device)
+        cp.start()
+        flying.append(cp)
+    rz[p.e] = pz[p.e]
+    for device, zi, ci in column_peers(p):
+        e = 2 * zi + ci
+        arrived(rz.at[e], 42 + e)
+    for half in range(2):
+        v = rz[half].astype(f32)
+        for k in range(1, 4):
+            v = v + rz[2 * k + half].astype(f32)
+        grad[:, 384 * half : 384 * half + 384] = v
+
+    for t in range(5):
+        to_core(t).wait_send()
+    for cp in flying:
+        cp.wait_send()
+    for half in range(2):
+        for par in range(2):
+            for k in range(2):
+
+                def slope_sent(half=half, par=par, k=k):
+                    slope_copy(half, par, k).wait_send()
+
+                pl.when(jnp.logical_not(to_self(half)))(slope_sent)
     for j in range(2):
-        remote(sl_home.at[j], sl_home.at[j], ss.at[0], rs.at[25 + j], other_core).wait_recv()
-    rowq = iota((128, 256), 0)
-    laneq = iota((128, 256), 1)
-    put_even = (laneq == 2 * rowq).astype(bf16)
-    put_odd = (laneq == 2 * rowq + 1).astype(bf16)
+
+        def out_here(j=j):
+            rows = out.at[pl.ds(512 * j, 512), :]
+            remote(rows, rows, ss.at[0], rs.at[23 + j], other_core).wait_recv()
+
+        pl.when(jnp.logical_not(is_self & (c == j)))(out_here)
     for j in range(2):
-        for k in range(4):
-            bins = pl.ds(128 * k, 128)
-            st = dot(sl_home[j, 0, bins, :], put_even, tn) + dot(sl_home[j, 1, bins, :], put_odd, tn)
-            lanes = pl.ds(1024 * j + 256 * k, 256)
-            xf = xt[:, lanes].astype(f32)
-            scaled = (xf - mean_c) * rs_c
-            ok = ((iota((1, 256), 1) + (1024 * j + 256 * k)).astype(f32) >= 2.0 * off_home).astype(f32)
-            gin[:, lanes] = ok * (scale_c * (st[0:HALF0] - bm_c - scaled * gm_c))
-
-    for k in range(2):
-
-        def sent(k=k):
-            out_copy(k).wait_send()
-            slope_copy(k).wait_send()
-
-        pl.when(jnp.logical_not(to_self(k)))(sent)
-    for j in range(2):
-        rows = out.at[pl.ds(512 * j, 512), :]
-        remote(rows, rows, ss.at[0], rs.at[23 + j], other_core).wait_recv()
+        for par in range(2):
+            for k in range(2):
+                part = sl_home.at[j, par, pl.ds(256 * k, 256), :]
+                remote(part, part, ss.at[0], rs.at[25 + 4 * j + 2 * par + k], other_core).wait_recv()
 
 
 VMEM = pl.BlockSpec(memory_space=pltpu.VMEM)
 ANY = pl.BlockSpec(memory_space=pl.ANY)
 
 
-def run_step(xt, offs, cot, w1, w2, wp, pvec, owners_row, consts):
+def run_step(xt, offsets, owners, cot, w1, w2, wp, params, consts):
     shape = jax.ShapeDtypeStruct
     dma = pltpu.SemaphoreType.DMA
     scratch = [
+        pltpu.VMEM((5, 4, 4, 48, PAD), bf16),
+        pltpu.VMEM((4, 4, 96, C1), bf16),
         pltpu.VMEM((2, HALF0, LANES), bf16),
         pltpu.VMEM((2, 576, PAD), bf16),
         pltpu.VMEM((6, WIN, PAD), bf16),
@@ -649,7 +785,6 @@
         pltpu.VMEM((WIN, C1), f32),
         pltpu.VMEM((WIN, C1), f32),
         pltpu.VMEM((WIN, C1), bf16),
-        pltpu.VMEM((3, WIN, C1), bf16),
         pltpu.VMEM((WIN, H), f32),
         pltpu.VMEM((WIN, H), f32),
         pltpu.VMEM((WIN, H), bf16),
@@ -659,41 +794,54 @@
         pltpu.VMEM((2, OWN, C1), bf16),
         pltpu.VMEM((C1, C1), bf16),
         pltpu.VMEM((256, PAD), f32),
-        pltpu.VMEM((2, 2, OWN, 384), bf16),
-        pltpu.VMEM((2, 2, OWN, 384), bf16),
-        pltpu.VMEM((WIN, C1), bf16),
         pltpu.VMEM((8, PAD), f32),
+        pltpu.VMEM((8, 128), f32),
         pltpu.VMEM((8, 128), f32),
         pltpu.VMEM((8, PAD), f32),
         pltpu.VMEM((2, 128, PAD), f32),
+        pltpu.VMEM((5, 4, 4, 48, 384), bf16),
+        pltpu.VMEM((4, 4, 96, 384), bf16),
+        pltpu.VMEM((5, 3, 4, 48, 384), bf16),
+        pltpu.VMEM((5, 3, 48, 384), bf16),
+        pltpu.VMEM((3, 4, 96, 384), bf16),
+        pltpu.VMEM((3, 96, 384), bf16),
+        pltpu.VMEM((5, 4, 48, 384), bf16),
+        pltpu.VMEM((4, 96, 384), bf16),
+        pltpu.VMEM((5, 48, 384), bf16),
+        pltpu.VMEM((8, 80, 384), bf16),
+        pltpu.VMEM((8, 80, 384), bf16),
         pltpu.VMEM((8, 8, PAD), f32),
         pltpu.VMEM((16, 8, PAD), f32),
         pltpu.VMEM((5, 8, 2, PAD), f32),
         pltpu.VMEM((5, 16, 2, PAD), f32),
-        dma((32,)),
-        dma((32,)),
+        dma((40,)),
+        dma((40,)),
         dma((4,)),
         dma((6, 8)),
         dma((6, 8)),
         dma((6, 16)),
         dma((6, 16)),
+        dma((52,)),
+        dma((52,)),
     ]
     return pl.pallas_call(
         step_kernel,
         out_shape=(
             shape((BINS, 384), bf16),
-            shape((HALF0, 2 * BINS), f32),
-            shape((5, C1, PAD), bf16),
-            shape((16, 96, C1), bf16),
-            shape((8, PAD), f32),
+            shape((2, 2, OWN, 384), bf16),
+            shape((80, PAD), f32),
+            shape((16, PAD), f32),
         ),
-        in_specs=[VMEM, VMEM, ANY, ANY, ANY, ANY] + [VMEM] * 6,
-        out_specs=(ANY, VMEM, VMEM, VMEM, VMEM),
+        in_specs=[VMEM, VMEM, VMEM, ANY, ANY, ANY, ANY] + [VMEM] * 12,
+        out_specs=(ANY, ANY, VMEM, VMEM),
         scratch_shapes=scratch,
         compiler_params=pltpu.CompilerParams(
             collective_id=0, has_side_effects=True, vmem_limit_bytes=63 * 2**20
         ),
-    )(xt, offs, cot, w1, w2, wp, pvec, owners_row, consts["e1"], consts["bw1"], consts["e2"], consts["bw2"])
+    )(
+        xt, offsets, owners, cot, w1, w2, wp, *params,
+        *[consts[n] for n in ("e1", "bw1", "e2", "bw2", "rep1", "rep2")],
+    )
 
 
 def adam_block(first, second, turned):
@@ -712,246 +860,276 @@
     return master_new, average_rate * average + (1.0 - average_rate) * master_new
 
 
-def tail_kernel(
-    s1, s2, b1, b2, b3,
-    m1, f1, q1, a1, m2, f2, q2, a2, m3, f3, q3, a3,
-    owners_row, owners_col, rep1, rep2, ec1, bwc1, e3, bw3,
-    cp1, cp2, cp3,
-    nm1, nf1, nq1, na1, nm2, nf2, nq2, na2, nm3, nf3, nq3, na3,
-    t1, t2, ra1, ua, ra2, rb1, rb2, ub1, ub2, rb3, rb4, pz, rz, dd, upd, nb, ga,
+def owner_kernel(
+    grad, b1, b2, b3,
+    m1, f1, q1, a1, m2, f2, q2, a2, m3, f3, q3, a3, pack_a, pack_b,
+    ga, gb, nm1, nf1, nq1, na1, nm2, nf2, nq2, na2, nm3, nf3, nq3, na3,
+    dd, nb, near, fa, fb, pa, pb,
     ss, rs, ls,
 ):
     p = Place()
     x, y, zh, zl, z, c = p.x, p.y, p.zh, p.zl, p.z, p.c
     other_core = p.at(c=1 - c)
+    over = p.at(z=lax.rem(z + 2, 4))
     xs = [(p.at(x=lax.rem(x + k, 4)), lax.rem(x + k, 4)) for k in (1, 2, 3)]
     ys = [(p.at(y=lax.rem(y + k, 4)), lax.rem(y + k, 4)) for k in (1, 2, 3)]
-    column = column_peers(p)
     bar = pltpu.get_barrier_semaphore()
-    for device, *_ in xs + ys + column:
+    for device in [d for d, _ in xs + ys] + [other_core, over]:
         pl.semaphore_signal(bar, inc=1, device_id=device, device_id_type=MESH)
-    pl.semaphore_wait(bar, 13)
-
-    mine = pl.ds(pl.multiple_of(384 * c, 128), 384)
-    others = pl.ds(pl.multiple_of(384 - 384 * c, 128), 384)
-    ca = remote(s1.at[:, :, :, :, others], t1, ss.at[0], rs.at[0], other_core)
-    cb = remote(s2.at[:, :, :, others], t2, ss.at[1], rs.at[1], other_core)
-    ca.start()
-    cb.start()
-    ca.wait()
-    cb.wait()
-    for t in range(5):
-        t1[t] = (t1[t].astype(f32) + s1[t, :, :, :, mine].astype(f32)).astype(bf16)
-    t2[...] = (t2[...].astype(f32) + s2[:, :, :, mine].astype(f32)).astype(bf16)
-
-    sent = []
-    for k in range(3):
-        xd, xi = xs[k]
-        yd, yi = ys[k]
-        sent.append(remote(t1.at[0:4, xi], ra1.at[k], ss.at[2 + k], rs.at[2 + k], xd))
-        sent.append(remote(t1.at[4, :, yi], rb1.at[k], ss.at[5 + k], rs.at[5 + k], yd))
-        sent.append(remote(t2.at[:, yi], rb2.at[k], ss.at[8 + k], rs.at[8 + k], yd))
-    for cp in sent:
-        cp.start()
-    for cp in sent:
-        cp.wait_recv()
-
-    def total(own, parts):
-        v = own.astype(f32)
-        for k in range(3):
-            v = v + parts[k].astype(f32)
-        return v
-
-    for t in range(4):
-        ua[t] = total(t1[t, x], [ra1[k, t] for k in range(3)]).astype(bf16)
-    ub1[...] = total(t1[4, :, y], [rb1[k] for k in range(3)]).astype(bf16)
-    ub2[...] = total(t2[:, y], [rb2[k] for k in range(3)]).astype(bf16)
-    late = []
-    for k in range(3):
-        xd, xi = xs[k]
-        yd, yi = ys[k]
-        late.append(remote(ua.at[:, yi], ra2.at[k], ss.at[11 + k], rs.at[11 + k], yd))
-        late.append(remote(ub1.at[xi], rb3.at[k], ss.at[14 + k], rs.at[14 + k], xd))
-        late.append(remote(ub2.at[xi], rb4.at[k], ss.at[17 + k], rs.at[17 + k], xd))
-    for cp in late:
-        cp.start()
-    for cp in late:
-        cp.wait_recv()
-    va = total(ua[:, y], [ra2[k] for k in range(3)]).astype(bf16).reshape(192, 384)
-    vb = total(ub1[x], [rb3[k] for k in range(3)]).astype(bf16)
-    vc = total(ub2[x], [rb4[k] for k in range(3)]).astype(bf16)
-    r1 = rep1[...]
-    g1 = dot(r1[:, 0:192], va) + dot(r1[:, 192:240], vb)
-    g2 = dot(rep2[...], vc)
-    for e in range(8):
-        pz[e, 0:48] = g1[48 * e : 48 * e + 48].astype(bf16)
-        pz[e, 48:80] = g2[32 * e : 32 * e + 32].astype(bf16)
-    near = []
-    for k, (device, zi, ci) in enumerate(column):
-        near.append(remote(pz.at[2 * zi + ci], rz.at[p.e], ss.at[20 + k], rs.at[20 + p.e], device))
-    for cp in near:
-        cp.start()
-    rz[p.e] = pz[p.e]
-    for device, zi, ci in column:
-        e = 2 * zi + ci
-        remote(rz.at[e], rz.at[e], ss.at[0], rs.at[20 + e], device).wait_recv()
-    halves = []
-    for half in range(2):
-        v = rz[half].astype(f32)
-        for k in range(1, 4):
-            v = v + rz[2 * k + half].astype(f32)
-        halves.append(v)
-    grad = jnp.concatenate(halves, axis=1)
 
     nt = ((1,), (1,))
+    nb[...] = jnp.zeros_like(nb)
+    dd[...] = jnp.zeros_like(dd)
     basis1 = b1[...].astype(bf16)
     turned = dot(grad[0:40, 0:C0].astype(bf16), basis1)
-    dd[...] = jnp.zeros_like(dd)
     for t in range(5):
         first_new, second_new, direction = adam_block(f1[t], q1[t], turned[8 * t : 8 * t + 6])
         nf1[t] = first_new
         nq1[t] = second_new
         dd[8 * t : 8 * t + 6, 0:C0] = direction
     update = dot(dd[0:40, 0:C0].astype(bf16), basis1, nt)
-    nb[...] = jnp.zeros_like(nb)
+    row_of = (0, 8, 16, 32, 40)
     for t in range(5):
         master_new, average_new = master_block(m1[t], update[8 * t : 8 * t + 6], 0.02, a1[t])
         nm1[t] = master_new
         na1[t] = average_new
-        nb[8 * t : 8 * t + 6, 0:C0] = master_new
+        nb[row_of[t] : row_of[t] + 6, 0:C0] = master_new
     basis2 = b2[...].astype(bf16)
     turned = dot(grad[48:72].astype(bf16), basis2)
     for t in range(3):
         first_new, second_new, direction = adam_block(f2[t], q2[t], turned[8 * t : 8 * t + 3])
         nf2[t] = first_new
         nq2[t] = second_new
-        dd[8 * t : 8 * t + 3, :] = direction
-    update = dot(dd[0:24].astype(bf16), basis2, nt)
+        dd[40 + 8 * t : 43 + 8 * t, :] = direction
+    update = dot(dd[40:64].astype(bf16), basis2, nt)
     for t in range(3):
         master_new, average_new = master_block(m2[t], update[8 * t : 8 * t + 3], 0.02, a2[t])
         nm2[t] = master_new
         na2[t] = average_new
-        nb[40 + 4 * t : 43 + 4 * t, :] = master_new
+        nb[48 + 4 * t : 51 + 4 * t, :] = master_new
     basis3 = b3[...].astype(bf16)
     turned = dot(grad[72:80].astype(bf16), basis3)
     first_new, second_new, direction = adam_block(f3[...], q3[...], turned[0:3])
     nf3[...] = first_new
     nq3[...] = second_new
-    dd[0:8] = jnp.zeros((8, PAD), f32)
-    dd[0:3] = direction
-    update = dot(dd[0:8].astype(bf16), basis3, nt)
+    dd[64:67] = direction
+    update = dot(dd[64:72].astype(bf16), basis3, nt)
     master_new, average_new = master_block(m3[...], update[0:3], 0.05, a3[...])
     nm3[...] = master_new
     na3[...] = average_new
-    nb[52:55, :] = master_new
-
-    ga[c, x, y, zh] = nb[...].astype(bf16)
-    mine_ga = ga.at[c, x, y, zh]
-    zcp = remote(mine_ga, mine_ga, ss.at[28], rs.at[28], p.at(z=lax.rem(z + 2, 4)))
-    zcp.start()
-    zcp.wait()
-    up, low = pl.ds(0, 32), pl.ds(32, 32)
-    cps = []
+    nb[24:27, :] = master_new
+
+    pl.semaphore_wait(bar, 8)
+    flying = []
+
+    def send(src, dst, sem, device, at=None):
+        cp = remote(src, dst, ss.at[sem], rs.at[sem if at is None else at], device)
+        cp.start()
+        flying.append(cp)
+
+    def arrived(dst, sem):
+        remote(dst, dst, ss.at[0], rs.at[sem], other_core).wait_recv()
+
+    near[zh] = nb[...].astype(bf16)
+    send(near.at[zh], near.at[zh], 0, over)
+    arrived(near.at[1 - zh], 0)
+    fa[y] = near[:, 0:32]
+    fb[x] = near[:, 32:64]
     for k in range(3):
-        xd, xi = xs[k]
-        yd, yi = ys[k]
-        va_ = ga.at[c, x, y, :, up]
-        vb_ = ga.at[c, x, y, :, low]
-        cps.append(remote(va_, va_, ss.at[29 + k], rs.at[29 + k], yd))
-        cps.append(remote(vb_, vb_, ss.at[32 + k], rs.at[32 + k], xd))
-    for cp in cps:
+        send(near.at[:, pl.ds(0, 32)], fa.at[y], 1 + k, ys[k][0])
+        send(near.at[:, pl.ds(32, 32)], fb.at[x], 4 + k, xs[k][0])
+    for k in range(3):
+        arrived(fa.at[lax.rem(y + 3 - k, 4)], 1 + k)
+    pa[...] = dot(pack_a[...], fa[...].reshape(256, PAD)).astype(bf16)
+    for k in range(3):
+        send(pa, ga.at[c, x], 7 + k, xs[k][0])
+    for k in range(3):
+        arrived(fb.at[lax.rem(x + 3 - k, 4)], 4 + k)
+    pb[...] = dot(pack_b[...], fb[...].reshape(256, PAD)).astype(bf16)
+    for k in range(3):
+        send(pb, gb.at[c, y], 10 + k, ys[k][0])
+    send(pa, ga.at[c, x], 13, other_core, at=13)
+    send(pb, gb.at[c, y], 17, other_core, at=17)
+    keep = [
+        pltpu.make_async_copy(pa, ga.at[c, x], ls.at[0]),
+        pltpu.make_async_copy(pb, gb.at[c, y], ls.at[1]),
+    ]
+    for cp in keep:
         cp.start()
     for k in range(3):
-        yi = lax.rem(y + 3 - k, 4)
-        xi = lax.rem(x + 3 - k, 4)
-        va_ = ga.at[c, x, yi, :, up]
-        vb_ = ga.at[c, xi, y, :, low]
-        remote(va_, va_, ss.at[0], rs.at[29 + k], other_core).wait_recv()
-        remote(vb_, vb_, ss.at[0], rs.at[32 + k], other_core).wait_recv()
-    cps2 = []
+        i = lax.rem(x + 3 - k, 4)
+        arrived(ga.at[c, i], 7 + k)
+        send(ga.at[c, i], ga.at[c, i], 14 + k, other_core)
+        i = lax.rem(y + 3 - k, 4)
+        arrived(gb.at[c, i], 10 + k)
+        send(gb.at[c, i], gb.at[c, i], 18 + k, other_core)
+    arrived(ga.at[1 - c, x], 13)
+    arrived(gb.at[1 - c, y], 17)
     for k in range(3):
-        xd, xi = xs[k]
-        yd, yi = ys[k]
-        va_ = ga.at[c, x, :, :, up]
-        vb_ = ga.at[c, :, y, :, low]
-        cps2.append(remote(va_, va_, ss.at[35 + k], rs.at[35 + k], xd))
-        cps2.append(remote(vb_, vb_, ss.at[38 + k], rs.at[38 + k], yd))
-    for cp in cps2:
-        cp.start()
-
-    natc = dot(ec1[...], owners_col[...]) * 6.0 + bwc1[...]
-    lane = iota((512, 128), 1)
-    place1 = jnp.concatenate(
-        [((lane + 128 * k).astype(f32) == natc).astype(bf16) for k in range(3)], axis=1
-    )
-    natr = dot(owners_row[...], e3[...])[0:1] * 3.0 + bw3[0:1]
-    place2 = (iota((768, 1024), 0).astype(f32) == natr).astype(bf16)
-    for k in range(3):
-        yi = lax.rem(y + 3 - k, 4)
-        xi = lax.rem(x + 3 - k, 4)
-        va_ = ga.at[c, xi, :, :, up]
-        vb_ = ga.at[c, :, yi, :, low]
-        remote(va_, va_, ss.at[0], rs.at[35 + k], other_core).wait_recv()
-        remote(vb_, vb_, ss.at[0], rs.at[38 + k], other_core).wait_recv()
-    both = remote(ga.at[c], ga.at[c], ss.at[41], rs.at[41], other_core)
-    both.start()
-    remote(ga.at[1 - c], ga.at[1 - c], ss.at[0], rs.at[41], other_core).wait_recv()
-    tn = ((0,), (0,))
-    for t in range(5):
-        block = ga[:, :, :, :, 8 * t : 8 * t + 8, :].reshape(512, PAD)
-        cp1[t] = dot(block[:, 0:C0], place1, tn).astype(bf16)
-    block = ga[:, :, :, :, 40:56, :].reshape(1024, PAD)
-    copy2 = dot(place2, block).astype(bf16)
-    for t in range(3):
-        cp2[t] = copy2[192 * t : 192 * t + 192]
-    cp3[...] = copy2[576:768]
-    for cp in sent + late + near + cps + cps2 + [both]:
+        arrived(ga.at[1 - c, lax.rem(x + 3 - k, 4)], 14 + k)
+        arrived(gb.at[1 - c, lax.rem(y + 3 - k, 4)], 18 + k)
+    for cp in keep:
+        cp.wait()
+    for cp in flying:
         cp.wait_send()
 
 
-def run_tail(s1, s2, bases, states, owners_row, owners_col, consts):
+def run_owner(grad, bases, states, consts):
     shape = jax.ShapeDtypeStruct
     dma = pltpu.SemaphoreType.DMA
     scratch = [
-        pltpu.VMEM((5, 4, 4, 48, 384), bf16),
-        pltpu.VMEM((4, 4, 96, 384), bf16),
-        pltpu.VMEM((3, 4, 4, 48, 384), bf16),
-        pltpu.VMEM((4, 4, 48, 384), bf16),
-        pltpu.VMEM((3, 4, 48, 384), bf16),
-        pltpu.VMEM((3, 4, 48, 384), bf16),
-        pltpu.VMEM((3, 4, 96, 384), bf16),
-        pltpu.VMEM((4, 48, 384), bf16),
-        pltpu.VMEM((4, 96, 384), bf16),
-        pltpu.VMEM((3, 48, 384), bf16),
-        pltpu.VMEM((3, 96, 384), bf16),
-        pltpu.VMEM((8, 80, 384), bf16),
-        pltpu.VMEM((8, 80, 384), bf16),
-        pltpu.VMEM((40, PAD), f32),
-        pltpu.VMEM((8, 128), f32),
+        pltpu.VMEM((72, PAD), f32),
         pltpu.VMEM((64, PAD), f32),
-        pltpu.VMEM((2, 4, 4, 2, 64, PAD), bf16),
-        dma((44,)),
-        dma((44,)),
-        dma((4,)),
+        pltpu.VMEM((2, 64, PAD), bf16),
+        pltpu.VMEM((4, 2, 32, PAD), bf16),
+        pltpu.VMEM((4, 2, 32, PAD), bf16),
+        pltpu.VMEM((176, PAD), bf16),
+        pltpu.VMEM((176, PAD), bf16),
+        dma((24,)),
+        dma((24,)),
+        dma((2,)),
     ]
-    wide = [shape(a.shape, f32) for a in states]
+    gathered = shape((2, 4, 176, PAD), bf16)
     return pl.pallas_call(
-        tail_kernel,
-        out_shape=(
-            shape((5, C0, 384), bf16),
-            shape((3, HALFH, C1), bf16),
-            shape((HALFH, C1), bf16),
-            *wide,
-        ),
-        in_specs=[VMEM] * (5 + 12 + 8),
-        out_specs=tuple([VMEM] * 15),
+        owner_kernel,
+        out_shape=(gathered, gathered, *[shape(a.shape, f32) for a in states]),
+        in_specs=[VMEM] * (4 + 12 + 2),
+        out_specs=(ANY, ANY, *[VMEM] * 12),
         scratch_shapes=scratch,
         compiler_params=pltpu.CompilerParams(
             collective_id=1, has_side_effects=True, vmem_limit_bytes=63 * 2**20
         ),
+    )(grad, *bases, *states, consts["pack_a"], consts["pack_b"])
+
+
+def norm_block(gradient, parameters, moments):
+    first_new, second_new, direction = adam_block(moments[0], moments[1], gradient)
+    return parameters - norm_rate * direction, first_new, second_new
+
+
+def finish_kernel(
+    xt, offsets, owners, slopes, stats, ga, gb, out_in, *rest,
+):
+    p = Place()
+    zl = p.zl
+    params = rest[0:6]
+    moments = rest[6:9]
+    rep_a, rep_b, at_a, at_b, rep2a, rep2b, at2a, at2b = rest[9:17]
+    states_in = rest[17:29]
+    out, gin, v1, v1f, v1s, v2, v2f, v2s, v3, v3f, v3s, cp1, cp2, cp3 = rest[29:43]
+    states_out = rest[43:55]
+    gav, gbv, held, tr, ls = rest[55:]
+    copies = [
+        pltpu.make_async_copy(ga, gav, ls.at[0]),
+        pltpu.make_async_copy(gb, gbv, ls.at[1]),
+    ]
+    for cp in copies:
+        cp.start()
+    out[...] = out_in[...]
+    for k in range(12):
+        states_out[k][...] = states_in[k][...]
+
+    vec = stats[...]
+    v326 = jnp.where(zl == 0, vec, pltpu.roll(vec, PAD - HALF0, 1))
+    tr[0:16, :] = v326[:, 0:384]
+    tr[16:128, :] = jnp.zeros((112, 384), f32)
+    cols = jnp.transpose(tr[...])
+    mean_c = cols[0:HALF0, 5:6]
+    rs_c = cols[0:HALF0, 6:7]
+    scale_c = cols[0:HALF0, 7:8]
+    gm_c = cols[0:HALF0, 8:9]
+    bm_c = cols[0:HALF0, 9:10]
+    off_home = offsets[...].astype(f32)
+    tn = ((0,), (0,))
+    rowq = iota((128, 256), 0)
+    laneq = iota((128, 256), 1)
+    put_even = (laneq == 2 * rowq).astype(bf16)
+    put_odd = (laneq == 2 * rowq + 1).astype(bf16)
+    back = []
+    for j in range(2):
+        for k in range(4):
+            bins = pl.ds(128 * k, 128)
+            st = dot(slopes[j, 0, bins, :], put_even, tn) + dot(slopes[j, 1, bins, :], put_odd, tn)
+            lanes = pl.ds(1024 * j + 256 * k, 256)
+            xf = xt[:, lanes].astype(f32)
+            scaled = (xf - mean_c) * rs_c
+            ok = ((iota((1, 256), 1) + (1024 * j + 256 * k)).astype(f32) >= 2.0 * off_home).astype(f32)
+            held[:, lanes] = ok * (scale_c * (st[0:HALF0] - bm_c - scaled * gm_c))
+        half = pl.ds(1024 * j, 1024)
+        back.append(pltpu.make_async_copy(held.at[:, half], gin.at[:, 0, half], ls.at[2 + j]))
+        back[j].start()
+
+    grads1 = v326[0:2, 0:HALF0]
+    v384 = jnp.where(zl == 0, vec, pltpu.roll(vec, PAD - HALF1, 1))
+    grads2 = v384[2:4, 0:HALF1]
+    v192 = jnp.where(zl == 0, vec, pltpu.roll(vec, PAD - HALFH, 1))
+    halves = [(grads1[0:1], grads1[1:2]), (grads2[0:1], grads2[1:2]), (v192[4:5, 0:HALFH], v192[4:5, H : H + HALFH])]
+    outs = [(v1, v1f, v1s), (v2, v2f, v2s), (v3, v3f, v3s)]
+    for n in range(3):
+        for r in range(2):
+            old = (moments[n][0, r : r + 1, :], moments[n][1, r : r + 1, :])
+            new = norm_block(halves[n][r], params[2 * n + r][...].reshape(1, -1), old)
+            for q in range(3):
+                outs[n][q][r : r + 1, :] = new[q]
+
+    own_row = jnp.broadcast_to(owners[...].astype(f32), (8, 64))
+
+    def column(rep, at, width):
+        own = jnp.sum(rep[...].astype(f32) * own_row[0:1], axis=1, keepdims=True)
+        return own * float(width) + at[...]
+
+    lane = iota((384, 384), 1).astype(f32)
+    place_a = (lane == column(rep_a, at_a, 6)).astype(bf16)
+    place_b = (lane == column(rep_b, at_b, 6)).astype(bf16)
+    own8 = own_row.astype(bf16)
+    place2a = (iota((HALFH, 256), 0).astype(f32) == (dot(own8, rep2a[...])[0:1] * 3.0 + at2a[...])).astype(bf16)
+    place2b = (
+        iota((3 * HALFH, 640), 0).astype(f32) == (dot(own8, rep2b[...])[0:1] * 3.0 + at2b[...])
+    ).astype(bf16)
+    copies[0].wait()
+    copies[1].wait()
+    for t in range(3):
+        block = gav[:, :, 48 * t : 48 * t + 48, :].reshape(384, PAD)
+        cp1[t] = dot(block[:, 0:C0], place_a, tn).astype(bf16)
+    for t in range(2):
+        block = gbv[:, :, 48 * t : 48 * t + 48, :].reshape(384, PAD)
+        cp1[3 + t] = dot(block[:, 0:C0], place_b, tn).astype(bf16)
+    cp3[...] = dot(place2a, gav[:, :, 144:176, :].reshape(256, PAD)).astype(bf16)
+    two = dot(place2b, gbv[:, :, 96:176, :].reshape(640, PAD)).astype(bf16)
+    for t in range(3):
+        cp2[t] = two[HALFH * t : HALFH * t + HALFH]
+    for cp in back:
+        cp.wait()
+
+
+def run_finish(xt, offsets, owners, slopes, stats, ga, gb, out, params, moments, states, consts):
+    shape = jax.ShapeDtypeStruct
+    vec = [shape((2, n), f32) for n in (HALF0,) * 3 + (HALF1,) * 3 + (HALFH,) * 3]
+    names = ("rep_a", "rep_b", "at_a", "at_b", "rep2a", "rep2b", "at2a", "at2b")
+    return pl.pallas_call(
+        finish_kernel,
+        out_shape=(
+            shape((BINS, 384), bf16),
+            shape((HALF0, 1, 2 * BINS), f32),
+            *vec,
+            shape((5, C0, 384), bf16),
+            shape((3, HALFH, C1), bf16),
+            shape((HALFH, C1), bf16),
+            *[shape(a.shape, f32) for a in states],
+        ),
+        in_specs=[VMEM] * 5 + [ANY] * 2 + [VMEM] * 30,
+        out_specs=(VMEM, ANY, *[VMEM] * 24),
+        scratch_shapes=[
+            pltpu.VMEM((2, 4, 176, PAD), bf16),
+            pltpu.VMEM((2, 4, 176, PAD), bf16),
+            pltpu.VMEM((HALF0, 2 * BINS), f32),
+            pltpu.VMEM((128, 384), f32),
+            pltpu.SemaphoreType.DMA((4,)),
+        ],
+        compiler_params=pltpu.CompilerParams(vmem_limit_bytes=63 * 2**20),
     )(
-        s1, s2, *bases, *states, owners_row, owners_col,
-        consts["rep1"], consts["rep2"], consts["ec1"], consts["bwc1"], consts["e3"], consts["bw3"],
+        xt, offsets, owners, slopes, stats, ga, gb, out, *params, *moments,
+        *[consts[n] for n in names], *states,
     )
 
 
@@ -979,37 +1157,51 @@
         for m in range(4):
             for w in range(3):
                 rep2[e * 32 + m * 8 + w, m * 24 + e * 3 + w] = 1
-    ec1 = np.zeros((512, 64), np.float32)
-    bwc1 = np.full((512, 128), -4096.0, np.float32)
-    e3 = np.zeros((64, 1024), np.float32)
-    bw3 = np.full((8, 1024), -4096.0, np.float32)
-    for k in range(64):
-        c, g, zh = k // 32, (k // 2) % 16, k % 2
-        s = g * 4 + zh * 2 + c
-        ec1[8 * k : 8 * k + 8, s] = 1
+    pack_a = np.zeros((176, 256), np.float32)
+    pack_b = np.zeros((176, 256), np.float32)
+    for o in range(8):
         for w in range(6):
-            bwc1[8 * k + w] = w
-        e3[s, 16 * k : 16 * k + 16] = 1
-        for m in range(4):
-            for w in range(3):
-                bw3[:, 16 * k + 4 * m + w] = 192 * m + w
+            for t in range(3):
+                pack_a[t * 48 + o * 6 + w, o * 32 + 8 * t + w] = 1
+            for t in range(2):
+                pack_b[t * 48 + o * 6 + w, o * 32 + 8 * t + w] = 1
+        for w in range(3):
+            pack_a[144 + o * 3 + w, o * 32 + 24 + w] = 1
+            for m in range(3):
+                pack_b[96 + m * 24 + o * 3 + w, o * 32 + 16 + 4 * m + w] = 1
+    rep_a = np.zeros((384, 64), np.float32)
+    rep_b = np.zeros((384, 64), np.float32)
+    at_a = np.zeros((384, 1), np.float32)
+    rep2a = np.zeros((64, 256), np.float32)
+    at2a = np.full((1, 256), -4096.0, np.float32)
+    rep2b = np.zeros((64, 640), np.float32)
+    at2b = np.full((1, 640), -4096.0, np.float32)
+    for c in range(2):
+        for i in range(4):
+            for o in range(8):
+                j, zh = o // 2, o % 2
+                s_a = ((i * 4 + j) * 2 + zh) * 2 + c
+                s_b = ((j * 4 + i) * 2 + zh) * 2 + c
+                for w in range(6):
+                    r = (c * 4 + i) * 48 + o * 6 + w
+                    rep_a[r, s_a] = 1
+                    rep_b[r, s_b] = 1
+                    at_a[r, 0] = w
+                for w in range(3):
+                    r = (c * 4 + i) * 32 + o * 3 + w
+                    rep2a[s_a, r] = 1
+                    at2a[0, r] = w
+                    for m in range(3):
+                        r = (c * 4 + i) * 80 + m * 24 + o * 3 + w
+                        rep2b[s_b, r] = 1
+                        at2b[0, r] = m * 192 + w
     low = lambda a: jnp.asarray(a, bf16)
     return {
         "e1": low(e1), "bw1": jnp.asarray(bw1), "e2": low(e2), "bw2": jnp.asarray(bw2),
-        "rep1": low(rep1), "rep2": low(rep2), "ec1": low(ec1), "bwc1": jnp.asarray(bwc1),
-        "e3": low(e3), "bw3": jnp.asarray(bw3),
+        "rep1": low(rep1), "rep2": low(rep2), "pack_a": low(pack_a), "pack_b": low(pack_b),
+        "rep_a": low(rep_a), "rep_b": low(rep_b), "at_a": jnp.asarray(at_a), "at_b": jnp.asarray(at_a),
+        "rep2a": low(rep2a), "rep2b": low(rep2b), "at2a": jnp.asarray(at2a), "at2b": jnp.asarray(at2b),
     }
-
-
-def norm_adam(gradient, parameters, moments):
-    first_new = beta_one * moments[0] + (1.0 - beta_one) * gradient
-    second_new = beta_two * moments[1] + (1.0 - beta_two) * gradient * gradient
-    direction = (
-        first_new
-        / (1.0 - beta_one**STEP)
-        / (jnp.sqrt(second_new / (1.0 - beta_two**STEP)) + adam_eps)
-    )
-    return (parameters - norm_rate * direction, first_new, second_new)
 
 
 def local(
@@ -1022,53 +1214,29 @@
     project_copy, project_master, project_first, project_second, project_average, basis3,
 ):
     consts = make_consts()
-    zl = lax.axis_index("ch")
-    leader = lax.axis_index(SEQ) == 0
-
-    def in_half(v, half, at=0):
-        wide = jnp.zeros((PAD,), f32)
-        return lax.dynamic_update_slice(wide, v, (at + zl * half,))
-
-    rows = jnp.stack(
-        [
-            in_half(norm1_gain, HALF0),
-            in_half(norm1_bias, HALF0),
-            in_half(norm2_gain, HALF1),
-            in_half(norm2_bias, HALF1),
-            in_half(norm3_gain, HALFH) + in_half(norm3_bias, HALFH, H),
-        ]
+    flip2 = lambda a: jnp.swapaxes(a, -1, -2)
+    xt = flip2(inputs[0])
+    offsets = offsets[None]
+    owners = owners[None]
+    params = [norm1_gain, norm1_bias, norm2_gain, norm2_bias, norm3_gain, norm3_bias]
+    out, slopes, grad, stats = run_step(
+        xt, offsets, owners, cotangent[0], conv1_copy, flip2(conv2_copy), flip2(project_copy), params, consts
     )
-    pvec = jnp.pad(jnp.where(leader, rows, 0.0), ((2, 1), (0, 0)))
-    offs = jnp.broadcast_to(offsets.astype(f32)[:, None], (8, 128))
-    owners_low = owners.astype(bf16)
-    owners_row = jnp.broadcast_to(owners_low[None], (8, 64))
-    owners_col = jnp.broadcast_to(owners_low[:, None], (64, 128))
-    out, gin, s1, s2, stats = run_step(
-        jnp.swapaxes(inputs[0], 0, 1), offs, cotangent[0], conv1_copy,
-        jnp.swapaxes(conv2_copy, 1, 2), jnp.swapaxes(project_copy, 0, 1),
-        pvec, owners_row, consts,
-    )
-    flip2 = lambda a: jnp.swapaxes(a, -1, -2)
     states = [
         conv1_master, conv1_first, conv1_second, conv1_average,
         conv2_master, conv2_first, conv2_second, conv2_average,
         project_master, project_first, project_second, project_average,
     ]
-    cp1, cp2, cp3, *new = run_tail(
-        s1.reshape(5, 4, 4, 48, PAD), s2.reshape(4, 4, 96, C1), (basis1, basis2, basis3),
-        [flip2(a) for a in states], owners_row, owners_col, consts,
+    ga, gb, *new = run_owner(grad, (basis1, basis2, basis3), [flip2(a) for a in states], consts)
+    result = run_finish(
+        xt, offsets, owners, slopes, stats, ga, gb, out, params,
+        (norm1_moments, norm2_moments, norm3_moments), new, consts,
     )
-    nm1, nf1, nq1, na1, nm2, nf2, nq2, na2, nm3, nf3, nq3, na3 = [flip2(a) for a in new]
-
-    def my_half(v, half):
-        return lax.dynamic_slice(v, (0, zl * half), (2, half))
-
-    g3 = stats[4].reshape(2, H)
-    s_1 = norm_adam(my_half(stats[0:2], HALF0), jnp.stack([norm1_gain, norm1_bias]), norm1_moments)
-    s_2 = norm_adam(my_half(stats[2:4], HALF1), jnp.stack([norm2_gain, norm2_bias]), norm2_moments)
-    s_3 = norm_adam(my_half(g3, HALFH), jnp.stack([norm3_gain, norm3_bias]), norm3_moments)
+    out, gin, *vec = result[0:11]
+    cp1, cp2, cp3 = result[11:14]
+    nm1, nf1, nq1, na1, nm2, nf2, nq2, na2, nm3, nf3, nq3, na3 = [flip2(a) for a in result[14:]]
     return (
-        out[None], jnp.swapaxes(gin, 0, 1)[None], *s_1, *s_2, *s_3,
+        out[None], jnp.transpose(gin, (1, 2, 0)), *vec,
         nm1, cp1, nf1, nq1, na1,
         nm2, flip2(cp2), nf2, nq2, na2,
         nm3, flip2(cp3), nf3, nq3, na3,

time: 307 us -> 227 us (0.74)
  Pallas kernels: 269 us -> 222 us
  local copies, waits for them, and re-layouts: 28.4 us -> 0 us
  other arithmetic: 3.39 us -> 0 us
    pallas_call x2 -> x3, Pallas kernels: 269 us -> 222 us  [the longest x1 175 us: run_step(): pl.pallas_call(step_kernel, out_shape=(shape((BINS, 384), bf16), shape((2...]
    unnamed x57 -> x0, local copies, waits for them, and re-layouts: 20.5 us -> none
where the time goes in v2:
time: 227 us; the launch traced here: 224 us
  Pallas kernels  222 us (98%)
    pallas_call x1, Pallas kernels, run_step(): pl.pallas_call(step_kernel, out_shape=(shape((BINS, 384), bf16), shape((2...  175 us
    pallas_call x1, Pallas kernels, run_owner(): pl.pallas_call(owner_kernel, out_shape=(gathered, gathered, *[shape(a.sha...  35.5 us
    pallas_call x1, Pallas kernels, run_finish(): pl.pallas_call(finish_kernel, out_shape=(shape((BINS, 384), bf16), shape(...  11.1 us

profile of v2, /device:TPU:1, one launch (start us, length us, event | category | flops | bytes accessed | tf_op | source)
XLA Modules:
  0.0 223.7 jit_solution(8121581551182293381)
XLA Ops:
  1.3 175.3 %shard_map.629 = (bf16[1024,384]{1,0:T(8,128)(2,1)}, bf16[2,2,512,384]{3,2,1,0:T(8,128)(2,1)}, f32[80,768]{1,0:T(8,128)}, f32[16,768]{1,0:T(8,128)}) custom-call(bf16[326,2048]{1,0:T(8,128)(2,1)} %bitcast.38, s32[1,1]{1,0:T(1,128)} %bitcast.36.offsets, s32[1,64]{1,0:T(1,128)} %bitcast.55, bf16[1024,384]{1,0:T(8,128)(2,1)} %bitcast.41, ...), custom_call_target="tpu_custom_call" | custom-call | tf_op jit(solution)/shard_map/pallas_call | solution.py:827
  176.7 35.5 %shard_map.630 = (bf16[2,4,176,768]{3,2,1,0:T(8,128)(2,1)}, bf16[2,4,176,768]{3,2,1,0:T(8,128)(2,1)}, f32[5,6,652]{2,1,0:T(8,128)}, f32[5,6,652]{2,1,0:T(8,128)}...) custom-call(f32[80,768]{1,0:T(8,128)} %get-tuple-element.72.grad, ...), custom_call_target="tpu_custom_call" | custom-call | tf_op jit(solution)/shard_map/pallas_call | solution.py:993
  212.1 11.1 %shard_map.631 = (bf16[1024,384]{1,0:T(8,128)(2,1)}, f32[326,1,2048]{2,1,0:T(1,128)}, f32[2,326]{1,0:T(2,128)}, f32[2,326]{1,0:T(2,128)}, f32[2,326]{1,0:T(2,128...) custom-call(bf16[326,2048]{1,0:T(8,128)(2,1)} %bitcast.39, ...), custom_call_target="tpu_custom_call" | custom-call | tf_op jit(solution)/shard_map/pallas_call | solution.py:1109

commit v3 on v2

--- a/solution.py
+++ b/solution.py
@@ -54,6 +54,22 @@
     return lax.broadcasted_iota(jnp.int32, shape, dim)
 
 
+def adam_block(first, second, turned):
+    first_new = beta_one * first + (1.0 - beta_one) * turned
+    second_new = beta_two * second + (1.0 - beta_two) * turned * turned
+    direction = (
+        first_new
+        / (1.0 - beta_one**STEP)
+        / (jnp.sqrt(second_new / (1.0 - beta_two**STEP)) + adam_eps)
+    )
+    return first_new, second_new, direction
+
+
+def master_block(master, update, rate, average):
+    master_new = master - rate * (update + decay_rate * master)
+    return master_new, average_rate * average + (1.0 - average_rate) * master_new
+
+
 class Place:
     def __init__(self):
         self.x, self.y, self.zh, self.c, self.zl = [lax.axis_index(n) for n in SEQ_CH]
@@ -89,6 +105,14 @@
         x = lax.rem(p.x + k // 4, 4)
         y = lax.rem(p.y + k % 4, 4)
         out.append((p.at(x=x, y=y), x, y))
+    return out
+
+
+def other_peers(p):
+    over = lax.rem(p.z + 2, 4)
+    out = [p.at(x=lax.rem(p.x + k, 4), c=1 - p.c) for k in (1, 2, 3)]
+    out += [p.at(x=lax.rem(p.x + k, 4), z=over) for k in (1, 2, 3)]
+    out += [p.at(y=lax.rem(p.y + k, 4), z=over) for k in (1, 2, 3)]
     return out
 
 
@@ -143,13 +167,16 @@
 
 def step_kernel(
     xt, offsets, owners, cot, w1, w2, wp, pg1, pb1, pg2, pb2, pg3, pb3,
-    e1, bw1, e2, bw2, rep1, rep2,
-    out, sl_home, grad, stats,
-    s1, s2, xw, raw, aa, ww1, ww2, wwp, pooled, diff, cc, hid, og, no, hh, mid, gg, gp, perm,
-    slope, small, offs, offw, acc, tr,
-    t1, t2, ra, rb, rd, re, ua, uc, va, pz, rz,
+    e1, bw1, e2, bw2, rep1, rep2, pack1, pack2, b1, b2, b3,
+    m1, f1, q1, a1, m2, f2, q2, a2, m3, f3, q3, a3,
+    out, sl_home, stats, ga1, gb1, ga2, gb2,
+    nm1, nf1, nq1, na1, nm2, nf2, nq2, na2, nm3, nf3, nq3, na3,
+    s1, s2, xw, raw, aa, ww1, ww2, wwp, pooled, diff, cc, hid, og, no, hh, mid, gg, gp,
+    slope, small, offs, offw, acc, tr, dv, dm,
+    t1, t2, ra, rb, rd, re, ua, uc, va, pz, rz, pz2, rz2,
+    b1f, bb1, grad, dd, nb, near1, near2, fa1, fb1, fa2, fb2, pa1, pb1_, pa2, pb2_,
     a1a, a1b, ab1, ab2,
-    ss, rs, ls, as1, ar1, as2, ar2, gs, gr,
+    ss, rs, ls, as1, ar1, as2, ar2, gs, gr, hs, hr, bs,
 ):
     mm = gg.at[0:3]
     p = Place()
@@ -164,44 +191,8 @@
         pl.semaphore_signal(bar, inc=1, device_id=device, device_id_type=MESH)
     for device, _, _ in plane_peers(p):
         pl.semaphore_signal(bar, inc=1, device_id=device, device_id_type=MESH)
-
-    own_w = [
-        pltpu.make_async_copy(w1, ww1.at[:, :, pl.ds(pl.multiple_of(384 * zl, 128), 384)], ls.at[0]),
-        pltpu.make_async_copy(w2, ww2.at[:, pl.ds(pl.multiple_of(192 * zl, 16), 192), :], ls.at[1]),
-        pltpu.make_async_copy(wp, wwp.at[pl.ds(pl.multiple_of(192 * zl, 16), 192), :], ls.at[2]),
-    ]
-    for cp in own_w:
-        cp.start()
-
-    pl.semaphore_wait(bar, 22)
-
-    is_self = c == zl
-    not_self = c != zl
-    home_chip = 2 * p.zh + c
-
-    def window(j):
-        return xt.at[:, pl.ds(pl.multiple_of(896 * j, 128), LANES)]
-
-    def cot_window(j):
-        return cot.at[pl.ds(pl.multiple_of(496 * j, 16), WIN), :]
-
-    cc_mine = cc.at[:, pl.ds(pl.multiple_of(384 * zl, 128), 384)]
-    x_a = remote(window(c), xw.at[zl], ss.at[0], rs.at[0 + zl], p.at(z=home_chip, c=c))
-    x_b = remote(window(1 - c), xw.at[zl], ss.at[1], rs.at[0 + zl], p.at(z=home_chip, c=1 - c))
-    c_a = remote(cot_window(c), cc_mine, ss.at[2], rs.at[2 + zl], p.at(z=home_chip, c=c))
-    c_b = remote(cot_window(1 - c), cc_mine, ss.at[3], rs.at[2 + zl], p.at(z=home_chip, c=1 - c))
-    o_a = remote(offs, offw, ss.at[4], rs.at[4], other_core)
-
-    @pl.when(not_self)
-    def _():
-        x_a.start()
-
-    @pl.when(is_self)
-    def _():
-        pltpu.make_async_copy(window(c), xw.at[zl], rs.at[0 + zl]).start()
-
-    x_b.start()
-    o_a.start()
+    for device in other_peers(p):
+        pl.semaphore_signal(bar, inc=1, device_id=device, device_id_type=MESH)
 
     mine = pl.ds(pl.multiple_of(384 * c, 128), 384)
     others = pl.ds(pl.multiple_of(384 - 384 * c, 128), 384)
@@ -210,21 +201,73 @@
     my_rows = pl.ds(pl.multiple_of(192 * zl, 16), 192)
     its_rows = pl.ds(pl.multiple_of(192 - 192 * zl, 16), 192)
 
+    def unit_ref(u, rows):
+        return ww2.at[u, rows, :] if u < 3 else wwp.at[rows, :]
+
+    own_w = [pltpu.make_async_copy(w1.at[t], ww1.at[t, :, my_lanes], ls.at[t]) for t in range(5)]
+    own_w += [
+        pltpu.make_async_copy(w2.at[u] if u < 3 else wp, unit_ref(u, my_rows), ls.at[5 + u])
+        for u in range(4)
+    ]
+    for cp in own_w:
+        cp.start()
+
+    pl.semaphore_wait(bar, 31)
+
+    is_self = c == zl
+    not_self = c != zl
+    home_chip = 2 * p.zh + c
+
+    def window(j, part):
+        at = 896 * j + (0, 256)[part]
+        return xt.at[:, pl.ds(pl.multiple_of(at, 128), (256, LANES - 256)[part])]
+
+    def window_there(k, part):
+        return xw.at[k, :, pl.ds((0, 256)[part], (256, LANES - 256)[part])]
+
+    def cot_window(j):
+        return cot.at[pl.ds(pl.multiple_of(496 * j, 16), WIN), :]
+
+    cc_mine = cc.at[:, pl.ds(pl.multiple_of(384 * zl, 128), 384)]
+    x_a = [
+        remote(window(c, h), window_there(zl, h), ss.at[33 * h], rs.at[33 * h + zl], p.at(z=home_chip, c=c))
+        for h in range(2)
+    ]
+    x_b = [
+        remote(
+            window(1 - c, h), window_there(zl, h), ss.at[33 * h + 1], rs.at[33 * h + zl],
+            p.at(z=home_chip, c=1 - c),
+        )
+        for h in range(2)
+    ]
+    c_a = remote(cot_window(c), cc_mine, ss.at[2], rs.at[2 + zl], p.at(z=home_chip, c=c))
+    c_b = remote(cot_window(1 - c), cc_mine, ss.at[3], rs.at[2 + zl], p.at(z=home_chip, c=1 - c))
+    o_a = remote(offs, offw, ss.at[4], rs.at[4], other_core)
+
+    def send_windows(h):
+        pl.when(not_self)(lambda: x_a[h].start())
+
+        def keep():
+            pltpu.make_async_copy(window(c, h), window_there(zl, h), rs.at[33 * h + zl]).start()
+
+        pl.when(is_self)(keep)
+        x_b[h].start()
+
+    send_windows(0)
+    o_a.start()
+
     def tap_over(t):
         to = direct if t == 4 else flip
-        return remote(w1.at[t], ww1.at[t, :, my_lanes], ss.at[5 + t], rs.at[5 + t], to)
+        return remote(ww1.at[t, :, my_lanes], ww1.at[t, :, my_lanes], ss.at[5 + t], rs.at[5 + t], to)
 
     def tap_here(t):
         return remote(
             ww1.at[t, :, its_lanes], ww1.at[t, :, its_lanes], ss.at[10 + t], rs.at[10 + t], other_core
         )
 
-    def unit_ref(u, rows):
-        return ww2.at[u, rows, :] if u < 3 else wwp.at[rows, :]
-
     def unit_over(u):
         return remote(
-            w2.at[u] if u < 3 else wp, unit_ref(u, my_rows), ss.at[15 + u], rs.at[15 + u], flip
+            unit_ref(u, my_rows), unit_ref(u, my_rows), ss.at[15 + u], rs.at[15 + u], flip
         )
 
     def unit_here(u):
@@ -232,20 +275,8 @@
             unit_ref(u, its_rows), unit_ref(u, its_rows), ss.at[19 + u], rs.at[19 + u], other_core
         )
 
-    for t in range(5):
-        pl.when(c == TAP_CORE[t])(lambda t=t: tap_over(t).start())
-
-    @pl.when(not_self)
-    def _():
-        c_a.start()
-
-    @pl.when(is_self)
-    def _():
-        pltpu.make_async_copy(cot_window(c), cc_mine, rs.at[2 + zl]).start()
-
-    c_b.start()
-    for u in range(4):
-        pl.when(c == UNIT_CORE[u])(lambda u=u: unit_over(u).start())
+    own_w[5].wait()
+    pl.when(c == 0)(lambda: unit_over(0).start())
 
     off_home = offs[0:1, 0:1]
     total_s = jnp.zeros((8, HALF0), f32)
@@ -286,21 +317,38 @@
     here = here + jnp.where((lane8 == PAD - 1) & (row8 == 0), count, 0.0)
     all1 = Total(p, (a1a, a1b), (as1.at[0], ar1.at[0], as2.at[0], ar2.at[0]))
     all1.start(here)
+    send_windows(1)
+    for t in range(5):
+        own_w[t].wait()
+        pl.when(c == TAP_CORE[t])(lambda t=t: tap_over(t).start())
+
+    @pl.when(not_self)
+    def _():
+        c_a.start()
+
+    @pl.when(is_self)
+    def _():
+        pltpu.make_async_copy(cot_window(c), cc_mine, rs.at[2 + zl]).start()
+
+    c_b.start()
+    for u in range(1, 4):
+        own_w[5 + u].wait()
+        pl.when(c == UNIT_CORE[u])(lambda u=u: unit_over(u).start())
     all1.middle()
 
     owners_row = jnp.broadcast_to(owners[...].astype(f32), (8, 64)).astype(bf16)
     nat1 = dot(owners_row, e1[...])[0:1] * 6.0 + bw1[0:1]
     nat2 = dot(owners_row, e2[...])[0:1] * 3.0 + bw2[0:1]
-    for k in range(6):
-        perm[pl.ds(128 * k, 128), :] = (
-            (iota((128, PAD), 0) + 128 * k).astype(f32) == nat1
-        ).astype(bf16)
+    for k in range(4):
+        s1[4, k] = ((iota((192, PAD), 0) + 192 * k).astype(f32) == nat1).astype(bf16).reshape(4, 48, PAD)
     perm2 = (iota((H, H), 0).astype(f32) == nat2).astype(bf16)
 
     row = iota((128, 128), 0)
     pick = (iota((128, 128), 1) == jnp.where(row < 64, 2 * row, 2 * row - 127)).astype(bf16)
     for k in range(2):
-        remote(xw.at[k], xw.at[k], ss.at[0], rs.at[0 + k], other_core).wait_recv()
+        for h in range(2):
+            part = window_there(k, h)
+            remote(part, part, ss.at[0], rs.at[33 * h + k], other_core).wait_recv()
     tr[...] = jnp.zeros_like(tr)
     for k in range(9):
         lanes = pl.ds(128 * k, 128)
@@ -364,7 +412,6 @@
             aa[2 + par, :, lanes] = v.astype(bf16)
             aa[4 + par, :, lanes] = after(v)
 
-    own_w[0].wait()
     for t in range(5):
 
         def there(t=t):
@@ -402,9 +449,17 @@
 
     all2 = Total(p, (ab1.at[0], ab2.at[0]), (as1.at[1], ar1.at[1], as2.at[1], ar2.at[1]))
     all2.start(acc[0:2])
+
+    def early_slopes(par):
+        @pl.loop(0, 6)
+        def _(q):
+            lanes = pl.ds(pl.multiple_of(128 * q, 128), 128)
+            xv = raw[par, pl.ds(rawown, OWN), lanes].astype(f32)
+            turn = gelu_slope(xv * small[0:1, lanes] + small[1:2, lanes])
+            dv[par, :, lanes] = (turn * valid_mask(OWN, 16 * c)).astype(bf16)
+
+    early_slopes(0)
     all2.middle()
-    own_w[1].wait()
-    own_w[2].wait()
     for u in range(4):
 
         def there_u(u=u):
@@ -422,13 +477,16 @@
         pl.when(c == UNIT_CORE[u])(lambda u=u: unit_here(u).wait_send())
         pl.when(c != UNIT_CORE[u])(lambda u=u: unit_here(u).wait_recv())
     og[...] = dot(cc[...], wwp[...], ((1,), (1,)))
+    early_slopes(1)
 
     @pl.when(not_self)
     def _():
-        x_a.wait_send()
+        x_a[0].wait_send()
+        x_a[1].wait_send()
         c_a.wait_send()
 
-    x_b.wait_send()
+    x_b[0].wait_send()
+    x_b[1].wait_send()
     c_b.wait_send()
 
     second = all2.end()
@@ -458,7 +516,50 @@
     acc[6:7, H : 2 * H] = jnp.sum(h2m * h2, axis=0, keepdims=True)
     all3 = Total(p, (ab1.at[1], ab2.at[1]), (as1.at[2], ar1.at[2], as2.at[2], ar2.at[2]))
     all3.start(acc[6:8])
+
+    def basis_rows(src, first, size, buf, sem):
+        return pltpu.make_async_copy(src.at[pl.ds(first, size)], buf, bs.at[sem])
+
+    slope_buf = [slope.at[pl.ds(0, 128)], slope.at[pl.ds(128, 128)]]
+    rows_buf = slope_buf + [tr.at[0], tr.at[1]]
+
+    def rounds(n):
+        got = []
+        for k in range(4):
+            block = 4 * n + k
+            src = b2 if block < 6 else b3
+            got.append(basis_rows(src, 128 * (block % 6), 128, rows_buf[k], k))
+        return got
+
+    def keep_round(n):
+        for k, cp in enumerate(rounds(n)):
+            cp.wait()
+            block = 4 * n + k
+            half, at = block // 3, 128 * (block % 3)
+            value = rows_buf[k][...].astype(bf16)
+            if half < 3:
+                ww2[half, pl.ds(at, 128), :] = value
+            else:
+                wwp[pl.ds(at, 128), :] = value
+
+    first_basis = pltpu.make_async_copy(b1, b1f, bs.at[4])
+    first_basis.start()
+
+    @pl.loop(0, 6)
+    def _(q):
+        lanes = pl.ds(pl.multiple_of(128 * q, 128), 128)
+        turn = gelu_slope(pooled[:, lanes] * acc[2:3, lanes] + acc[3:4, lanes])
+        dm[:, lanes] = (turn * valid_mask(WIN)).astype(bf16)
+
     all3.middle()
+
+    @pl.loop(0, 6)
+    def _(q):
+        lanes = pl.ds(pl.multiple_of(128 * q, 128), 128)
+        diff[:, lanes] = 1.0 / (1.0 + jnp.exp(-diff[:, lanes]))
+
+    first_basis.wait()
+    bb1[...] = b1f[...].astype(bf16)
     third = all3.end()
     mean3 = third[0:1, 0:H] * inv_n2
     var3 = third[0:1, H : 2 * H] * inv_n2 - mean3 * mean3
@@ -492,7 +593,7 @@
 
     def out_local(k):
         return pltpu.make_async_copy(
-            gp.at[0, :, pl.ds(384 * k, 384)], out.at[out_rows, :], ls.at[3]
+            gp.at[0, :, pl.ds(384 * k, 384)], out.at[out_rows, :], ls.at[9]
         )
 
     def to_self(k):
@@ -509,6 +610,8 @@
     tn = ((0,), (0,))
     nop = dot(no[own_rows, :], perm2).astype(bf16)
     put2(3, dot(nop, cc[own_rows, :], tn))
+    for cp in rounds(0):
+        cp.start()
     fourth = all4.end()
     stats[4:5] = fourth[0:1]
     gain_mean = fourth[0:1, 0:H] * inv_n2
@@ -526,7 +629,7 @@
     def _(k):
         lanes = pl.ds(pl.multiple_of(128 * k, 128), 128)
         v = pooled[:, lanes]
-        slopes = gelu_slope(v * acc[2:3, lanes] + acc[3:4, lanes]) * mid[:, lanes] * valid_mask(WIN)
+        slopes = dm[:, lanes].astype(f32) * mid[:, lanes]
         scaled = (v - acc[4:5, lanes]) * acc[5:6, lanes]
         mid[:, lanes] = slopes
         pooled[:, lanes] = scaled
@@ -538,11 +641,17 @@
     all5.start(acc[0:2])
     hp = dot(hh[1, own_rows, :], perm2).astype(bf16)
     put2(0, dot(hp, mm[0, own_rows, :], tn))
+    keep_round(0)
     all5.middle()
+    for cp in rounds(1):
+        cp.start()
     for t in range(1, 3):
         put2(t, dot(hp, mm[t, own_rows, :], tn))
     s2_over = remote(s2.at[:, :, :, others], t2, gs.at[0], gr.at[0], other_core)
     s2_over.start()
+    keep_round(1)
+    for cp in rounds(2):
+        cp.start()
     fifth = all5.end()
     stats[2:4] = fifth
     acc[0:2] = fifth * inv_n2
@@ -554,7 +663,7 @@
             mid[:, lanes] - acc[1:2, lanes] - pooled[:, lanes] * acc[0:1, lanes]
         )
         pg = cc[:, lanes].astype(f32) + back * valid_mask(WIN)
-        even = 1.0 / (1.0 + jnp.exp(-diff[:, lanes]))
+        even = diff[:, lanes]
         ge = pg * even
         go = pg * (1.0 - even)
         gg[0, :, lanes] = after(go)
@@ -574,6 +683,9 @@
         if axis == "x":
             i = lax.rem(p.x + k + 1, 4)
             return p.at(x=i), i
+        if axis == "z":
+            i = lax.rem(p.z + k + 1, 4)
+            return p.at(z=i), i
         i = lax.rem(p.y + k + 1, 4)
         return p.at(y=i), i
 
@@ -590,8 +702,9 @@
         remote(dst, dst, gs.at[0], gr.at[sem], other_core).wait_recv()
 
     for k in range(3):
-        device, i = along(k, "y")
-        send(t2.at[:, i], rd.at[k], 1 + k, device)
+        device, i = along(k, "z")
+        send(t2.at[i], rd.at[k], 1 + k, device)
+    keep_round(2)
 
     for k in range(2):
 
@@ -600,8 +713,9 @@
 
         pl.when(jnp.logical_not(to_self(k)))(out_sent)
         pl.when(to_self(k))(lambda k=k: out_local(k).wait())
-    gp[0] = dot(gg[3, own_rows, :], perm[...]).astype(bf16)
-    gp[1] = dot(gg[2, own_rows, :], perm[...]).astype(bf16)
+    perm = s1[4].reshape(PAD, PAD)
+    gp[0] = dot(gg[3, own_rows, :], perm).astype(bf16)
+    gp[1] = dot(gg[2, own_rows, :], perm).astype(bf16)
 
     TAP_AXIS = ("x", "y", "x", "y", "x")
 
@@ -640,12 +754,20 @@
         if t > 0:
             to_axis(t - 1)
     to_axis(4)
-    for k in range(3):
-        arrived(rd.at[k], 1 + k)
-    uc[...] = total(t2[:, p.y], [rd[k] for k in range(3)])
-    for k in range(3):
-        device, i = along(k, "x")
-        send(uc.at[i], re.at[k], 4 + k, device)
+
+    def second_of_two():
+        for k in range(3):
+            arrived(rd.at[k], 1 + k)
+        uc[...] = total(t2[p.z], [rd[k] for k in range(3)])
+        for k in range(3):
+            device, i = along(k, "y")
+            send(uc.at[i], re.at[k], 4 + k, device)
+
+    def xc_peers():
+        for k in range(1, 8):
+            xi = lax.rem(p.x + k // 2, 4)
+            ci = lax.rem(c + k % 2, 2)
+            yield p.at(x=xi, c=ci), 2 * xi + ci
 
     def slope_part(half, par, k):
         return (
@@ -676,8 +798,7 @@
             def _(q, par=par, k=k):
                 lanes = pl.ds(pl.multiple_of(128 * q, 128), 128)
                 xv = raw[par, pl.ds(pl.multiple_of(rawown + 256 * k, 16), 256), lanes].astype(f32)
-                valid = valid_mask(256, 16 * c + 256 * k)
-                slopes = gelu_slope(xv * small[0:1, lanes] + small[1:2, lanes]) * slope[:, lanes] * valid
+                slopes = dv[par, pl.ds(256 * k, 256), lanes].astype(f32) * slope[:, lanes]
                 scaled = (xv - small[2:3, lanes]) * small[3:4, lanes]
                 slope[:, lanes] = slopes
                 small[4:5, lanes] += jnp.sum(slopes * scaled, axis=0, keepdims=True)
@@ -686,28 +807,179 @@
             dst = pl.ds(256 * k, 256)
             gp[par, dst, 0:384] = slope[:, 0:384].astype(bf16)
             gp[par, dst, 384:768] = pltpu.roll(slope[...], PAD - HALF0, 1)[:, 0:384].astype(bf16)
-            for half in range(2):
-
-                def send_slope(half=half, par=par, k=k):
-                    slope_copy(half, par, k).start()
-
-                def keep_slope(half=half, par=par, k=k):
-                    slope_local(half, par, k).start()
-
-                pl.when(jnp.logical_not(to_self(half)))(send_slope)
-                pl.when(to_self(half))(keep_slope)
+            if (par, k) == (0, 1):
+                second_of_two()
             if (par, k) == (1, 0):
                 to_other_axis(0)
                 to_other_axis(1)
 
+    def send_slopes(par):
+        for half in range(2):
+            for k in range(2):
+
+                def send_slope(half=half, k=k):
+                    slope_copy(half, par, k).start()
+
+                def keep_slope(half=half, k=k):
+                    slope_local(half, par, k).start()
+
+                pl.when(jnp.logical_not(to_self(half)))(send_slope)
+                pl.when(to_self(half))(keep_slope)
+
     all6 = Total(p, (ab1.at[4], ab2.at[4]), (as1.at[5], ar1.at[5], as2.at[5], ar2.at[5]))
     all6.start(small[4:6])
 
     to_other_axis(2)
+    to_other_axis(3)
     all6.middle()
-    to_other_axis(3)
-    for t in range(2):
+    send_slopes(0)
+    for k in range(3):
+        arrived(re.at[k], 4 + k)
+    g2 = dot(rep2[...], total(uc[p.y], [re[k] for k in range(3)]))
+    e2_own = 2 * p.x + c
+    for e in range(8):
+        pz2[e] = g2[32 * e : 32 * e + 32].astype(bf16)
+    for k, (device, e) in enumerate(xc_peers()):
+        cp = remote(pz2.at[e], rz2.at[e2_own], gs.at[50 + k], gr.at[50 + e2_own], device)
+        cp.start()
+        flying.append(cp)
+    rz2[e2_own] = pz2[e2_own]
+    to_other_axis(4)
+    for t in range(4):
         last_of(t)
+
+    def summed(parts, half):
+        v = parts[half].astype(f32)
+        for k in range(1, 4):
+            v = v + parts[2 * k + half].astype(f32)
+        return v
+
+    for _, e in xc_peers():
+        arrived(rz2.at[e], 50 + e)
+    for half in range(2):
+        grad[48:80, 384 * half : 384 * half + 384] = summed(rz2, half)
+    nt = ((1,), (1,))
+    nb[...] = jnp.zeros_like(nb)
+    dd[...] = jnp.zeros_like(dd)
+
+    def turn2(v):
+        return dot(v[:, 0:384], ww2[0]) + dot(v[:, 384:768], ww2[1])
+
+    def turn3(v):
+        return dot(v[:, 0:384], ww2[2]) + dot(v[:, 384:768], wwp[...])
+
+    turned = turn2(grad[48:72].astype(bf16))
+    for t in range(3):
+        first_new, second_new, direction = adam_block(f2[t], q2[t], turned[8 * t : 8 * t + 3])
+        nf2[t] = first_new
+        nq2[t] = second_new
+        dd[40 + 8 * t : 43 + 8 * t, :] = direction
+    turned = turn3(grad[72:80].astype(bf16))
+    first_new, second_new, direction = adam_block(f3[...], q3[...], turned[0:3])
+    nf3[...] = first_new
+    nq3[...] = second_new
+    dd[64:67] = direction
+    d2 = dd[40:64].astype(bf16)
+    update = jnp.concatenate([dot(d2, ww2[0], nt), dot(d2, ww2[1], nt)], axis=1)
+    row_of_two = (68, 80, 84)
+    for t in range(3):
+        master_new, average_new = master_block(m2[t], update[8 * t : 8 * t + 3], 0.02, a2[t])
+        nm2[t] = master_new
+        na2[t] = average_new
+        nb[row_of_two[t] : row_of_two[t] + 3, :] = master_new
+    d3 = dd[64:72].astype(bf16)
+    update = jnp.concatenate([dot(d3, ww2[2], nt), dot(d3, wwp[...], nt)], axis=1)
+    master_new, average_new = master_block(m3[...], update[0:3], 0.05, a3[...])
+    nm3[...] = master_new
+    na3[...] = average_new
+    nb[64:67, :] = master_new
+
+    def hop(src, dst, send_at, recv_at, device):
+        cp = remote(src, dst, hs.at[send_at], hr.at[recv_at], device)
+        cp.start()
+        flying.append(cp)
+
+    def landed(dst, sem):
+        remote(dst, dst, hs.at[0], hr.at[sem], other_core).wait_recv()
+
+    qa = 2 * p.y + p.zh
+    qb = 2 * p.x + p.zh
+
+    def near_peers(axis):
+        for k in range(1, 8):
+            i = lax.rem((p.y if axis == "y" else p.x) + k // 2, 4)
+            zh = lax.rem(p.zh + k % 2, 2)
+            z = 2 * zh + zl
+            yield (p.at(y=i, z=z) if axis == "y" else p.at(x=i, z=z)), 2 * i + zh
+
+    def gather_near(near, fa, fb, rows, base):
+        fa[qa] = near[0:rows]
+        fb[qb] = near[rows : 2 * rows]
+        for k, (device, _) in enumerate(near_peers("y")):
+            hop(near.at[pl.ds(0, rows)], fa.at[qa], base + k, base + qa, device)
+        for k, (device, _) in enumerate(near_peers("x")):
+            hop(near.at[pl.ds(rows, rows)], fb.at[qb], base + 8 + k, base + 8 + qb, device)
+
+    def gather_far(fa, fb, pack, pa, pb, parts_a, parts_b, ga, gb, base):
+        for _, q in near_peers("y"):
+            landed(fa.at[q], base + q)
+        pa[...] = dot(pack, fa[...].reshape(8 * fa.shape[1], PAD)).astype(bf16)
+        for k in range(3):
+            device, _ = along(k, "x")
+            for n, part in enumerate(parts_a):
+                hop(pa.at[part], ga.at[(c, p.x) + part], base + 16 + 8 * n + k, base + 16 + 8 * n + p.x, device)
+        for _, q in near_peers("x"):
+            landed(fb.at[q], base + 8 + q)
+        pb[...] = dot(pack, fb[...].reshape(8 * fb.shape[1], PAD)).astype(bf16)
+        for k in range(3):
+            device, _ = along(k, "y")
+            for n, part in enumerate(parts_b):
+                hop(pb.at[part], gb.at[(c, p.y) + part], base + 20 + 8 * n + k, base + 20 + 8 * n + p.y, device)
+        kept = []
+        for n, part in enumerate(parts_a):
+            hop(pa.at[part], ga.at[(c, p.x) + part], base + 35 + 8 * n, base + 32 + 8 * n + p.x, other_core)
+            kept.append(pltpu.make_async_copy(pa.at[part], ga.at[(c, p.x) + part], bs.at[8 + n]))
+        for n, part in enumerate(parts_b):
+            hop(pb.at[part], gb.at[(c, p.y) + part], base + 39 + 8 * n, base + 36 + 8 * n + p.y, other_core)
+            kept.append(pltpu.make_async_copy(pb.at[part], gb.at[(c, p.y) + part], bs.at[10 + n]))
+        for cp in kept:
+            cp.start()
+        return kept
+
+    def gather_over(parts_a, parts_b, ga, gb, base):
+        for k in range(3):
+            _, i = along(2 - k, "x")
+            for n, part in enumerate(parts_a):
+                ref = ga.at[(c, i) + part]
+                landed(ref, base + 16 + 8 * n + i)
+                hop(ref, ref, base + 32 + 8 * n + k, base + 32 + 8 * n + i, other_core)
+            _, i = along(2 - k, "y")
+            for n, part in enumerate(parts_b):
+                ref = gb.at[(c, i) + part]
+                landed(ref, base + 20 + 8 * n + i)
+                hop(ref, ref, base + 36 + 8 * n + k, base + 36 + 8 * n + i, other_core)
+
+    def gather_end(parts_a, parts_b, ga, gb, base):
+        for i in range(4):
+            for n, part in enumerate(parts_a):
+                landed(ga.at[(1 - c, i) + part], base + 32 + 8 * n + i)
+            for n, part in enumerate(parts_b):
+                landed(gb.at[(1 - c, i) + part], base + 36 + 8 * n + i)
+
+    whole2 = ((slice(None), slice(None)),)
+    near2[...] = nb[64:96].astype(bf16)
+    gather_near(near2, fa2, fb2, 16, 0)
+
+    last_of(4)
+    g1 = dot(rep1[...], va[...].reshape(240, 384))
+    for e in range(8):
+        pz[e] = g1[48 * e : 48 * e + 48].astype(bf16)
+    for k, (device, zi, ci) in enumerate(column_peers(p)):
+        cp = remote(pz.at[2 * zi + ci], rz.at[p.e], gs.at[42 + k], gr.at[42 + p.e], device)
+        cp.start()
+        flying.append(cp)
+    rz[p.e] = pz[p.e]
+    kept2 = gather_far(fa2, fb2, pack2[...], pa2, pb2_, whole2, whole2, ga2, gb2, 0)
     sixth = all6.end()
     stats[0:2] = sixth
     stats[5:6] = mean1
@@ -715,30 +987,40 @@
     stats[7:8] = rs1 * gain1
     stats[8:10] = sixth * inv_n1
     stats[10:16] = jnp.zeros((6, PAD), f32)
-    to_other_axis(4)
-    for k in range(3):
-        arrived(re.at[k], 4 + k)
-    vc = total(uc[p.x], [re[k] for k in range(3)])
-    for t in range(2, 5):
-        last_of(t)
-    g1 = dot(rep1[...], va[...].reshape(240, 384))
-    g2 = dot(rep2[...], vc)
-    for e in range(8):
-        pz[e, 0:48] = g1[48 * e : 48 * e + 48].astype(bf16)
-        pz[e, 48:80] = g2[32 * e : 32 * e + 32].astype(bf16)
-    for k, (device, zi, ci) in enumerate(column_peers(p)):
-        cp = remote(pz.at[2 * zi + ci], rz.at[p.e], gs.at[42 + k], gr.at[42 + p.e], device)
-        cp.start()
-        flying.append(cp)
-    rz[p.e] = pz[p.e]
+
     for device, zi, ci in column_peers(p):
         e = 2 * zi + ci
         arrived(rz.at[e], 42 + e)
     for half in range(2):
-        v = rz[half].astype(f32)
-        for k in range(1, 4):
-            v = v + rz[2 * k + half].astype(f32)
-        grad[:, 384 * half : 384 * half + 384] = v
+        grad[0:48, 384 * half : 384 * half + 384] = summed(rz, half)
+    turned = dot(grad[0:40, 0:C0].astype(bf16), bb1[...])
+    for t in range(5):
+        first_new, second_new, direction = adam_block(f1[t], q1[t], turned[8 * t : 8 * t + 6])
+        nf1[t] = first_new
+        nq1[t] = second_new
+        dd[8 * t : 8 * t + 6, 0:C0] = direction
+    update = dot(dd[0:40, 0:C0].astype(bf16), bb1[...], nt)
+    row_of = (0, 8, 16, 32, 40)
+    for t in range(5):
+        master_new, average_new = master_block(m1[t], update[8 * t : 8 * t + 6], 0.02, a1[t])
+        nm1[t] = master_new
+        na1[t] = average_new
+        nb[row_of[t] : row_of[t] + 6, 0:C0] = master_new
+        if t == 2:
+            nb[48:54, 0:C0] = master_new
+    near1[...] = nb[0:64].astype(bf16)
+    gather_near(near1, fa1, fb1, 32, 48)
+    send_slopes(1)
+    gather_over(whole2, whole2, ga2, gb2, 0)
+    taps2 = (pl.ds(0, 96), slice(None))
+    parts_a = (taps2, (pl.ds(96, 48), pl.ds(0, 384)))
+    parts_b = (taps2, (pl.ds(96, 48), pl.ds(384, 384)))
+    kept1 = gather_far(fa1, fb1, pack1[...], pa1, pb1_, parts_a, parts_b, ga1, gb1, 48)
+    gather_over(parts_a, parts_b, ga1, gb1, 48)
+    gather_end(whole2, whole2, ga2, gb2, 0)
+    gather_end(parts_a, parts_b, ga1, gb1, 48)
+    for cp in kept1 + kept2:
+        cp.wait()
 
     for t in range(5):
         to_core(t).wait_send()
@@ -770,7 +1052,7 @@
 ANY = pl.BlockSpec(memory_space=pl.ANY)
 
 
-def run_step(xt, offsets, owners, cot, w1, w2, wp, params, consts):
+def run_step(xt, offsets, owners, cot, w1, w2, wp, params, bases, states, consts):
     shape = jax.ShapeDtypeStruct
     dma = pltpu.SemaphoreType.DMA
     scratch = [
@@ -792,13 +1074,14 @@
         pltpu.VMEM((WIN, C1), f32),
         pltpu.VMEM((6, WIN, C1), bf16),
         pltpu.VMEM((2, OWN, C1), bf16),
-        pltpu.VMEM((C1, C1), bf16),
         pltpu.VMEM((256, PAD), f32),
         pltpu.VMEM((8, PAD), f32),
         pltpu.VMEM((8, 128), f32),
         pltpu.VMEM((8, 128), f32),
         pltpu.VMEM((8, PAD), f32),
         pltpu.VMEM((2, 128, PAD), f32),
+        pltpu.VMEM((2, OWN, PAD), bf16),
+        pltpu.VMEM((WIN, C1), bf16),
         pltpu.VMEM((5, 4, 4, 48, 384), bf16),
         pltpu.VMEM((4, 4, 96, 384), bf16),
         pltpu.VMEM((5, 3, 4, 48, 384), bf16),
@@ -808,198 +1091,67 @@
         pltpu.VMEM((5, 4, 48, 384), bf16),
         pltpu.VMEM((4, 96, 384), bf16),
         pltpu.VMEM((5, 48, 384), bf16),
-        pltpu.VMEM((8, 80, 384), bf16),
-        pltpu.VMEM((8, 80, 384), bf16),
+        pltpu.VMEM((8, 48, 384), bf16),
+        pltpu.VMEM((8, 48, 384), bf16),
+        pltpu.VMEM((8, 32, 384), bf16),
+        pltpu.VMEM((8, 32, 384), bf16),
+        pltpu.VMEM((C0, C0), f32),
+        pltpu.VMEM((C0, C0), bf16),
+        pltpu.VMEM((80, PAD), f32),
+        pltpu.VMEM((72, PAD), f32),
+        pltpu.VMEM((96, PAD), f32),
+        pltpu.VMEM((64, PAD), bf16),
+        pltpu.VMEM((32, PAD), bf16),
+        pltpu.VMEM((8, 32, PAD), bf16),
+        pltpu.VMEM((8, 32, PAD), bf16),
+        pltpu.VMEM((8, 16, PAD), bf16),
+        pltpu.VMEM((8, 16, PAD), bf16),
+        pltpu.VMEM((144, PAD), bf16),
+        pltpu.VMEM((144, PAD), bf16),
+        pltpu.VMEM((48, PAD), bf16),
+        pltpu.VMEM((48, PAD), bf16),
         pltpu.VMEM((8, 8, PAD), f32),
         pltpu.VMEM((16, 8, PAD), f32),
         pltpu.VMEM((5, 8, 2, PAD), f32),
         pltpu.VMEM((5, 16, 2, PAD), f32),
         dma((40,)),
         dma((40,)),
-        dma((4,)),
+        dma((10,)),
         dma((6, 8)),
         dma((6, 8)),
         dma((6, 16)),
         dma((6, 16)),
-        dma((52,)),
-        dma((52,)),
+        dma((60,)),
+        dma((60,)),
+        dma((96,)),
+        dma((96,)),
+        dma((12,)),
     ]
+    one = shape((2, 4, 144, PAD), bf16)
+    two = shape((2, 4, 48, PAD), bf16)
     return pl.pallas_call(
         step_kernel,
         out_shape=(
             shape((BINS, 384), bf16),
             shape((2, 2, OWN, 384), bf16),
-            shape((80, PAD), f32),
             shape((16, PAD), f32),
+            one,
+            one,
+            two,
+            two,
+            *[shape(a.shape, f32) for a in states],
         ),
-        in_specs=[VMEM, VMEM, VMEM, ANY, ANY, ANY, ANY] + [VMEM] * 12,
-        out_specs=(ANY, ANY, VMEM, VMEM),
+        in_specs=[VMEM, VMEM, VMEM, ANY, ANY, ANY, ANY] + [VMEM] * 14 + [ANY] * 3 + [VMEM] * 12,
+        out_specs=(ANY, ANY, VMEM, ANY, ANY, ANY, ANY, *[VMEM] * 12),
         scratch_shapes=scratch,
         compiler_params=pltpu.CompilerParams(
             collective_id=0, has_side_effects=True, vmem_limit_bytes=63 * 2**20
         ),
     )(
         xt, offsets, owners, cot, w1, w2, wp, *params,
-        *[consts[n] for n in ("e1", "bw1", "e2", "bw2", "rep1", "rep2")],
+        *[consts[n] for n in ("e1", "bw1", "e2", "bw2", "rep1", "rep2", "pack1", "pack2")],
+        *bases, *states,
     )
-
-
-def adam_block(first, second, turned):
-    first_new = beta_one * first + (1.0 - beta_one) * turned
-    second_new = beta_two * second + (1.0 - beta_two) * turned * turned
-    direction = (
-        first_new
-        / (1.0 - beta_one**STEP)
-        / (jnp.sqrt(second_new / (1.0 - beta_two**STEP)) + adam_eps)
-    )
-    return first_new, second_new, direction
-
-
-def master_block(master, update, rate, average):
-    master_new = master - rate * (update + decay_rate * master)
-    return master_new, average_rate * average + (1.0 - average_rate) * master_new
-
-
-def owner_kernel(
-    grad, b1, b2, b3,
-    m1, f1, q1, a1, m2, f2, q2, a2, m3, f3, q3, a3, pack_a, pack_b,
-    ga, gb, nm1, nf1, nq1, na1, nm2, nf2, nq2, na2, nm3, nf3, nq3, na3,
-    dd, nb, near, fa, fb, pa, pb,
-    ss, rs, ls,
-):
-    p = Place()
-    x, y, zh, zl, z, c = p.x, p.y, p.zh, p.zl, p.z, p.c
-    other_core = p.at(c=1 - c)
-    over = p.at(z=lax.rem(z + 2, 4))
-    xs = [(p.at(x=lax.rem(x + k, 4)), lax.rem(x + k, 4)) for k in (1, 2, 3)]
-    ys = [(p.at(y=lax.rem(y + k, 4)), lax.rem(y + k, 4)) for k in (1, 2, 3)]
-    bar = pltpu.get_barrier_semaphore()
-    for device in [d for d, _ in xs + ys] + [other_core, over]:
-        pl.semaphore_signal(bar, inc=1, device_id=device, device_id_type=MESH)
-
-    nt = ((1,), (1,))
-    nb[...] = jnp.zeros_like(nb)
-    dd[...] = jnp.zeros_like(dd)
-    basis1 = b1[...].astype(bf16)
-    turned = dot(grad[0:40, 0:C0].astype(bf16), basis1)
-    for t in range(5):
-        first_new, second_new, direction = adam_block(f1[t], q1[t], turned[8 * t : 8 * t + 6])
-        nf1[t] = first_new
-        nq1[t] = second_new
-        dd[8 * t : 8 * t + 6, 0:C0] = direction
-    update = dot(dd[0:40, 0:C0].astype(bf16), basis1, nt)
-    row_of = (0, 8, 16, 32, 40)
-    for t in range(5):
-        master_new, average_new = master_block(m1[t], update[8 * t : 8 * t + 6], 0.02, a1[t])
-        nm1[t] = master_new
-        na1[t] = average_new
-        nb[row_of[t] : row_of[t] + 6, 0:C0] = master_new
-    basis2 = b2[...].astype(bf16)
-    turned = dot(grad[48:72].astype(bf16), basis2)
-    for t in range(3):
-        first_new, second_new, direction = adam_block(f2[t], q2[t], turned[8 * t : 8 * t + 3])
-        nf2[t] = first_new
-        nq2[t] = second_new
-        dd[40 + 8 * t : 43 + 8 * t, :] = direction
-    update = dot(dd[40:64].astype(bf16), basis2, nt)
-    for t in range(3):
-        master_new, average_new = master_block(m2[t], update[8 * t : 8 * t + 3], 0.02, a2[t])
-        nm2[t] = master_new
-        na2[t] = average_new
-        nb[48 + 4 * t : 51 + 4 * t, :] = master_new
-    basis3 = b3[...].astype(bf16)
-    turned = dot(grad[72:80].astype(bf16), basis3)
-    first_new, second_new, direction = adam_block(f3[...], q3[...], turned[0:3])
-    nf3[...] = first_new
-    nq3[...] = second_new
-    dd[64:67] = direction
-    update = dot(dd[64:72].astype(bf16), basis3, nt)
-    master_new, average_new = master_block(m3[...], update[0:3], 0.05, a3[...])
-    nm3[...] = master_new
-    na3[...] = average_new
-    nb[24:27, :] = master_new
-
-    pl.semaphore_wait(bar, 8)
-    flying = []
-
-    def send(src, dst, sem, device, at=None):
-        cp = remote(src, dst, ss.at[sem], rs.at[sem if at is None else at], device)
-        cp.start()
-        flying.append(cp)
-
-    def arrived(dst, sem):
-        remote(dst, dst, ss.at[0], rs.at[sem], other_core).wait_recv()
-
-    near[zh] = nb[...].astype(bf16)
-    send(near.at[zh], near.at[zh], 0, over)
-    arrived(near.at[1 - zh], 0)
-    fa[y] = near[:, 0:32]
-    fb[x] = near[:, 32:64]
-    for k in range(3):
-        send(near.at[:, pl.ds(0, 32)], fa.at[y], 1 + k, ys[k][0])
-        send(near.at[:, pl.ds(32, 32)], fb.at[x], 4 + k, xs[k][0])
-    for k in range(3):
-        arrived(fa.at[lax.rem(y + 3 - k, 4)], 1 + k)
-    pa[...] = dot(pack_a[...], fa[...].reshape(256, PAD)).astype(bf16)
-    for k in range(3):
-        send(pa, ga.at[c, x], 7 + k, xs[k][0])
-    for k in range(3):
-        arrived(fb.at[lax.rem(x + 3 - k, 4)], 4 + k)
-    pb[...] = dot(pack_b[...], fb[...].reshape(256, PAD)).astype(bf16)
-    for k in range(3):
-        send(pb, gb.at[c, y], 10 + k, ys[k][0])
-    send(pa, ga.at[c, x], 13, other_core, at=13)
-    send(pb, gb.at[c, y], 17, other_core, at=17)
-    keep = [
-        pltpu.make_async_copy(pa, ga.at[c, x], ls.at[0]),
-        pltpu.make_async_copy(pb, gb.at[c, y], ls.at[1]),
-    ]
-    for cp in keep:
-        cp.start()
-    for k in range(3):
-        i = lax.rem(x + 3 - k, 4)
-        arrived(ga.at[c, i], 7 + k)
-        send(ga.at[c, i], ga.at[c, i], 14 + k, other_core)
-        i = lax.rem(y + 3 - k, 4)
-        arrived(gb.at[c, i], 10 + k)
-        send(gb.at[c, i], gb.at[c, i], 18 + k, other_core)
-    arrived(ga.at[1 - c, x], 13)
-    arrived(gb.at[1 - c, y], 17)
-    for k in range(3):
-        arrived(ga.at[1 - c, lax.rem(x + 3 - k, 4)], 14 + k)
-        arrived(gb.at[1 - c, lax.rem(y + 3 - k, 4)], 18 + k)
-    for cp in keep:
-        cp.wait()
-    for cp in flying:
-        cp.wait_send()
-
-
-def run_owner(grad, bases, states, consts):
-    shape = jax.ShapeDtypeStruct
-    dma = pltpu.SemaphoreType.DMA
-    scratch = [
-        pltpu.VMEM((72, PAD), f32),
-        pltpu.VMEM((64, PAD), f32),
-        pltpu.VMEM((2, 64, PAD), bf16),
-        pltpu.VMEM((4, 2, 32, PAD), bf16),
-        pltpu.VMEM((4, 2, 32, PAD), bf16),
-        pltpu.VMEM((176, PAD), bf16),
-        pltpu.VMEM((176, PAD), bf16),
-        dma((24,)),
-        dma((24,)),
-        dma((2,)),
-    ]
-    gathered = shape((2, 4, 176, PAD), bf16)
-    return pl.pallas_call(
-        owner_kernel,
-        out_shape=(gathered, gathered, *[shape(a.shape, f32) for a in states]),
-        in_specs=[VMEM] * (4 + 12 + 2),
-        out_specs=(ANY, ANY, *[VMEM] * 12),
-        scratch_shapes=scratch,
-        compiler_params=pltpu.CompilerParams(
-            collective_id=1, has_side_effects=True, vmem_limit_bytes=63 * 2**20
-        ),
-    )(grad, *bases, *states, consts["pack_a"], consts["pack_b"])
 
 
 def norm_block(gradient, parameters, moments):
@@ -1008,7 +1160,7 @@
 
 
 def finish_kernel(
-    xt, offsets, owners, slopes, stats, ga, gb, out_in, *rest,
+    xt, offsets, owners, slopes, stats, ga1, gb1, ga2, gb2, out_in, *rest,
 ):
     p = Place()
     zl = p.zl
@@ -1018,10 +1170,17 @@
     states_in = rest[17:29]
     out, gin, v1, v1f, v1s, v2, v2f, v2s, v3, v3f, v3s, cp1, cp2, cp3 = rest[29:43]
     states_out = rest[43:55]
-    gav, gbv, held, tr, ls = rest[55:]
+    gav, gbv, gav2, gbv2, held, tr, ls = rest[55:]
+    third_a = (slice(None), slice(None), pl.ds(96, 48), pl.ds(0, 384))
+    third_b = (slice(None), slice(None), pl.ds(96, 48), pl.ds(384, 384))
+    taps2 = (slice(None), slice(None), pl.ds(0, 96))
     copies = [
-        pltpu.make_async_copy(ga, gav, ls.at[0]),
-        pltpu.make_async_copy(gb, gbv, ls.at[1]),
+        pltpu.make_async_copy(ga1.at[taps2], gav.at[taps2], ls.at[0]),
+        pltpu.make_async_copy(gb1.at[taps2], gbv.at[taps2], ls.at[1]),
+        pltpu.make_async_copy(ga1.at[third_a], gav.at[third_a], ls.at[4]),
+        pltpu.make_async_copy(gb1.at[third_b], gbv.at[third_b], ls.at[5]),
+        pltpu.make_async_copy(ga2, gav2, ls.at[6]),
+        pltpu.make_async_copy(gb2, gbv2, ls.at[7]),
     ]
     for cp in copies:
         cp.start()
@@ -1082,27 +1241,28 @@
     place_a = (lane == column(rep_a, at_a, 6)).astype(bf16)
     place_b = (lane == column(rep_b, at_b, 6)).astype(bf16)
     own8 = own_row.astype(bf16)
-    place2a = (iota((HALFH, 256), 0).astype(f32) == (dot(own8, rep2a[...])[0:1] * 3.0 + at2a[...])).astype(bf16)
-    place2b = (
-        iota((3 * HALFH, 640), 0).astype(f32) == (dot(own8, rep2b[...])[0:1] * 3.0 + at2b[...])
-    ).astype(bf16)
-    copies[0].wait()
-    copies[1].wait()
-    for t in range(3):
+    place2a = (iota((H, H), 0).astype(f32) == (dot(own8, rep2a[...])[0:1] * 3.0 + at2a[...])).astype(bf16)
+    place2b = (iota((H, H), 0).astype(f32) == (dot(own8, rep2b[...])[0:1] * 3.0 + at2b[...])).astype(bf16)
+    for cp in copies:
+        cp.wait()
+    for t in range(2):
         block = gav[:, :, 48 * t : 48 * t + 48, :].reshape(384, PAD)
         cp1[t] = dot(block[:, 0:C0], place_a, tn).astype(bf16)
-    for t in range(2):
         block = gbv[:, :, 48 * t : 48 * t + 48, :].reshape(384, PAD)
         cp1[3 + t] = dot(block[:, 0:C0], place_b, tn).astype(bf16)
-    cp3[...] = dot(place2a, gav[:, :, 144:176, :].reshape(256, PAD)).astype(bf16)
-    two = dot(place2b, gbv[:, :, 96:176, :].reshape(640, PAD)).astype(bf16)
-    for t in range(3):
-        cp2[t] = two[HALFH * t : HALFH * t + HALFH]
+    cp1[2, 0:384] = dot(gav[:, :, 96:144, 0:384].reshape(384, 384), place_a, tn).astype(bf16)
+    cp1[2, 384:C0] = dot(gbv[:, :, 96:144, 384:C0].reshape(384, C0 - 384), place_b, tn).astype(bf16)
+    two = dot(place2a, gav2[...].reshape(384, PAD)).astype(bf16)
+    cp3[...] = two[0:HALFH]
+    cp2[0] = two[HALFH:H]
+    two = dot(place2b, gbv2[...].reshape(384, PAD)).astype(bf16)
+    cp2[1] = two[0:HALFH]
+    cp2[2] = two[HALFH:H]
     for cp in back:
         cp.wait()
 
 
-def run_finish(xt, offsets, owners, slopes, stats, ga, gb, out, params, moments, states, consts):
+def run_finish(xt, offsets, owners, slopes, stats, gathered, out, params, moments, states, consts):
     shape = jax.ShapeDtypeStruct
     vec = [shape((2, n), f32) for n in (HALF0,) * 3 + (HALF1,) * 3 + (HALFH,) * 3]
     names = ("rep_a", "rep_b", "at_a", "at_b", "rep2a", "rep2b", "at2a", "at2b")
@@ -1117,18 +1277,20 @@
             shape((HALFH, C1), bf16),
             *[shape(a.shape, f32) for a in states],
         ),
-        in_specs=[VMEM] * 5 + [ANY] * 2 + [VMEM] * 30,
+        in_specs=[VMEM] * 5 + [ANY] * 4 + [VMEM] * 30,
         out_specs=(VMEM, ANY, *[VMEM] * 24),
         scratch_shapes=[
-            pltpu.VMEM((2, 4, 176, PAD), bf16),
-            pltpu.VMEM((2, 4, 176, PAD), bf16),
+            pltpu.VMEM((2, 4, 144, PAD), bf16),
+            pltpu.VMEM((2, 4, 144, PAD), bf16),
+            pltpu.VMEM((2, 4, 48, PAD), bf16),
+            pltpu.VMEM((2, 4, 48, PAD), bf16),
             pltpu.VMEM((HALF0, 2 * BINS), f32),
             pltpu.VMEM((128, 384), f32),
-            pltpu.SemaphoreType.DMA((4,)),
+            pltpu.SemaphoreType.DMA((8,)),
         ],
         compiler_params=pltpu.CompilerParams(vmem_limit_bytes=63 * 2**20),
     )(
-        xt, offsets, owners, slopes, stats, ga, gb, out, *params, *moments,
+        xt, offsets, owners, slopes, stats, *gathered, out, *params, *moments,
         *[consts[n] for n in names], *states,
     )
 
@@ -1145,9 +1307,10 @@
             for w in range(6):
                 e1[s, (g * 8 + e) * 6 + w] = 1
                 bw1[:, (g * 8 + e) * 6 + w] = b * 384 + w
+            block = ((2 * zh + b) * 4 + g % 4) * 8 + (g // 4) * 2 + c
             for w in range(3):
-                e2[s, (g * 8 + e) * 3 + w] = 1
-                bw2[:, (g * 8 + e) * 3 + w] = b * 192 + w
+                e2[s, block * 3 + w] = 1
+                bw2[:, block * 3 + w] = b * 192 + w
     rep1 = np.zeros((8 * 48, 240), np.float32)
     rep2 = np.zeros((8 * 32, 96), np.float32)
     for e in range(8):
@@ -1157,25 +1320,21 @@
         for m in range(4):
             for w in range(3):
                 rep2[e * 32 + m * 8 + w, m * 24 + e * 3 + w] = 1
-    pack_a = np.zeros((176, 256), np.float32)
-    pack_b = np.zeros((176, 256), np.float32)
+    pack1 = np.zeros((144, 256), np.float32)
+    pack2 = np.zeros((48, 128), np.float32)
     for o in range(8):
         for w in range(6):
             for t in range(3):
-                pack_a[t * 48 + o * 6 + w, o * 32 + 8 * t + w] = 1
-            for t in range(2):
-                pack_b[t * 48 + o * 6 + w, o * 32 + 8 * t + w] = 1
+                pack1[t * 48 + o * 6 + w, o * 32 + 8 * t + w] = 1
         for w in range(3):
-            pack_a[144 + o * 3 + w, o * 32 + 24 + w] = 1
-            for m in range(3):
-                pack_b[96 + m * 24 + o * 3 + w, o * 32 + 16 + 4 * m + w] = 1
+            for m in range(2):
+                pack2[m * 24 + o * 3 + w, o * 16 + 4 * m + w] = 1
     rep_a = np.zeros((384, 64), np.float32)
     rep_b = np.zeros((384, 64), np.float32)
     at_a = np.zeros((384, 1), np.float32)
-    rep2a = np.zeros((64, 256), np.float32)
-    at2a = np.full((1, 256), -4096.0, np.float32)
-    rep2b = np.zeros((64, 640), np.float32)
-    at2b = np.full((1, 640), -4096.0, np.float32)
+    rep2a = np.zeros((64, 384), np.float32)
+    rep2b = np.zeros((64, 384), np.float32)
+    at2 = np.zeros((1, 384), np.float32)
     for c in range(2):
         for i in range(4):
             for o in range(8):
@@ -1187,20 +1346,18 @@
                     rep_a[r, s_a] = 1
                     rep_b[r, s_b] = 1
                     at_a[r, 0] = w
-                for w in range(3):
-                    r = (c * 4 + i) * 32 + o * 3 + w
-                    rep2a[s_a, r] = 1
-                    at2a[0, r] = w
-                    for m in range(3):
-                        r = (c * 4 + i) * 80 + m * 24 + o * 3 + w
+                for m in range(2):
+                    for w in range(3):
+                        r = (c * 4 + i) * 48 + m * 24 + o * 3 + w
+                        rep2a[s_a, r] = 1
                         rep2b[s_b, r] = 1
-                        at2b[0, r] = m * 192 + w
+                        at2[0, r] = m * 192 + w
     low = lambda a: jnp.asarray(a, bf16)
     return {
         "e1": low(e1), "bw1": jnp.asarray(bw1), "e2": low(e2), "bw2": jnp.asarray(bw2),
-        "rep1": low(rep1), "rep2": low(rep2), "pack_a": low(pack_a), "pack_b": low(pack_b),
+        "rep1": low(rep1), "rep2": low(rep2), "pack1": low(pack1), "pack2": low(pack2),
         "rep_a": low(rep_a), "rep_b": low(rep_b), "at_a": jnp.asarray(at_a), "at_b": jnp.asarray(at_a),
-        "rep2a": low(rep2a), "rep2b": low(rep2b), "at2a": jnp.asarray(at2a), "at2b": jnp.asarray(at2b),
+        "rep2a": low(rep2a), "rep2b": low(rep2b), "at2a": jnp.asarray(at2), "at2b": jnp.asarray(at2),
     }
 
 
@@ -1219,17 +1376,18 @@
     offsets = offsets[None]
     owners = owners[None]
     params = [norm1_gain, norm1_bias, norm2_gain, norm2_bias, norm3_gain, norm3_bias]
-    out, slopes, grad, stats = run_step(
-        xt, offsets, owners, cotangent[0], conv1_copy, flip2(conv2_copy), flip2(project_copy), params, consts
-    )
     states = [
         conv1_master, conv1_first, conv1_second, conv1_average,
         conv2_master, conv2_first, conv2_second, conv2_average,
         project_master, project_first, project_second, project_average,
     ]
-    ga, gb, *new = run_owner(grad, (basis1, basis2, basis3), [flip2(a) for a in states], consts)
+    out, slopes, stats, *more = run_step(
+        xt, offsets, owners, cotangent[0], conv1_copy, flip2(conv2_copy), flip2(project_copy), params,
+        (basis1, basis2, basis3), [flip2(a) for a in states], consts,
+    )
+    gathered, new = more[0:4], more[4:]
     result = run_finish(
-        xt, offsets, owners, slopes, stats, ga, gb, out, params,
+        xt, offsets, owners, slopes, stats, gathered, out, params,
         (norm1_moments, norm2_moments, norm3_moments), new, consts,
     )
     out, gin, *vec = result[0:11]

time: 227 us -> 195 us (0.86)
  Pallas kernels: 222 us -> 190 us
    pallas_call x1 -> x0, Pallas kernels: 35.5 us -> none  [run_owner(): pl.pallas_call(owner_kernel, out_shape=(gathered, gathered, *[shape(a.sha...]
    pallas_call x1, Pallas kernels: 175 us -> 180 us  [run_step(): pl.pallas_call(step_kernel, out_shape=(shape((BINS, 384), bf16), shape((2...]
where the time goes in v3:
time: 195 us; the launch traced here: 192 us
  Pallas kernels  190 us (97%)
    pallas_call x1, Pallas kernels, run_step(): pl.pallas_call(step_kernel, out_shape=(shape((BINS, 384), bf16), shape((2...  180 us
    pallas_call x1, Pallas kernels, run_finish(): pl.pallas_call(finish_kernel, out_shape=(shape((BINS, 384), bf16), shape(...  10.2 us

profile of v3, /device:TPU:1, one launch (start us, length us, event | category | flops | bytes accessed | tf_op | source)
XLA Modules:
  0.0 191.9 jit_solution(6287094421715917112)
XLA Ops:
  1.3 180.2 %shard_map.620 = (bf16[1024,384]{1,0:T(8,128)(2,1)}, bf16[2,2,512,384]{3,2,1,0:T(8,128)(2,1)}, f32[16,768]{1,0:T(8,128)}, bf16[2,4,144,768]{3,2,1,0:T(8,128)(2,1...) custom-call(bf16[326,2048]{1,0:T(8,128)(2,1)} %bitcast.38, ...), custom_call_target="tpu_custom_call" | custom-call | tf_op jit(solution)/shard_map/pallas_call | solution.py:1132
  181.5 10.2 %shard_map.621 = (bf16[1024,384]{1,0:T(8,128)(2,1)}, f32[326,1,2048]{2,1,0:T(1,128)}, f32[2,326]{1,0:T(2,128)}, f32[2,326]{1,0:T(2,128)}, f32[2,326]{1,0:T(2,128...) custom-call(bf16[326,2048]{1,0:T(8,128)(2,1)} %bitcast.39, ...), custom_call_target="tpu_custom_call" | custom-call | tf_op jit(solution)/shard_map/pallas_call | solution.py:1269
